TPU v7x, 128 devices: a whole 4x4x4 slice. The times are simulated.
128 devices in a mesh: orb: 8 (over y, core), pair: 16 (over x, z).
Axes of the slice: x: 4, y: 4, z: 4, core: 2. Of those that a mesh axis runs over, the one named last changes fastest.
Arguments:
- integrals: bfloat16 [16, 2048, 768], P('orb', 'pair'), may hold values from -0.75 to 0.75
- pno_maps: bfloat16 [384, 768, 384], P('orb'), may hold values from -0.21875 to 0.21875
- pair_orbs: int32 [384, 2], P('orb'), may hold values from 0 to 15
- pair_class: int32 [384], P(('orb', 'pair')), may hold values from 0 to 1
- orbital_energy: float32 [16], replicated, may hold values from -2 to -0.3
- pno_energy: float32 [384, 384], P(('orb', 'pair')), may hold values from 0.2 to 3
- amplitudes: float32 [384, 384, 384], P(('orb', 'pair')), may hold values from -2 to 2
Outputs:
- residual: float32 [384, 384, 384], P(('orb', 'pair'))
Inputs may be any that keep to these rules, and one draw needn't show every extreme that they name: pair_class is 0 for a domain of 256 PNOs and 1 for one of 384. `pair_orbs`: orbital indices of each pair; i may equal j.
All inputs are finite; a program needn't handle non-finite values.
Results may differ from a plain program's by a relative error of at most 0.0017.
Values may be sent and summed in bfloat16 or wider, within the bound.
No kernel may reach another device: no remote copies, remote signals or barrier semaphores. Data moves between devices by JAX's collectives and lax.ppermute only.
A program may use at most 192 MiB of HBM per device.

v0:
```python
import jax
import jax.numpy as jnp
from jax import lax
from jax.sharding import PartitionSpec as P

NSMALL = 256


def body(integrals, pno_maps, pair_orbs, pair_class, orbital_energy, pno_energy, amplitudes):
    everyone = lax.all_gather(integrals, "orb", axis=0, tiled=True)
    groups = lax.axis_size("pair")
    local_pairs = pair_orbs.shape[0]
    owned = local_pairs // groups
    width = pno_maps.shape[2]
    left = jnp.einsum(
        "pqv,pva->pqa", everyone[pair_orbs[:, 0]], pno_maps, preferred_element_type=jnp.float32
    ).astype(jnp.bfloat16)
    right = jnp.einsum(
        "pqv,pva->pqa", everyone[pair_orbs[:, 1]], pno_maps, preferred_element_type=jnp.float32
    ).astype(jnp.bfloat16)
    left, right = (left, right)
    exchange = lax.psum_scatter(
        jnp.einsum("pqa,pqb->pab", left, right, preferred_element_type=jnp.float32),
        "pair",
        scatter_dimension=0,
        tiled=True,
    )
    first = lax.axis_index("pair") * owned
    mine = lax.dynamic_slice_in_dim(pair_orbs, first, owned, 0)
    sizes = NSMALL + pair_class * (width - NSMALL)
    places = jnp.arange(width, dtype=jnp.int32)
    keep = places[None, :] < sizes[:, None]
    window = keep[:, :, None] & keep[:, None, :]
    occupied = orbital_energy[mine[:, 0]] + orbital_energy[mine[:, 1]]
    denom = pno_energy[:, :, None] + pno_energy[:, None, :] - occupied[:, None, None]
    return jnp.where(window, exchange + denom * amplitudes, jnp.zeros_like(exchange))


def solution(mesh):
    return jax.shard_map(
        body,
        mesh=mesh,
        in_specs=(
            P("orb", "pair", None),
            P("orb", None, None),
            P("orb", None),
            P(("orb", "pair")),
            P(),
            P(("orb", "pair"), None),
            P(("orb", "pair"), None, None),
        ),
        out_specs=P(("orb", "pair"), None, None),
        check_vma=False,
    )
```

profile of v0, /device:TPU:1, one launch (start us, length us, event | category | flops | bytes accessed | tf_op | source)
XLA Modules:
  0.0 285.2 jit_solution(4380829159753672111)
XLA Ops:
  6.5 0.0 copy-start
  6.5 0.0 all-gather.2.cloned.1.call-start
  6.5 0.7 all-gather.2.cloned.1.call-update
  7.3 0.0 reduce-scatter.4.cloned.1.call-start
  7.3 0.8 fusion.4
  8.1 32.4 %all-gather.2.cloned.1.call-done = bf16[16,128,768]{2,1,0:T(8,128)(2,1)} async-done(((bf16[2,128,768]{2,1,0:T(8,128)(2,1)}), bf16[16,128,768]{2,1,0:T(8,128)(2,1)}) %all-gather.2.cloned.1.call-update) | async-done | bytes 3145744 | tf_op jit(solution)/shard_map/all_gather | solution.py:10
  40.5 8.3 %gather_fusion = bf16[48,128,768]{2,1,0:T(8,128)(2,1)} fusion(bf16[16,128,768]{2,1,0:T(8,128)(2,1)} %all-gather.2.cloned.1.call-done, s32[1024]{0:T(1024)S(1)} %get-tuple-element.10), kind=kCustom, calls=%fused_computation | custom fusion | bytes 18874560 | tf_op jit(solution)/shard_map/gather | solution.py:16
  48.7 17.0 %fusion.7 = bf16[48,128,384]{2,1,0:T(8,128)(2,1)} fusion(bf16[48,128,768]{2,1,0:T(8,128)(2,1)} %gather_fusion, bf16[48,768,384]{2,1,0:T(8,128)(2,1)} %param.8), kind=kOutput, calls=%fused_computation.23 | convolution fusion | flops 3623878656 | bytes 42467328 | tf_op jit(solution)/shard_map/pqv,pva->pqa/dot_general | solution.py:15
  65.7 0.0 copy-done.1
  65.7 6.4 %gather_fusion.1 = bf16[48,128,768]{2,1,0:T(8,128)(2,1)} fusion(bf16[16,128,768]{2,1,0:T(8,128)(2,1)S(1)} %copy-done.1, s32[1024]{0:T(1024)S(1)} %get-tuple-element.9), kind=kCustom, calls=%fused_computation.1 | custom fusion | bytes 18874560 | tf_op jit(solution)/shard_map/gather | solution.py:19
  72.1 16.9 %fusion.8 = bf16[48,128,384]{2,1,0:T(8,128)(2,1)} fusion(bf16[48,128,768]{2,1,0:T(8,128)(2,1)} %gather_fusion.1, bf16[48,768,384]{2,1,0:T(8,128)(2,1)} %param.8), kind=kOutput, calls=%fused_computation.24 | convolution fusion | flops 3623878656 | bytes 42467328 | tf_op jit(solution)/shard_map/pqv,pva->pqa/dot_general | solution.py:18
  89.0 17.0 %fusion.9 = f32[48,384,384]{2,1,0:T(8,128)} fusion(bf16[48,128,384]{2,1,0:T(8,128)(2,1)} %fusion.7, bf16[48,128,384]{2,1,0:T(8,128)(2,1)} %fusion.8), kind=kOutput, calls=%fused_computation.25 | convolution fusion | flops 1811939328 | bytes 37748736 | tf_op jit(solution)/shard_map/pqa,pqb->pab/dot_general | solution.py:23
  106.0 0.0 reduce-scatter.4.cloned.1.call-update
  106.0 0.6 copy-done.4
  106.6 0.1 constant_dynamic-slice_fusion
  106.7 0.0 copy-done
  106.7 0.6 gather_fusion.2
  107.4 0.6 gather_fusion.3
  108.0 0.0 copy-done.5
  108.0 0.1 iota_compare_fusion
  108.1 167.0 %reduce-scatter.4.cloned.1.call-done = f32[3,384,384]{2,1,0:T(8,128)} async-done(((f32[48,384,384]{2,1,0:T(8,128)}), f32[3,384,384]{2,1,0:T(8,128)}) %reduce-scatter.4.cloned.1.call-update) | async-done | bytes 1769488
  275.1 0.0 copy-done.2
  275.1 0.0 copy-done.3
  275.1 3.2 %add_select_fusion = f32[3,384,384]{2,1,0:T(8,128)} fusion(f32[3,384,384]{2,1,0:T(8,128)} %reduce-scatter.4.cloned.1.call-done, f32[3,384,384]{2,1,0:T(8,128)S(1)} %copy-done.2, f32[3]{0:T(128)S(1)} %add.56, f32[3,384]{1,0:T(4,128)S(1)} %copy-done.3, pred[3,384]{1,0:T(4,128)(4,1)S(1)} %iota_compare_fusion), kind=kLoop, calls=%fused_computation.7 | loop fusion | flops 2654208 | bytes 5314188 | tf_op jit(solution)/shard_map/jit(_where)/select_n | solution.py:36
  (10 shorter events, 0.0 us)
Async XLA Ops:
  6.5 100.2 %copy-start = (f32[16]{0:T(128)S(1)}, f32[16]{0:T(128)}, u32[]{:S(2)}) copy-start(f32[16]{0:T(128)} %param.11) | copy-start | bytes 196
  6.5 33.9 %all-gather.2.cloned.1.call-start = ((), (), s32[]{:S(2)}) async-start(), calls=%async_computation.1 | async-start | bytes 3538944 | tf_op jit(solution)/shard_map/all_gather | solution.py:10
  7.3 267.8 %reduce-scatter.4.cloned.1.call-start = ((), (), s32[]{:S(2)}) async-start(), calls=%async_computation.2 | async-start | bytes 30081024
  48.7 17.0 %copy-start.1 = (bf16[16,128,768]{2,1,0:T(8,128)(2,1)S(1)}, bf16[16,128,768]{2,1,0:T(8,128)(2,1)}, u32[]{:S(2)}) copy-start(bf16[16,128,768]{2,1,0:T(8,128)(2,1)} %all-gather.2.cloned.1.call-done) | copy-start | bytes 9437188
  105.9 0.7 copy-start.4
  106.0 2.1 copy-start.5
  106.0 169.2 %copy-start.2 = (f32[3,384,384]{2,1,0:T(8,128)S(1)}, f32[3,384,384]{2,1,0:T(8,128)}, u32[]{:S(2)}) copy-start(f32[3,384,384]{2,1,0:T(8,128)} %param.13) | copy-start | bytes 5308420
  106.0 169.2 %copy-start.3 = (f32[3,384]{1,0:T(4,128)S(1)}, f32[3,384]{1,0:T(4,128)}, u32[]{:S(2)}) copy-start(f32[3,384]{1,0:T(4,128)} %param.12) | copy-start | bytes 13828
Sparse Core Ops, SparseCore 0:
  9.0 31.3 all-gather.1
  106.1 168.9 reduce-scatter.3
where the time goes:
time: 285 us
  waiting for transfers between devices  200 us (70%)
  matrix products  50.8 us (18%)
  local copies, waits for them, and re-layouts  16.6 us (6%)
  between operations  13.4 us (5%)
  other arithmetic  4.08 us (1%)
    unnamed x3, waiting for transfers between devices  168 us
    all_gather x1, waiting for transfers between devices, body(): everyone = lax.all_gather(integrals, 'orb', axis=0, tiled=True)  32.4 us
    dot_general x1, matrix products, body(): jnp.einsum('pqa,pqb->pab', left, right, preferred_element_type=jnp.float32)  17 us
    dot_general x1, matrix products, body(): jnp.einsum('pqv,pva->pqa', everyone[pair_orbs[:, 0]], pno_maps, preferred...  17 us
    dot_general x1, matrix products, body(): jnp.einsum('pqv,pva->pqa', everyone[pair_orbs[:, 1]], pno_maps, preferred...  16.9 us
    gather x1, local copies, waits for them, and re-layouts, body(): everyone[pair_orbs[:, 0]]  8.26 us
    gather x1, local copies, waits for them, and re-layouts, body(): everyone[pair_orbs[:, 1]]  6.38 us
  transfers between devices with their start and end apart: 2, of which 2 were waited for; matrix products, arithmetic and copies ran while one was open for 1% of the time, Pallas kernels for 0%

commit v1 on v0

v1 whole, which is shorter than its diff:
```python
import functools

import jax
import jax.numpy as jnp
from jax import lax
from jax.experimental import pallas as pl
from jax.experimental.pallas import tpu as pltpu
from jax.sharding import PartitionSpec as P

NSMALL = 256
AXES = ("orb", "pair")
Y, C, X, Z = 4, 2, 4, 4
VMEM = 40 * 1024 * 1024


def flat(y, c, x, z):
    return (((y % Y) * C + c) * X + x % X) * Z + z % Z


def route(hop):
    return [
        (flat(y, c, x, z), flat(*hop(y, c, x, z)))
        for y in range(Y)
        for c in range(C)
        for x in range(X)
        for z in range(Z)
    ]


Y_ROUTE = route(lambda y, c, x, z: (y + 1 - 2 * c, c, x, z))
Z_ROUTE = route(lambda y, c, x, z: (y, c, x, z + 1 - 2 * c))
Y_FAR = route(lambda y, c, x, z: (y + 2, c, x, z))
Z_FAR = route(lambda y, c, x, z: (y, c, x, z + 2))
SWAP = route(lambda y, c, x, z: (y, 1 - c, x, z))
X_UP = route(lambda y, c, x, z: (y, c, x + 1, z))
X_DOWN = route(lambda y, c, x, z: (y, c, x - 1, z))


def send(value, way):
    return lax.ppermute(value, AXES, way)


def gather(own):
    other = send(own, SWAP)
    w = jnp.stack([own, other])
    ry, rz = send(w, Y_ROUTE), send(w, Z_ROUTE)
    ry2, rz2 = send(own, Y_FAR), send(own, Z_FAR)
    sy, sz = send(ry, SWAP), send(rz, SWAP)
    sy2, sz2 = send(ry2, SWAP), send(rz2, SWAP)
    rz3 = send(jnp.stack([ry[0, 0], ry[1, 0], sy[1, 0], sy[0, 0], ry2[0], sy2[0]]), Z_ROUTE)
    ry3 = send(jnp.stack([rz[0, 1], rz[1, 1], sz[1, 1], sz[0, 1], rz2[1], sz2[1]]), Y_ROUTE)
    rz5 = send(jnp.stack([rz3[0], rz3[2], rz3[4]]), Z_ROUTE)
    ry5 = send(jnp.stack([ry3[0], ry3[2], ry3[4]]), Y_ROUTE)
    sz3, sy3 = send(rz3, SWAP), send(ry3, SWAP)
    sz5, sy5 = send(rz5, SWAP), send(ry5, SWAP)
    pieces = dict(
        w=w, ry=ry, rz=rz, ry2=ry2, rz2=rz2, sy=sy, sz=sz, sy2=sy2, sz2=sz2,
        rz3=rz3, ry3=ry3, rz5=rz5, ry5=ry5, sz3=sz3, sy3=sy3, sz5=sz5, sy5=sy5,
    )
    flip = (0, 2, 1, 3)
    place = {}
    for l in range(2):
        for dc in range(2):
            place[0, 0, l, dc] = "w", (dc, l)
            for line in "yz":
                at = lambda d: (0, d) if line == "y" else (d, 0)
                place[(*at(1), l, dc)] = "r" + line, (dc, l)
                place[(*at(2), l, dc)] = "s" + line, (1 - dc, l)
                place[(*at(3), l, dc)] = "rs"[dc] + line + "2", (l,)
    for dc in range(2):
        for d in (1, 2, 3):
            for line, l in (("z", 0), ("y", 1)):
                at = lambda far: (far, d, l, dc) if line == "z" else (d, far, l, dc)
                place[at(1)] = "r" + line + "3", ((d - 1) * 2 + dc,)
                place[at(2)] = "s" + line + "3", ((flip[d] - 1) * 2 + 1 - dc,)
                place[at(3)] = ("r" + line + "5", (d - 1,)) if dc == 0 else ("s" + line + "5", (flip[d] - 1,))
    names = list(pieces)
    return list(pieces.values()), {k: (names.index(n), i) for k, (n, i) in place.items()}


def product(place, n_pieces, group, steps, rel, first, maps, pieces, buf, sems):
    step = pl.program_id(0)

    def copies(slot, side, r):
        found = []
        for dz in range(Z):
            piece, index = place[dz, r // 4, r // 2 % 2, r % 2]
            found.append(pltpu.make_async_copy(pieces[piece].at[index], buf.at[slot, side, dz], sems.at[slot, side, dz]))
        return found

    def fetch(which, slot):
        row = first[group] + which
        for side in range(2):
            mine = rel[row * 2 + side]
            for r in range(16):

                @pl.when(mine == r)
                def _(side=side, r=r):
                    for copy in copies(slot, side, r):
                        copy.start()

    slot = lax.rem(step, 2)

    @pl.when(step == 0)
    def _():
        fetch(0, 0)

    @pl.when(step + 1 < steps)
    def _():
        fetch(step + 1, 1 - slot)

    for side in range(2):
        for copy in copies(slot, side, 0):
            copy.wait()
    q, v = buf.shape[2] * buf.shape[3], buf.shape[4]
    dmap = maps[0]
    half = [
        jnp.dot(buf[slot, side].reshape(q, v), dmap, preferred_element_type=jnp.float32).astype(jnp.bfloat16)
        for side in range(2)
    ]
    return lax.dot_general(half[0], half[1], (((0,), (0,)), ((), ())), preferred_element_type=jnp.float32)


def partial_kernel(place, n, group, steps, rel, first, maps, *refs):
    pieces, (top, bottom), (buf, sems) = refs[:n], refs[n : n + 2], refs[n + 2 :]
    exchange = product(place, n, group, steps, rel, first, maps, pieces, buf, sems)
    rows = top.shape[1]
    top[0] = exchange[:rows].astype(top.dtype)
    bottom[0] = exchange[rows:].astype(bottom.dtype)


def own_kernel(place, n, group, steps, rel, first, maps, *refs):
    pieces, (high, low, occ, erow, ecol, amp), out, (buf, sems) = refs[:n], refs[n : n + 6], refs[n + 6], refs[n + 7 :]
    exchange = product(place, n, group, steps, rel, first, maps, pieces, buf, sems)
    denom = ecol[0] + erow[0] - occ[pl.program_id(0)]
    total = exchange + denom * amp[0]
    rows = high.shape[1]
    out[0, :rows] = total[:rows] + high[0].astype(jnp.float32)
    out[0, rows:] = total[rows:] + low[0].astype(jnp.float32)


def last_kernel(sizes, acc, high, low, out):
    p, h = pl.program_id(0), pl.program_id(1)
    size = sizes[p]
    rows, width = acc.shape[1:]
    a = lax.broadcasted_iota(jnp.int32, (rows, width), 0) + h * rows
    b = lax.broadcasted_iota(jnp.int32, (rows, width), 1)
    late = jnp.where(h == 0, high[0], low[0]).astype(jnp.float32)
    out[0] = jnp.where((a < size) & (b < size), acc[0] + late, 0.0)


def body(integrals, pno_maps, pair_orbs, pair_class, orbital_energy, pno_energy, amplitudes):
    groups = X * Z
    local_pairs, vectors, width = pno_maps.shape
    owned = local_pairs // groups
    rows = width // 2
    orb, spot = lax.axis_index("orb"), lax.axis_index("pair")
    y, c, x, z = orb // C, orb % C, spot // Z, spot % Z

    away = (pair_orbs // (2 * C) - y) % Y
    dy = jnp.where(away == 0, 0, jnp.where(away == 2, 3, jnp.where((away == 3) == (c == 0), 1, 2)))
    dc = (pair_orbs // 2 % C) ^ c
    rel = ((dy * 2 + pair_orbs % 2) * 2 + dc).reshape(-1).astype(jnp.int32)
    first = jnp.stack([owned * ((x + k) % X * Z + z) for k in range(X)]).astype(jnp.int32)

    pieces, place = gather(integrals)
    n = len(pieces)
    q = integrals.shape[1]
    anywhere = [pl.BlockSpec(memory_space=pl.ANY)] * n
    scratch = [
        pltpu.VMEM((2, 2, Z, q, vectors), jnp.bfloat16),
        pltpu.SemaphoreType.DMA((2, 2, Z)),
    ]
    flops = owned * (8 * Z * q * vectors * width // 2 + 2 * Z * q * width * width)
    cost = pl.CostEstimate(flops=flops, bytes_accessed=owned * (4 * Z * q * vectors + 2 * vectors * width + 4 * width * width), transcendentals=0)
    params = pltpu.CompilerParams(vmem_limit_bytes=VMEM)
    half = pl.BlockSpec((1, rows, width), lambda p, *_: (p, 0, 0))
    whole = pl.BlockSpec((1, width, width), lambda p, *_: (p, 0, 0))

    def maps_of(group):
        return pl.BlockSpec((1, vectors, width), lambda p, rel, first: (first[group] + p, 0, 0))

    def partial(group, kinds):
        return pl.pallas_call(
            functools.partial(partial_kernel, place, n, group, owned),
            grid_spec=pltpu.PrefetchScalarGridSpec(
                num_scalar_prefetch=2,
                grid=(owned,),
                in_specs=[maps_of(group), *anywhere],
                out_specs=[half, half],
                scratch_shapes=scratch,
            ),
            out_shape=[jax.ShapeDtypeStruct((owned, rows, width), kind) for kind in kinds],
            compiler_params=params,
            cost_estimate=cost,
        )(rel, first, pno_maps, *pieces)

    bf, f32 = jnp.bfloat16, jnp.float32
    far_top, far_bottom = partial(2, (bf, bf))
    far_top, far_bottom = send(far_top, X_UP), send(far_bottom, X_DOWN)
    up_top, up_bottom = partial(1, (f32, bf))
    up_bottom = send(up_bottom, X_UP)
    down_top, down_bottom = partial(3, (bf, f32))
    down_top = send(down_top, X_DOWN)
    up_top = send((up_top + far_top.astype(f32)).astype(bf), X_UP)
    down_bottom = send((down_bottom + far_bottom.astype(f32)).astype(bf), X_DOWN)

    start = spot * owned
    mine = lax.dynamic_slice_in_dim(pair_orbs, start, owned, 0)
    occupied = orbital_energy[mine[:, 0]] + orbital_energy[mine[:, 1]]
    sizes = NSMALL + pair_class * (width - NSMALL)
    acc = pl.pallas_call(
        functools.partial(own_kernel, place, n, 0, owned),
        grid_spec=pltpu.PrefetchScalarGridSpec(
            num_scalar_prefetch=2,
            grid=(owned,),
            in_specs=[
                maps_of(0),
                *anywhere,
                half,
                half,
                pl.BlockSpec(memory_space=pltpu.SMEM),
                pl.BlockSpec((1, 1, width), lambda p, *_: (p, 0, 0)),
                pl.BlockSpec((1, width, 1), lambda p, *_: (p, 0, 0)),
                whole,
            ],
            out_specs=whole,
            scratch_shapes=scratch,
        ),
        out_shape=jax.ShapeDtypeStruct((owned, width, width), f32),
        compiler_params=params,
        cost_estimate=cost,
    )(
        rel, first, pno_maps, *pieces, down_top, up_bottom, occupied,
        pno_energy[:, None, :], pno_energy[:, :, None], amplitudes,
    )
    part = pl.BlockSpec((1, rows, width), lambda p, h, *_: (p, h, 0))
    late = pl.BlockSpec((1, rows, width), lambda p, h, *_: (p, 0, 0))
    return pl.pallas_call(
        last_kernel,
        grid_spec=pltpu.PrefetchScalarGridSpec(
            num_scalar_prefetch=1, grid=(owned, 2), in_specs=[part, late, late], out_specs=part
        ),
        out_shape=jax.ShapeDtypeStruct((owned, width, width), f32),
        compiler_params=params,
    )(sizes, acc, up_top, down_bottom)


def solution(mesh):
    return jax.shard_map(
        body,
        mesh=mesh,
        in_specs=(
            P("orb", "pair", None),
            P("orb", None, None),
            P("orb", None),
            P(("orb", "pair")),
            P(),
            P(("orb", "pair"), None),
            P(("orb", "pair"), None, None),
        ),
        out_specs=P(("orb", "pair"), None, None),
        check_vma=False,
    )
```

time: 285 us -> 156 us (0.55); the launches traced: 285 us -> 153 us
  waiting for transfers between devices: 200 us -> 35.9 us
  matrix products: 50.8 us -> 0 us
  Pallas kernels: 0 us -> 50.3 us
  starting transfers between devices: 0.04 us -> 35.4 us
  between operations: 13.4 us -> 0.32 us
  local copies, waits for them, and re-layouts: 16.6 us -> 26.8 us
    unnamed x3 -> x0, waiting for transfers between devices: 168 us -> none
    dot_general x3 -> x0, matrix products: 50.8 us -> none  [the longest x1 17 us: body(): jnp.einsum('pqa,pqb->pab', left, right, preferred_element_type=jnp.float32)]
    pallas_call x0 -> x5, Pallas kernels: none -> 50.3 us  [the longest x3 32.4 us: partial(): pl.pallas_call(functools.partial(partial_kernel, place, n, group, owned),...]
    ppermute x0 -> x23, waiting for transfers between devices: none -> 35.9 us  [send(): return lax.ppermute(value, AXES, way)]
    ppermute x0 -> x23, starting transfers between devices: none -> 35.4 us  [send(): return lax.ppermute(value, AXES, way)]
    all_gather x1 -> x0, waiting for transfers between devices: 32.4 us -> none  [body(): everyone = lax.all_gather(integrals, 'orb', axis=0, tiled=True)]
    unnamed x12 -> x66, local copies, waits for them, and re-layouts: 0.66 us -> 20.2 us
    gather x2 -> x0, local copies, waits for them, and re-layouts: 14.6 us -> none  [the longest x1 8.26 us: body(): everyone[pair_orbs[:, 0]]]
  transfers between devices with their start and end apart: 2 -> 23, of which waited for: 2 -> 7; matrix products, arithmetic and copies ran while one was open for 1% -> 7% of each run, Pallas kernels for 0% -> 23%
where the time goes in v1:
time: 156 us; the launch traced here: 153 us
  Pallas kernels  50.3 us (32%)
  waiting for transfers between devices  35.9 us (23%)
  starting transfers between devices  35.4 us (23%)
  local copies, waits for them, and re-layouts  26.8 us (17%)
  other arithmetic  4.41 us (3%)
    ppermute x23, waiting for transfers between devices, send(): return lax.ppermute(value, AXES, way)  35.9 us
    ppermute x23, starting transfers between devices, send(): return lax.ppermute(value, AXES, way)  35.4 us
    pallas_call x3, Pallas kernels, partial(): pl.pallas_call(functools.partial(partial_kernel, place, n, group, owned),...  32.4 us
    unnamed x66, local copies, waits for them, and re-layouts  20.2 us
    pallas_call x1, Pallas kernels, body(): pl.pallas_call(functools.partial(own_kernel, place, n, 0, owned), grid_sp...  12.9 us
    pallas_call x1, Pallas kernels, body(): pl.pallas_call(last_kernel, grid_spec=pltpu.PrefetchScalarGridSpec(num_sc...  4.97 us
  transfers between devices with their start and end apart: 23, of which 7 were waited for; matrix products, arithmetic and copies ran while one was open for 7% of the time, Pallas kernels for 23%

profile of v1, /device:TPU:1, one launch (start us, length us, event | category | flops | bytes accessed | tf_op | source)
XLA Modules:
  0.0 153.1 jit_solution(15971303281307481323)
XLA Ops:
  0.0 1.4 collective-permute-start
  1.4 1.6 %collective-permute-done = bf16[2,128,768]{2,1,0:T(8,128)(2,1)S(1)} collective-permute-done((bf16[2,128,768]{2,1,0:T(8,128)(2,1)}, bf16[2,128,768]{2,1,0:T(8,128)(2,1)S(1)}, u32[]{:S(2)}, u32[]{:S(2)}) %collective-permute-start) | collective-permute-done | bytes 393248 | tf_op jit(solution)/shard_map/ppermute | solution.py:40
  4.1 3.9 %collective-permute-start.2 = (bf16[2,2,128,768]{3,2,1,0:T(8,128)(2,1)S(1)}, bf16[2,2,128,768]{3,2,1,0:T(8,128)(2,1)S(1)}, u32[]{:S(2)}, u32[]{:S(2)}) collective-permute-start(bf16[2,2,128,768]{3,2,1,0:T(8,128)(2,1)S(1)} %pad_maximum_fusion.refs_0_), channel_id=1, source_target_pairs={{0,1},{1,2},{2,3},{3,0},{4,5},{5,6},{6,7},{7,4},{8,9},{9,10},{10,1... | collective-permute-start | bytes 2359304 | tf_op jit(solution)/shard_map/ppermute | solution.py:40
  8.0 2.7 %collective-permute-start.1 = (bf16[2,2,128,768]{3,2,1,0:T(8,128)(2,1)S(1)}, bf16[2,2,128,768]{3,2,1,0:T(8,128)(2,1)S(1)}, u32[]{:S(2)}, u32[]{:S(2)}) collective-permute-start(bf16[2,2,128,768]{3,2,1,0:T(8,128)(2,1)S(1)} %pad_maximum_fusion.refs_0_), channel_id=1, source_target_pairs={{0,32},{1,33},{2,34},{3,35},{4,36},{5,37},{6,38},{7,39},{8,40},{9,... | collective-permute-start | bytes 2359304 | tf_op jit(solution)/shard_map/ppermute | solution.py:40
  11.1 12.1 %collective-permute-done.4.refs_4_ = bf16[2,128,768]{2,1,0:T(8,128)(2,1)S(1)} collective-permute-done((bf16[2,128,768]{2,1,0:T(8,128)(2,1)S(1)}, bf16[2,128,768]{2,1,0:T(8,128)(2,1)S(1)}, u32[]{:S(2)}, u32[]{:S(2)}) %collective-permute-start.4) | collective-permute-done | bytes 393248 | tf_op jit(solution)/shard_map/ppermute | solution.py:40
  23.1 5.4 %collective-permute-start.8 = (bf16[2,128,768]{2,1,0:T(8,128)(2,1)S(1)}, bf16[2,128,768]{2,1,0:T(8,128)(2,1)S(1)}, u32[]{:S(2)}, u32[]{:S(2)}) collective-permute-start(bf16[2,128,768]{2,1,0:T(8,128)(2,1)S(1)} %collective-permute-done.4.refs_4_), channel_id=1, source_target_pairs={{0,16},{1,17},{2,18},{3,19},{4,20},{5,21},{6,22},{7,23},{8,24},{9,... | collective-permute-start | bytes 1179656 | tf_op jit(solution)/shard_map/ppermute | solution.py:40
  30.1 1.8 %collective-permute-done.6.refs_6_ = bf16[2,2,128,768]{3,2,1,0:T(8,128)(2,1)S(1)} collective-permute-done((bf16[2,2,128,768]{3,2,1,0:T(8,128)(2,1)S(1)}, bf16[2,2,128,768]{3,2,1,0:T(8,128)(2,1)S(1)}, u32[]{:S(2)}, u32[]{:S(2)}) %collective-permute-start.6) | collective-permute-done | bytes 786464 | tf_op jit(solution)/shard_map/ppermute | solution.py:40
  32.8 2.4 %collective-permute-start.10 = (bf16[6,128,768]{2,1,0:T(8,128)(2,1)S(1)}, bf16[6,128,768]{2,1,0:T(8,128)(2,1)S(1)}, u32[]{:S(2)}, u32[]{:S(2)}) collective-permute-start(bf16[6,128,768]{2,1,0:T(8,128)(2,1)S(1)} %slice_dynamic-update-slice_fusion), channel_id=1, source_target_pairs={{0,32},{1,33},{2,34},{3,35},{4,36},{5,37},{6,38},{7,39},{8,40},{9,... | collective-permute-start | bytes 3538952 | tf_op jit(solution)/shard_map/ppermute | solution.py:40
  36.3 12.1 %collective-permute-done.10.refs_10_ = bf16[6,128,768]{2,1,0:T(8,128)(2,1)S(1)} collective-permute-done((bf16[6,128,768]{2,1,0:T(8,128)(2,1)S(1)}, bf16[6,128,768]{2,1,0:T(8,128)(2,1)S(1)}, u32[]{:S(2)}, u32[]{:S(2)}) %collective-permute-start.10) | collective-permute-done | bytes 1179680 | tf_op jit(solution)/shard_map/ppermute | solution.py:40
  48.5 3.5 %collective-permute-start.12 = (bf16[3,128,768]{2,1,0:T(8,128)(2,1)S(1)}, bf16[3,128,768]{2,1,0:T(8,128)(2,1)}, u32[]{:S(2)}, u32[]{:S(2)}) collective-permute-start(bf16[3,128,768]{2,1,0:T(8,128)(2,1)S(1)} %pad_maximum_fusion.2), channel_id=1, source_target_pairs={{0,32},{1,33},{2,34},{3,35},{4,36},{5,37},{6,38},{7,39},{8,40},{9,... | collective-permute-start | bytes 1769480 | tf_op jit(solution)/shard_map/ppermute | solution.py:40
  53.2 5.7 %collective-permute-done.12.refs_12_ = bf16[3,128,768]{2,1,0:T(8,128)(2,1)} collective-permute-done((bf16[3,128,768]{2,1,0:T(8,128)(2,1)S(1)}, bf16[3,128,768]{2,1,0:T(8,128)(2,1)}, u32[]{:S(2)}, u32[]{:S(2)}) %collective-permute-start.12) | collective-permute-done | bytes 589856 | tf_op jit(solution)/shard_map/ppermute | solution.py:40
  58.8 3.2 %collective-permute-start.16 = (bf16[3,128,768]{2,1,0:T(8,128)(2,1)}, bf16[3,128,768]{2,1,0:T(8,128)(2,1)}, u32[]{:S(2)}, u32[]{:S(2)}) collective-permute-start(bf16[3,128,768]{2,1,0:T(8,128)(2,1)} %collective-permute-done.12.refs_12_), channel_id=1, source_target_pairs={{0,16},{1,17},{2,18},{3,19},{4,20},{5,21},{6,22},{7,23},{8,24},{9,... | collective-permute-start | bytes 1769480 | tf_op jit(solution)/shard_map/ppermute | solution.py:40
  62.0 2.2 %collective-permute-start.15 = (bf16[3,128,768]{2,1,0:T(8,128)(2,1)}, bf16[3,128,768]{2,1,0:T(8,128)(2,1)}, u32[]{:S(2)}, u32[]{:S(2)}) collective-permute-start(bf16[3,128,768]{2,1,0:T(8,128)(2,1)} %collective-permute-done.11.refs_11_), channel_id=1, source_target_pairs={{0,16},{1,17},{2,18},{3,19},{4,20},{5,21},{6,22},{7,23},{8,24},{9,... | collective-permute-start | bytes 1769480 | tf_op jit(solution)/shard_map/ppermute | solution.py:40
  73.7 9.5 %shard_map.76 = (bf16[3,192,384]{2,1,0:T(8,128)(2,1)S(1)}, bf16[3,192,384]{2,1,0:T(8,128)(2,1)S(1)}) custom-call(s32[96]{0:T(128)S(1)} %reshape.3.rel, s32[4]{0:T(128)S(1)} %pad_add_fusion.first, bf16[48,768,384]{2,1,0:T(8,128)(2,1)} %maps.7, bf16[2,2,128,768]{3,2,1,0:T(8,128)(2,1)S(1)} %pad_maximum_fusion.refs_0_, bf16[2,2,128,768]{3,2,1,0:T(8,128)(2,1)S(1)} %copy-done.5, ...), custom_call_target="tpu_custom_call" | custom-call | flops 2264924160 | bytes 8257536 | tf_op jit(solution)/shard_map/pallas_call | solution.py:184
  83.1 2.6 %collective-permute-start.21 = (bf16[3,192,384]{2,1,0:T(8,128)(2,1)S(1)}, bf16[3,192,384]{2,1,0:T(8,128)(2,1)S(1)}, u32[]{:S(2)}, u32[]{:S(2)}) collective-permute-start(bf16[3,192,384]{2,1,0:T(8,128)(2,1)S(1)} %get-tuple-element.16), channel_id=1, source_target_pairs={{0,12},{1,13},{2,14},{3,15},{4,0},{5,1},{6,2},{7,3},{8,4},{9,5},{1... | collective-permute-start | bytes 1327112 | tf_op jit(solution)/shard_map/ppermute | solution.py:40
  85.7 1.6 %collective-permute-start.19 = (bf16[3,192,384]{2,1,0:T(8,128)(2,1)S(1)}, bf16[3,192,384]{2,1,0:T(8,128)(2,1)S(1)}, u32[]{:S(2)}, u32[]{:S(2)}) collective-permute-start(bf16[3,192,384]{2,1,0:T(8,128)(2,1)S(1)} %get-tuple-element.14), channel_id=1, source_target_pairs={{0,4},{1,5},{2,6},{3,7},{4,8},{5,9},{6,10},{7,11},{8,12},{9,13},{1... | collective-permute-start | bytes 1327112 | tf_op jit(solution)/shard_map/ppermute | solution.py:40
  87.3 10.1 %shard_map.74 = (f32[3,192,384]{2,1,0:T(8,128)S(1)}, bf16[3,192,384]{2,1,0:T(8,128)(2,1)}) custom-call(s32[96]{0:T(128)S(1)} %reshape.3.rel, s32[4]{0:T(128)S(1)} %pad_add_fusion.first, bf16[48,768,384]{2,1,0:T(8,128)(2,1)} %maps.7, bf16[2,2,128,768]{3,2,1,0:T(8,128)(2,1)S(1)} %pad_maximum_fusion.refs_0_, bf16[2,2,128,768]{3,2,1,0:T(8,128)(2,1)S(1)} %copy-done.5, ...), custom_call_target="tpu_custom_call" | custom-call | flops 2264924160 | bytes 8257536 | tf_op jit(solution)/shard_map/pallas_call | solution.py:184
  97.4 1.6 %collective-permute-start.18 = (bf16[3,192,384]{2,1,0:T(8,128)(2,1)}, bf16[3,192,384]{2,1,0:T(8,128)(2,1)}, u32[]{:S(2)}, u32[]{:S(2)}) collective-permute-start(bf16[3,192,384]{2,1,0:T(8,128)(2,1)} %get-tuple-element.12), channel_id=1, source_target_pairs={{0,4},{1,5},{2,6},{3,7},{4,8},{5,9},{6,10},{7,11},{8,12},{9,13},{1... | collective-permute-start | bytes 1327112 | tf_op jit(solution)/shard_map/ppermute | solution.py:40
  99.0 12.9 %shard_map.73 = (bf16[3,192,384]{2,1,0:T(8,128)(2,1)}, f32[3,192,384]{2,1,0:T(8,128)S(1)}) custom-call(s32[96]{0:T(128)S(1)} %reshape.3.rel, s32[4]{0:T(128)S(1)} %pad_add_fusion.first, bf16[48,768,384]{2,1,0:T(8,128)(2,1)} %maps.7, bf16[2,2,128,768]{3,2,1,0:T(8,128)(2,1)S(1)} %pad_maximum_fusion.refs_0_, bf16[2,2,128,768]{3,2,1,0:T(8,128)(2,1)S(1)} %copy-done.5, ...), custom_call_target="tpu_custom_call" | custom-call | flops 2264924160 | bytes 8257536 | tf_op jit(solution)/shard_map/pallas_call | solution.py:184
  118.9 1.8 %copy.10.refs_21_ = f32[3,384,1]{2,1,0:T(8,128)} copy(f32[3,384,1]{1,0,2:T(4,128)} %bitcast.45) | data formatting | bytes 9216 | tf_op jit(solution)/shard_map/broadcast_in_dim | solution.py:235
  122.0 2.5 %collective-permute-done.17.refs_17_ = bf16[3,192,384]{2,1,0:T(8,128)(2,1)} collective-permute-done((bf16[3,192,384]{2,1,0:T(8,128)(2,1)}, bf16[3,192,384]{2,1,0:T(8,128)(2,1)}, u32[]{:S(2)}, u32[]{:S(2)}) %collective-permute-start.17) | collective-permute-done | bytes 442400 | tf_op jit(solution)/shard_map/ppermute | solution.py:40
  133.7 12.9 %shard_map.75.acc = f32[3,384,384]{2,1,0:T(8,128)} custom-call(s32[96]{0:T(128)S(1)} %reshape.3.rel, s32[4]{0:T(128)S(1)} %copy-done.25, bf16[48,768,384]{2,1,0:T(8,128)(2,1)} %maps.7, bf16[2,2,128,768]{3,2,1,0:T(8,128)(2,1)S(1)} %pad_maximum_fusion.refs_0_, bf16[2,2,128,768]{3,2,1,0:T(8,128)(2,1)S(1)} %copy-done.6, bf16[2,2,128,768]{3,2,1,0:T(8,128)(2,1)S(1)} %copy-done.3, ...), custom_call_target="tpu_custom_call" | custom-call | flops 2264924160 | bytes 8257536 | tf_op jit(solution)/shard_map/pallas_call | solution.py:212
  146.6 1.5 copy-done.22
  148.1 5.0 %shard_map.77 = f32[3,384,384]{2,1,0:T(8,128)} custom-call(s32[3]{0:T(128)S(1)} %multiply_add_fusion.sizes, f32[3,384,384]{2,1,0:T(8,128)S(1)} %copy-done.22, bf16[3,192,384]{2,1,0:T(8,128)(2,1)} %collective-permute-done.20.high, bf16[3,192,384]{2,1,0:T(8,128)(2,1)} %collective-permute-done.22.low), custom_call_target="tpu_custom_call" | custom-call | tf_op jit(solution)/shard_map/pallas_call | solution.py:239
  (115 shorter events, 33.1 us)
Async XLA Ops:
  0.0 115.7 %copy-start = (f32[16]{0:T(128)S(1)}, f32[16]{0:T(128)}, u32[]{:S(2)}) copy-start(f32[16]{0:T(128)} %param.11) | copy-start | bytes 196
  0.0 3.0 %collective-permute-start = (bf16[2,128,768]{2,1,0:T(8,128)(2,1)}, bf16[2,128,768]{2,1,0:T(8,128)(2,1)S(1)}, u32[]{:S(2)}, u32[]{:S(2)}) collective-permute-start(bf16[2,128,768]{2,1,0:T(8,128)(2,1)} %param.7), channel_id=1, source_target_pairs={{0,16},{1,17},{2,18},{3,19},{4,20},{5,21},{6,22},{7,23},{8,24},{9,... | collective-permute-start | bytes 1179656 | tf_op jit(solution)/shard_map/ppermute | solution.py:40
  4.1 25.3 %collective-permute-start.2 = (bf16[2,2,128,768]{3,2,1,0:T(8,128)(2,1)S(1)}, bf16[2,2,128,768]{3,2,1,0:T(8,128)(2,1)S(1)}, u32[]{:S(2)}, u32[]{:S(2)}) collective-permute-start(bf16[2,2,128,768]{3,2,1,0:T(8,128)(2,1)S(1)} %pad_maximum_fusion.refs_0_), channel_id=1, source_target_pairs={{0,1},{1,2},{2,3},{3,0},{4,5},{5,6},{6,7},{7,4},{8,9},{9,10},{10,1... | collective-permute-start | bytes 2359304 | tf_op jit(solution)/shard_map/ppermute | solution.py:40
  8.0 21.5 %collective-permute-start.1 = (bf16[2,2,128,768]{3,2,1,0:T(8,128)(2,1)S(1)}, bf16[2,2,128,768]{3,2,1,0:T(8,128)(2,1)S(1)}, u32[]{:S(2)}, u32[]{:S(2)}) collective-permute-start(bf16[2,2,128,768]{3,2,1,0:T(8,128)(2,1)S(1)} %pad_maximum_fusion.refs_0_), channel_id=1, source_target_pairs={{0,32},{1,33},{2,34},{3,35},{4,36},{5,37},{6,38},{7,39},{8,40},{9,... | collective-permute-start | bytes 2359304 | tf_op jit(solution)/shard_map/ppermute | solution.py:40
  10.7 12.4 %collective-permute-start.4 = (bf16[2,128,768]{2,1,0:T(8,128)(2,1)S(1)}, bf16[2,128,768]{2,1,0:T(8,128)(2,1)S(1)}, u32[]{:S(2)}, u32[]{:S(2)}) collective-permute-start(bf16[2,128,768]{2,1,0:T(8,128)(2,1)S(1)} %copy-done.26), channel_id=1, source_target_pairs={{0,2},{1,3},{2,0},{3,1},{4,6},{5,7},{6,4},{7,5},{8,10},{9,11},{10,... | collective-permute-start | bytes 1179656 | tf_op jit(solution)/shard_map/ppermute | solution.py:40
  10.7 17.8 %collective-permute-start.3 = (bf16[2,128,768]{2,1,0:T(8,128)(2,1)S(1)}, bf16[2,128,768]{2,1,0:T(8,128)(2,1)S(1)}, u32[]{:S(2)}, u32[]{:S(2)}) collective-permute-start(bf16[2,128,768]{2,1,0:T(8,128)(2,1)S(1)} %copy-done.26), channel_id=1, source_target_pairs={{0,64},{1,65},{2,66},{3,67},{4,68},{5,69},{6,70},{7,71},{8,72},{9,... | collective-permute-start | bytes 1179656 | tf_op jit(solution)/shard_map/ppermute | solution.py:40
  23.1 8.8 %collective-permute-start.8 = (bf16[2,128,768]{2,1,0:T(8,128)(2,1)S(1)}, bf16[2,128,768]{2,1,0:T(8,128)(2,1)S(1)}, u32[]{:S(2)}, u32[]{:S(2)}) collective-permute-start(bf16[2,128,768]{2,1,0:T(8,128)(2,1)S(1)} %collective-permute-done.4.refs_4_), channel_id=1, source_target_pairs={{0,16},{1,17},{2,18},{3,19},{4,20},{5,21},{6,22},{7,23},{8,24},{9,... | collective-permute-start | bytes 1179656 | tf_op jit(solution)/shard_map/ppermute | solution.py:40
  28.5 6.8 %collective-permute-start.7 = (bf16[2,128,768]{2,1,0:T(8,128)(2,1)S(1)}, bf16[2,128,768]{2,1,0:T(8,128)(2,1)S(1)}, u32[]{:S(2)}, u32[]{:S(2)}) collective-permute-start(bf16[2,128,768]{2,1,0:T(8,128)(2,1)S(1)} %collective-permute-done.3.refs_3_), channel_id=1, source_target_pairs={{0,16},{1,17},{2,18},{3,19},{4,20},{5,21},{6,22},{7,23},{8,24},{9,... | collective-permute-start | bytes 1179656 | tf_op jit(solution)/shard_map/ppermute | solution.py:40
  29.4 2.5 %collective-permute-start.6 = (bf16[2,2,128,768]{3,2,1,0:T(8,128)(2,1)S(1)}, bf16[2,2,128,768]{3,2,1,0:T(8,128)(2,1)S(1)}, u32[]{:S(2)}, u32[]{:S(2)}) collective-permute-start(bf16[2,2,128,768]{3,2,1,0:T(8,128)(2,1)S(1)} %collective-permute-done.2.refs_2_), channel_id=1, source_target_pairs={{0,16},{1,17},{2,18},{3,19},{4,20},{5,21},{6,22},{7,23},{8,24},{9,... | collective-permute-start | bytes 2359304 | tf_op jit(solution)/shard_map/ppermute | solution.py:40
  29.5 5.7 %collective-permute-start.5 = (bf16[2,2,128,768]{3,2,1,0:T(8,128)(2,1)S(1)}, bf16[2,2,128,768]{3,2,1,0:T(8,128)(2,1)S(1)}, u32[]{:S(2)}, u32[]{:S(2)}) collective-permute-start(bf16[2,2,128,768]{3,2,1,0:T(8,128)(2,1)S(1)} %collective-permute-done.1.refs_1_), channel_id=1, source_target_pairs={{0,16},{1,17},{2,18},{3,19},{4,20},{5,21},{6,22},{7,23},{8,24},{9,... | collective-permute-start | bytes 2359304 | tf_op jit(solution)/shard_map/ppermute | solution.py:40
  32.8 15.5 %collective-permute-start.10 = (bf16[6,128,768]{2,1,0:T(8,128)(2,1)S(1)}, bf16[6,128,768]{2,1,0:T(8,128)(2,1)S(1)}, u32[]{:S(2)}, u32[]{:S(2)}) collective-permute-start(bf16[6,128,768]{2,1,0:T(8,128)(2,1)S(1)} %slice_dynamic-update-slice_fusion), channel_id=1, source_target_pairs={{0,32},{1,33},{2,34},{3,35},{4,36},{5,37},{6,38},{7,39},{8,40},{9,... | collective-permute-start | bytes 3538952 | tf_op jit(solution)/shard_map/ppermute | solution.py:40
  36.2 15.8 %collective-permute-start.9 = (bf16[6,128,768]{2,1,0:T(8,128)(2,1)S(1)}, bf16[6,128,768]{2,1,0:T(8,128)(2,1)S(1)}, u32[]{:S(2)}, u32[]{:S(2)}) collective-permute-start(bf16[6,128,768]{2,1,0:T(8,128)(2,1)S(1)} %slice_dynamic-update-slice_fusion.2), channel_id=1, source_target_pairs={{0,1},{1,2},{2,3},{3,0},{4,5},{5,6},{6,7},{7,4},{8,9},{9,10},{10,1... | collective-permute-start | bytes 3538952 | tf_op jit(solution)/shard_map/ppermute | solution.py:40
  48.5 10.3 %collective-permute-start.12 = (bf16[3,128,768]{2,1,0:T(8,128)(2,1)S(1)}, bf16[3,128,768]{2,1,0:T(8,128)(2,1)}, u32[]{:S(2)}, u32[]{:S(2)}) collective-permute-start(bf16[3,128,768]{2,1,0:T(8,128)(2,1)S(1)} %pad_maximum_fusion.2), channel_id=1, source_target_pairs={{0,32},{1,33},{2,34},{3,35},{4,36},{5,37},{6,38},{7,39},{8,40},{9,... | collective-permute-start | bytes 1769480 | tf_op jit(solution)/shard_map/ppermute | solution.py:40
  52.1 9.9 %collective-permute-start.11 = (bf16[3,128,768]{2,1,0:T(8,128)(2,1)S(1)}, bf16[3,128,768]{2,1,0:T(8,128)(2,1)}, u32[]{:S(2)}, u32[]{:S(2)}) collective-permute-start(bf16[3,128,768]{2,1,0:T(8,128)(2,1)S(1)} %pad_maximum_fusion.1), channel_id=1, source_target_pairs={{0,1},{1,2},{2,3},{3,0},{4,5},{5,6},{6,7},{7,4},{8,9},{9,10},{10,1... | collective-permute-start | bytes 1769480 | tf_op jit(solution)/shard_map/ppermute | solution.py:40
  52.6 13.5 %collective-permute-start.14 = (bf16[6,128,768]{2,1,0:T(8,128)(2,1)S(1)}, bf16[6,128,768]{2,1,0:T(8,128)(2,1)}, u32[]{:S(2)}, u32[]{:S(2)}) collective-permute-start(bf16[6,128,768]{2,1,0:T(8,128)(2,1)S(1)} %collective-permute-done.10.refs_10_), channel_id=1, source_target_pairs={{0,16},{1,17},{2,18},{3,19},{4,20},{5,21},{6,22},{7,23},{8,24},{9,... | collective-permute-start | bytes 3538952 | tf_op jit(solution)/shard_map/ppermute | solution.py:40
  53.1 13.1 %collective-permute-start.13 = (bf16[6,128,768]{2,1,0:T(8,128)(2,1)S(1)}, bf16[6,128,768]{2,1,0:T(8,128)(2,1)}, u32[]{:S(2)}, u32[]{:S(2)}) collective-permute-start(bf16[6,128,768]{2,1,0:T(8,128)(2,1)S(1)} %collective-permute-done.9.refs_9_), channel_id=1, source_target_pairs={{0,16},{1,17},{2,18},{3,19},{4,20},{5,21},{6,22},{7,23},{8,24},{9,... | collective-permute-start | bytes 3538952 | tf_op jit(solution)/shard_map/ppermute | solution.py:40
  58.8 7.1 %collective-permute-start.16 = (bf16[3,128,768]{2,1,0:T(8,128)(2,1)}, bf16[3,128,768]{2,1,0:T(8,128)(2,1)}, u32[]{:S(2)}, u32[]{:S(2)}) collective-permute-start(bf16[3,128,768]{2,1,0:T(8,128)(2,1)} %collective-permute-done.12.refs_12_), channel_id=1, source_target_pairs={{0,16},{1,17},{2,18},{3,19},{4,20},{5,21},{6,22},{7,23},{8,24},{9,... | collective-permute-start | bytes 1769480 | tf_op jit(solution)/shard_map/ppermute | solution.py:40
  62.0 4.1 %collective-permute-start.15 = (bf16[3,128,768]{2,1,0:T(8,128)(2,1)}, bf16[3,128,768]{2,1,0:T(8,128)(2,1)}, u32[]{:S(2)}, u32[]{:S(2)}) collective-permute-start(bf16[3,128,768]{2,1,0:T(8,128)(2,1)} %collective-permute-done.11.refs_11_), channel_id=1, source_target_pairs={{0,16},{1,17},{2,18},{3,19},{4,20},{5,21},{6,22},{7,23},{8,24},{9,... | collective-permute-start | bytes 1769480 | tf_op jit(solution)/shard_map/ppermute | solution.py:40
  83.1 28.9 %collective-permute-start.21 = (bf16[3,192,384]{2,1,0:T(8,128)(2,1)S(1)}, bf16[3,192,384]{2,1,0:T(8,128)(2,1)S(1)}, u32[]{:S(2)}, u32[]{:S(2)}) collective-permute-start(bf16[3,192,384]{2,1,0:T(8,128)(2,1)S(1)} %get-tuple-element.16), channel_id=1, source_target_pairs={{0,12},{1,13},{2,14},{3,15},{4,0},{5,1},{6,2},{7,3},{8,4},{9,5},{1... | collective-permute-start | bytes 1327112 | tf_op jit(solution)/shard_map/ppermute | solution.py:40
  85.7 28.0 %collective-permute-start.19 = (bf16[3,192,384]{2,1,0:T(8,128)(2,1)S(1)}, bf16[3,192,384]{2,1,0:T(8,128)(2,1)S(1)}, u32[]{:S(2)}, u32[]{:S(2)}) collective-permute-start(bf16[3,192,384]{2,1,0:T(8,128)(2,1)S(1)} %get-tuple-element.14), channel_id=1, source_target_pairs={{0,4},{1,5},{2,6},{3,7},{4,8},{5,9},{6,10},{7,11},{8,12},{9,13},{1... | collective-permute-start | bytes 1327112 | tf_op jit(solution)/shard_map/ppermute | solution.py:40
  97.4 24.6 %collective-permute-start.18 = (bf16[3,192,384]{2,1,0:T(8,128)(2,1)}, bf16[3,192,384]{2,1,0:T(8,128)(2,1)}, u32[]{:S(2)}, u32[]{:S(2)}) collective-permute-start(bf16[3,192,384]{2,1,0:T(8,128)(2,1)} %get-tuple-element.12), channel_id=1, source_target_pairs={{0,4},{1,5},{2,6},{3,7},{4,8},{5,9},{6,10},{7,11},{8,12},{9,13},{1... | collective-permute-start | bytes 1327112 | tf_op jit(solution)/shard_map/ppermute | solution.py:40
  111.9 12.5 %collective-permute-start.17 = (bf16[3,192,384]{2,1,0:T(8,128)(2,1)}, bf16[3,192,384]{2,1,0:T(8,128)(2,1)}, u32[]{:S(2)}, u32[]{:S(2)}) collective-permute-start(bf16[3,192,384]{2,1,0:T(8,128)(2,1)} %get-tuple-element.11), channel_id=1, source_target_pairs={{0,12},{1,13},{2,14},{3,15},{4,0},{5,1},{6,2},{7,3},{8,4},{9,5},{1... | collective-permute-start | bytes 1327112 | tf_op jit(solution)/shard_map/ppermute | solution.py:40
  112.9 33.7 %collective-permute-start.22 = (bf16[3,192,384]{2,1,0:T(8,128)(2,1)}, bf16[3,192,384]{2,1,0:T(8,128)(2,1)}, u32[]{:S(2)}, u32[]{:S(2)}) collective-permute-start(bf16[3,192,384]{2,1,0:T(8,128)(2,1)} %add_convert_fusion), channel_id=1, source_target_pairs={{0,12},{1,13},{2,14},{3,15},{4,0},{5,1},{6,2},{7,3},{8,4},{9,5},{1... | collective-permute-start | bytes 1327112 | tf_op jit(solution)/shard_map/ppermute | solution.py:40
  114.6 32.1 %collective-permute-start.20 = (bf16[3,192,384]{2,1,0:T(8,128)(2,1)}, bf16[3,192,384]{2,1,0:T(8,128)(2,1)}, u32[]{:S(2)}, u32[]{:S(2)}) collective-permute-start(bf16[3,192,384]{2,1,0:T(8,128)(2,1)} %add_convert_fusion.1), channel_id=1, source_target_pairs={{0,4},{1,5},{2,6},{3,7},{4,8},{5,9},{6,10},{7,11},{8,12},{9,13},{1... | collective-permute-start | bytes 1327112 | tf_op jit(solution)/shard_map/ppermute | solution.py:40
  (27 other events, 95.7 us)

commit v2 on v0

v2 whole, which is shorter than its diff:
```python
import functools

import jax
import jax.numpy as jnp
from jax import lax
from jax.experimental import pallas as pl
from jax.experimental.pallas import tpu as pltpu
from jax.sharding import PartitionSpec as P

NSMALL = 256
AXES = ("orb", "pair")
Y, C, X, Z = 4, 2, 4, 4
VMEM = 16 * 1024 * 1024


def flat(y, c, x, z):
    return (((y % Y) * C + c) * X + x % X) * Z + z % Z


def route(hop):
    return [
        (flat(y, c, x, z), flat(*hop(y, c, x, z)))
        for y in range(Y)
        for c in range(C)
        for x in range(X)
        for z in range(Z)
    ]


Y_ROUTE = route(lambda y, c, x, z: (y + 1 - 2 * c, c, x, z))
Z_ROUTE = route(lambda y, c, x, z: (y, c, x, z + 1 - 2 * c))
Y_FAR = route(lambda y, c, x, z: (y + 2, c, x, z))
Z_FAR = route(lambda y, c, x, z: (y, c, x, z + 2))
SWAP = route(lambda y, c, x, z: (y, 1 - c, x, z))
X_UP = route(lambda y, c, x, z: (y, c, x + 1, z))
X_DOWN = route(lambda y, c, x, z: (y, c, x - 1, z))


def send(value, way):
    return lax.ppermute(value, AXES, way)


def after(value, *others):
    return lax.optimization_barrier((value, *others))[0]


def gather(own):
    ry2, rz2 = send(own, Y_FAR), send(own, Z_FAR)
    other = send(own, SWAP)
    wa, wb = jnp.stack([own[0], other[0]]), jnp.stack([own[1], other[1]])
    ya, zb = send(wa, Y_ROUTE), send(wb, Z_ROUTE)
    yb, za = send(after(wb, ya, zb), Y_ROUTE), send(after(wa, ya, zb), Z_ROUTE)
    sya, szb, sry2, srz2 = (send(v, SWAP) for v in (ya, zb, ry2, rz2))
    on_z = jnp.stack([jnp.stack([ya[0], sya[1], ry2[0]]), jnp.stack([ya[1], sya[0], sry2[0]])])
    on_y = jnp.stack([jnp.stack([zb[0], szb[1], rz2[1]]), jnp.stack([zb[1], szb[0], srz2[1]])])
    rz3, ry3 = send(on_z, Z_ROUTE), send(on_y, Y_ROUTE)
    rz5, ry5 = send(rz3[0], Z_ROUTE), send(ry3[0], Y_ROUTE)
    syb, sza = send(after(yb, on_z, on_y), SWAP), send(after(za, on_z, on_y), SWAP)
    srz3, sry3, srz5, sry5 = (send(v, SWAP) for v in (rz3, ry3, rz5, ry5))
    return wa, wb, ya, sya, yb, syb, za, sza, zb, szb, ry2, sry2, rz2, srz2, rz3, srz3, rz5, srz5, ry3, sry3, ry5, sry5


FLIP = (0, 2, 1, 3)
N_PIECES = 22


def fetch(pieces, dy, l, dc, dst, sem):
    wa, wb, ya, sya, yb, syb, za, sza, zb, szb, ry2, sry2, rz2, srz2, rz3, srz3, rz5, srz5, ry3, sry3, ry5, sry5 = pieces
    def copy(src, dz):
        pltpu.make_async_copy(src, dst.at[dz], sem).start()

    flipped = jnp.where(dy == 3, 3, 3 - dy)

    @pl.when((l == 0) & (dy == 0))
    def _():
        copy(wa.at[dc], 0)
        copy(za.at[dc], 1)
        copy(sza.at[1 - dc], 2)

    @pl.when((l == 1) & (dy == 0))
    def _():
        copy(wb.at[dc], 0)
        copy(zb.at[dc], 1)
        copy(szb.at[1 - dc], 2)

    @pl.when((dy == 0) & (dc == 0))
    def _():
        copy(rz2.at[l], 3)

    @pl.when((dy == 0) & (dc == 1))
    def _():
        copy(srz2.at[l], 3)

    @pl.when((dy == 3) & (dc == 0))
    def _():
        copy(ry2.at[l], 0)

    @pl.when((dy == 3) & (dc == 1))
    def _():
        copy(sry2.at[l], 0)

    @pl.when((l == 0) & (dy != 0))
    def _():
        @pl.when(dy == 1)
        def _():
            copy(ya.at[dc], 0)

        @pl.when(dy == 2)
        def _():
            copy(sya.at[1 - dc], 0)

        copy(rz3.at[dc, dy - 1], 1)
        copy(srz3.at[1 - dc, flipped - 1], 2)

        @pl.when(dc == 0)
        def _():
            copy(rz5.at[dy - 1], 3)

        @pl.when(dc == 1)
        def _():
            copy(srz5.at[flipped - 1], 3)

    @pl.when((l == 1) & (dy == 1))
    def _():
        copy(yb.at[dc], 0)
        for dz in (1, 2, 3):
            copy(ry3.at[dc, dz - 1], dz)

    @pl.when((l == 1) & (dy == 2))
    def _():
        copy(syb.at[1 - dc], 0)
        for dz in (1, 2, 3):
            copy(sry3.at[1 - dc, FLIP[dz] - 1], dz)

    @pl.when((l == 1) & (dy == 3))
    def _():
        @pl.when(dc == 0)
        def _():
            for dz in (1, 2, 3):
                copy(ry5.at[dz - 1], dz)

        @pl.when(dc == 1)
        def _():
            for dz in (1, 2, 3):
                copy(sry5.at[FLIP[dz] - 1], dz)


def products(groups, here, orbs, maps, pieces, rows_of, dmaps, row_sems, sems, act):
    owned = dmaps.shape[0] // len(groups)
    pairs = owned * len(groups)

    def pair_of(n):
        row = here[2 + groups[0]] + n
        for i, group in enumerate(groups[1:], 1):
            row = jnp.where(n >= i * owned, here[2 + group] + n - i * owned, row)
        return row

    def start(n):
        pltpu.make_async_copy(maps.at[pair_of(n)], dmaps.at[n], sems.at[n]).start()

        @pl.loop(0, 2)
        def _(side):
            k = orbs[side, pair_of(n)]
            away = lax.rem(k // (2 * C) + Y - here[0], Y)
            near = jnp.where((away == 3) == (here[1] == 0), 1, 2)
            dy = jnp.where(away == 0, 0, jnp.where(away == 2, 3, near))
            slot = lax.rem(n, 2)
            fetch(pieces, dy, lax.rem(k, 2), lax.rem(k // 2 + here[1], 2), rows_of.at[slot, side], row_sems.at[slot, side])

    @pl.loop(0, pairs + 1)
    def _(n):
        @pl.when(n < pairs)
        def _():
            start(n)

        @pl.when(n > 0)
        def _():
            m = n - 1
            slot = lax.rem(m, 2)
            for side in range(2):
                rows = rows_of.at[slot, side]
                pltpu.make_async_copy(rows, rows, row_sems.at[slot, side]).wait()
            pltpu.make_async_copy(maps.at[0], dmaps.at[m], sems.at[m]).wait()
            q, v = rows_of.shape[2] * rows_of.shape[3], rows_of.shape[4]
            dmap = dmaps[m]
            half = [
                jnp.dot(rows_of[slot, side].reshape(q, v), dmap, preferred_element_type=jnp.float32).astype(jnp.bfloat16)
                for side in range(2)
            ]
            exchange = lax.dot_general(half[0], half[1], (((0,), (0,)), ((), ())), preferred_element_type=jnp.float32)
            for i, group in enumerate(groups):
                if len(groups) == 1:
                    act(group, m, exchange)
                else:

                    @pl.when((m >= i * owned) & (m < (i + 1) * owned))
                    def _(i=i, group=group):
                        act(group, m - i * owned, exchange)


def partial_kernel(groups, here, orbs, maps, *refs):
    pieces, outs, scratch = refs[:N_PIECES], refs[N_PIECES : N_PIECES + 2 * len(groups)], refs[-4:]

    def act(group, p, exchange):
        top, bottom = outs[2 * groups.index(group) :][:2]
        rows = top.shape[1]
        top[p] = exchange[:rows].astype(top.dtype)
        bottom[p] = exchange[rows:].astype(bottom.dtype)

    products(groups, here, orbs, maps, pieces, *scratch, act)


def own_kernel(here, orbs, maps, *refs):
    pieces, (high, low, orbital_energy, energy, amp, out) = refs[:N_PIECES], refs[N_PIECES : N_PIECES + 6]

    def act(_, p, exchange):
        row = here[2] + p
        occupied = orbital_energy[orbs[0, row]] + orbital_energy[orbs[1, row]]
        along = jnp.broadcast_to(energy[pl.ds(p, 1), :], exchange.shape)
        total = exchange + (along.T + along - occupied) * amp[p]
        rows = high.shape[1]
        out[p, :rows] = total[:rows] + high[p].astype(jnp.float32)
        out[p, rows:] = total[rows:] + low[p].astype(jnp.float32)

    products((0,), here, orbs, maps, pieces, *refs[-4:], act)


def last_kernel(kinds, acc, high, low, out, staged, sems):
    owned, rows, width = high.shape
    b = lax.broadcasted_iota(jnp.int32, (rows, width), 1)
    copies = []
    for p in range(owned):
        size = NSMALL + kinds[p] * (width - NSMALL)
        for begin, late in ((0, high), (rows, low)):
            a = lax.broadcasted_iota(jnp.int32, (rows, width), 0) + begin
            part = pl.ds(begin, rows)
            staged[p, part] = jnp.where((a < size) & (b < size), acc[p, part] + late[p].astype(jnp.float32), 0.0)
        copies.append(pltpu.make_async_copy(staged.at[p], out.at[p], sems.at[p]))
        copies[-1].start()
    for copy in copies:
        copy.wait()


def body(integrals, pno_maps, pair_orbs, pair_class, orbital_energy, pno_energy, amplitudes):
    local_pairs, vectors, width = pno_maps.shape
    owned = local_pairs // (X * Z)
    rows = width // 2
    orb, spot = lax.axis_index("orb"), lax.axis_index("pair")
    x, z = spot // Z, spot % Z
    here = jnp.stack([orb // C, orb % C] + [owned * ((x + k) % X * Z + z) for k in range(X)]).astype(jnp.int32)
    orbs = pair_orbs.T
    pno_maps = pltpu.with_memory_space_constraint(pno_maps, pltpu.HBM)

    pieces = [pltpu.with_memory_space_constraint(piece, pltpu.HBM) for piece in gather(integrals)]
    q = integrals.shape[1]
    smem, vmem, anywhere = (pl.BlockSpec(memory_space=m) for m in (pltpu.SMEM, pltpu.VMEM, pl.ANY))
    params = pltpu.CompilerParams(vmem_limit_bytes=VMEM)
    bf, f32 = jnp.bfloat16, jnp.float32

    def call(kernel, n_groups, shapes, *late):
        pairs = owned * n_groups
        return pl.pallas_call(
            kernel,
            in_specs=[smem, smem, anywhere] + [anywhere] * N_PIECES + [vmem, vmem, smem, vmem, vmem][: len(late)],
            out_specs=[vmem] * len(shapes),
            out_shape=shapes,
            scratch_shapes=[
                pltpu.VMEM((2, 2, Z, q, vectors), bf),
                pltpu.VMEM((pairs, vectors, width), bf),
                pltpu.SemaphoreType.DMA((2, 2)),
                pltpu.SemaphoreType.DMA((pairs,)),
            ],
            compiler_params=params,
            cost_estimate=pl.CostEstimate(
                flops=pairs * (4 * Z * q * vectors * width + 2 * Z * q * width * width),
                bytes_accessed=pairs * (2 * vectors * width + 4 * width * width),
                transcendentals=0,
            ),
        )(here, orbs, pno_maps, *pieces, *late)

    def partial(groups, *kinds):
        shapes = [jax.ShapeDtypeStruct((owned, rows, width), kind) for kind in kinds]
        return call(functools.partial(partial_kernel, groups), len(groups), shapes)

    far_top, far_bottom = partial((2,), bf, bf)
    far_top, far_bottom = send(far_top, X_UP), send(far_bottom, X_DOWN)
    up_top, up_bottom = partial((1,), f32, bf)
    up_bottom = send(up_bottom, X_UP)
    down_top, down_bottom = partial((3,), bf, f32)
    down_top = send(down_top, X_DOWN)
    up_top = send((up_top + far_top.astype(f32)).astype(bf), X_UP)
    down_bottom = send((down_bottom + far_bottom.astype(f32)).astype(bf), X_DOWN)

    whole = jax.ShapeDtypeStruct((owned, width, width), f32)
    (acc,) = call(own_kernel, 1, [whole], down_top, up_bottom, orbital_energy, pno_energy, amplitudes)
    return pl.pallas_call(
        last_kernel,
        in_specs=[smem, vmem, vmem, vmem],
        out_specs=anywhere,
        out_shape=whole,
        scratch_shapes=[pltpu.VMEM((owned, width, width), f32), pltpu.SemaphoreType.DMA((owned,))],
        compiler_params=params,
    )(pair_class, acc, up_top, down_bottom)


def solution(mesh):
    return jax.shard_map(
        body,
        mesh=mesh,
        in_specs=(
            P("orb", "pair", None),
            P("orb", None, None),
            P("orb", None),
            P(("orb", "pair")),
            P(),
            P(("orb", "pair"), None),
            P(("orb", "pair"), None, None),
        ),
        out_specs=P(("orb", "pair"), None, None),
        check_vma=False,
    )
```

time: 285 us -> 108 us (0.38)
  waiting for transfers between devices: 200 us -> 35.7 us
  matrix products: 50.8 us -> 0 us
  starting transfers between devices: 0.04 us -> 37.1 us
  Pallas kernels: 0 us -> 27.5 us
  between operations: 13.4 us -> 0.48 us
  local copies, waits for them, and re-layouts: 16.6 us -> 6.1 us
  other arithmetic: 4.08 us -> 0.78 us
    unnamed x3 -> x0, waiting for transfers between devices: 168 us -> none
    dot_general x3 -> x0, matrix products: 50.8 us -> none  [the longest x1 17 us: body(): jnp.einsum('pqa,pqb->pab', left, right, preferred_element_type=jnp.float32)]
    ppermute x0 -> x27, starting transfers between devices: none -> 37.1 us  [send(): return lax.ppermute(value, AXES, way)]
    ppermute x0 -> x27, waiting for transfers between devices: none -> 35.7 us  [send(): return lax.ppermute(value, AXES, way)]
    all_gather x1 -> x0, waiting for transfers between devices: 32.4 us -> none  [body(): everyone = lax.all_gather(integrals, 'orb', axis=0, tiled=True)]
    pallas_call x0 -> x5, Pallas kernels: none -> 27.5 us  [the longest x4 25.7 us: call(): pl.pallas_call(kernel, in_specs=[smem, smem, anywhere] + [anywhere] * N_P...]
    gather x4 -> x0, local copies, waits for them, and re-layouts: 15.9 us -> none  [the longest x1 8.26 us: body(): everyone[pair_orbs[:, 0]]]
    select_n x3 -> x0, other arithmetic: 3.98 us -> none  [the longest x1 3.21 us: body(): jnp.where(window, exchange + denom * amplitudes, jnp.zeros_like(exchange))]
  transfers between devices with their start and end apart: 2 -> 27, of which waited for: 2 -> 11; matrix products, arithmetic and copies ran while one was open for 1% -> 2% of each run, Pallas kernels for 0% -> 18%
where the time goes in v2:
time: 108 us
  starting transfers between devices  37.1 us (34%)
  waiting for transfers between devices  35.7 us (33%)
  Pallas kernels  27.5 us (25%)
  local copies, waits for them, and re-layouts  6.1 us (6%)
    ppermute x27, starting transfers between devices, send(): return lax.ppermute(value, AXES, way)  37.1 us
    ppermute x27, waiting for transfers between devices, send(): return lax.ppermute(value, AXES, way)  35.7 us
    pallas_call x4, Pallas kernels, call(): pl.pallas_call(kernel, in_specs=[smem, smem, anywhere] + [anywhere] * N_P...  25.7 us
    unnamed x40, local copies, waits for them, and re-layouts  3.58 us
  transfers between devices with their start and end apart: 27, of which 11 were waited for; matrix products, arithmetic and copies ran while one was open for 2% of the time, Pallas kernels for 18%

profile of v2, /device:TPU:1, one launch (start us, length us, event | category | flops | bytes accessed | tf_op | source)
XLA Modules:
  0.0 107.7 jit_solution(16051069486599145328)
XLA Ops:
  0.0 1.4 %collective-permute-start = (bf16[2,128,768]{2,1,0:T(8,128)(2,1)}, bf16[2,128,768]{2,1,0:T(8,128)(2,1)S(1)}, u32[]{:S(2)}, u32[]{:S(2)}) collective-permute-start(bf16[2,128,768]{2,1,0:T(8,128)(2,1)} %param.7), channel_id=1, source_target_pairs={{0,16},{1,17},{2,18},{3,19},{4,20},{5,21},{6,22},{7,23},{8,24},{9,... | collective-permute-start | bytes 1179656 | tf_op jit(solution)/shard_map/ppermute | solution.py:40
  1.4 3.7 %collective-permute-start.8 = (bf16[2,128,768]{2,1,0:T(8,128)(2,1)}, bf16[2,128,768]{2,1,0:T(8,128)(2,1)S(1)}, u32[]{:S(2)}, u32[]{:S(2)}) collective-permute-start(bf16[2,128,768]{2,1,0:T(8,128)(2,1)} %param.7), channel_id=1, source_target_pairs={{0,2},{1,3},{2,0},{3,1},{4,6},{5,7},{6,4},{7,5},{8,10},{9,11},{10,... | collective-permute-start | bytes 1179656 | tf_op jit(solution)/shard_map/ppermute | solution.py:40
  5.1 2.9 %collective-permute-start.5 = (bf16[2,128,768]{2,1,0:T(8,128)(2,1)}, bf16[2,128,768]{2,1,0:T(8,128)(2,1)S(1)}, u32[]{:S(2)}, u32[]{:S(2)}) collective-permute-start(bf16[2,128,768]{2,1,0:T(8,128)(2,1)} %param.7), channel_id=1, source_target_pairs={{0,64},{1,65},{2,66},{3,67},{4,68},{5,69},{6,70},{7,71},{8,72},{9,... | collective-permute-start | bytes 1179656 | tf_op jit(solution)/shard_map/ppermute | solution.py:40
  10.6 4.2 %collective-permute-done.8.refs_12_ = bf16[2,128,768]{2,1,0:T(8,128)(2,1)S(1)} collective-permute-done((bf16[2,128,768]{2,1,0:T(8,128)(2,1)}, bf16[2,128,768]{2,1,0:T(8,128)(2,1)S(1)}, u32[]{:S(2)}, u32[]{:S(2)}) %collective-permute-start.8) | collective-permute-done | bytes 393248 | tf_op jit(solution)/shard_map/ppermute | solution.py:40
  15.4 1.9 %collective-permute-done.5.refs_10_ = bf16[2,128,768]{2,1,0:T(8,128)(2,1)S(1)} collective-permute-done((bf16[2,128,768]{2,1,0:T(8,128)(2,1)}, bf16[2,128,768]{2,1,0:T(8,128)(2,1)S(1)}, u32[]{:S(2)}, u32[]{:S(2)}) %collective-permute-start.5) | collective-permute-done | bytes 393248 | tf_op jit(solution)/shard_map/ppermute | solution.py:40
  18.5 3.7 %collective-permute-done.1.refs_2_ = bf16[2,128,768]{2,1,0:T(8,128)(2,1)S(1)} collective-permute-done((bf16[2,128,768]{2,1,0:T(8,128)(2,1)S(1)}, bf16[2,128,768]{2,1,0:T(8,128)(2,1)S(1)}, u32[]{:S(2)}, u32[]{:S(2)}) %collective-permute-start.1) | collective-permute-done | bytes 393248 | tf_op jit(solution)/shard_map/ppermute | solution.py:40
  27.3 2.4 %collective-permute-start.17 = (bf16[2,3,128,768]{3,2,1,0:T(8,128)(2,1)S(1)}, bf16[2,3,128,768]{3,2,1,0:T(8,128)(2,1)S(1)}, u32[]{:S(2)}, u32[]{:S(2)}) collective-permute-start(bf16[2,3,128,768]{3,2,1,0:T(8,128)(2,1)S(1)} %pad_maximum_fusion.1), channel_id=1, source_target_pairs={{0,32},{1,33},{2,34},{3,35},{4,36},{5,37},{6,38},{7,39},{8,40},{9,... | collective-permute-start | bytes 3538952 | tf_op jit(solution)/shard_map/ppermute | solution.py:40
  30.7 10.7 %collective-permute-done.13.refs_14_ = bf16[2,3,128,768]{3,2,1,0:T(8,128)(2,1)S(1)} collective-permute-done((bf16[2,3,128,768]{3,2,1,0:T(8,128)(2,1)S(1)}, bf16[2,3,128,768]{3,2,1,0:T(8,128)(2,1)S(1)}, u32[]{:S(2)}, u32[]{:S(2)}) %collective-permute-start.13) | collective-permute-done | bytes 1179680 | tf_op jit(solution)/shard_map/ppermute | solution.py:40
  41.4 1.7 %collective-permute-start.15 = (bf16[3,128,768]{2,1,0:T(8,128)(2,1)S(1)}, bf16[3,128,768]{2,1,0:T(8,128)(2,1)}, u32[]{:S(2)}, u32[]{:S(2)}) collective-permute-start(bf16[3,128,768]{2,1,0:T(8,128)(2,1)S(1)} %slice_bitcast_fusion.1), channel_id=1, source_target_pairs={{0,1},{1,2},{2,3},{3,0},{4,5},{5,6},{6,7},{7,4},{8,9},{9,10},{10,1... | collective-permute-start | bytes 1769480 | tf_op jit(solution)/shard_map/ppermute | solution.py:40
  43.2 3.4 %collective-permute-start.19 = (bf16[3,128,768]{2,1,0:T(8,128)(2,1)S(1)}, bf16[3,128,768]{2,1,0:T(8,128)(2,1)}, u32[]{:S(2)}, u32[]{:S(2)}) collective-permute-start(bf16[3,128,768]{2,1,0:T(8,128)(2,1)S(1)} %slice_bitcast_fusion), channel_id=1, source_target_pairs={{0,32},{1,33},{2,34},{3,35},{4,36},{5,37},{6,38},{7,39},{8,40},{9,... | collective-permute-start | bytes 1769480 | tf_op jit(solution)/shard_map/ppermute | solution.py:40
  47.1 2.8 %collective-permute-start.18 = (bf16[2,3,128,768]{3,2,1,0:T(8,128)(2,1)S(1)}, bf16[2,3,128,768]{3,2,1,0:T(8,128)(2,1)}, u32[]{:S(2)}, u32[]{:S(2)}) collective-permute-start(bf16[2,3,128,768]{3,2,1,0:T(8,128)(2,1)S(1)} %collective-permute-done.17.refs_18_), channel_id=1, source_target_pairs={{0,16},{1,17},{2,18},{3,19},{4,20},{5,21},{6,22},{7,23},{8,24},{9,... | collective-permute-start | bytes 3538952 | tf_op jit(solution)/shard_map/ppermute | solution.py:40
  52.0 3.1 %collective-permute-start.16 = (bf16[3,128,768]{2,1,0:T(8,128)(2,1)}, bf16[3,128,768]{2,1,0:T(8,128)(2,1)}, u32[]{:S(2)}, u32[]{:S(2)}) collective-permute-start(bf16[3,128,768]{2,1,0:T(8,128)(2,1)} %collective-permute-done.15.refs_16_), channel_id=1, source_target_pairs={{0,16},{1,17},{2,18},{3,19},{4,20},{5,21},{6,22},{7,23},{8,24},{9,... | collective-permute-start | bytes 1769480 | tf_op jit(solution)/shard_map/ppermute | solution.py:40
  55.1 2.0 %collective-permute-start.20 = (bf16[3,128,768]{2,1,0:T(8,128)(2,1)}, bf16[3,128,768]{2,1,0:T(8,128)(2,1)}, u32[]{:S(2)}, u32[]{:S(2)}) collective-permute-start(bf16[3,128,768]{2,1,0:T(8,128)(2,1)} %collective-permute-done.19.refs_20_), channel_id=1, source_target_pairs={{0,16},{1,17},{2,18},{3,19},{4,20},{5,21},{6,22},{7,23},{8,24},{9,... | collective-permute-start | bytes 1769480 | tf_op jit(solution)/shard_map/ppermute | solution.py:40
  57.9 2.0 %collective-permute-done.12.refs_7_ = bf16[2,128,768]{2,1,0:T(8,128)(2,1)} collective-permute-done((bf16[2,128,768]{2,1,0:T(8,128)(2,1)}, bf16[2,128,768]{2,1,0:T(8,128)(2,1)}, u32[]{:S(2)}, u32[]{:S(2)}) %collective-permute-start.12) | collective-permute-done | bytes 393248 | tf_op jit(solution)/shard_map/ppermute | solution.py:40
  61.0 6.2 %shard_map.76 = (bf16[3,192,384]{2,1,0:T(8,128)(2,1)S(1)}, bf16[3,192,384]{2,1,0:T(8,128)(2,1)S(1)}) custom-call(s32[6]{0:T(128)S(1)} %stack.63.here, s32[2,48]{1,0:T(2,128)S(1)} %bitcast.19, bf16[48,768,384]{2,1,0:T(8,128)(2,1)} %maps.7, bf16[2,128,768]{2,1,0:T(8,128)(2,1)} %copy-done.8, bf16[2,128,768]{2,1,0:T(8,128)(2,1)} %copy-done.10, ...), custom_call_target="tpu_custom_call" | custom-call | flops 2264924160 | bytes 3538944 | tf_op jit(solution)/shard_map/pallas_call | solution.py:262
  67.2 1.9 %collective-permute-start.23 = (bf16[3,192,384]{2,1,0:T(8,128)(2,1)S(1)}, bf16[3,192,384]{2,1,0:T(8,128)(2,1)S(1)}, u32[]{:S(2)}, u32[]{:S(2)}) collective-permute-start(bf16[3,192,384]{2,1,0:T(8,128)(2,1)S(1)} %get-tuple-element.22), channel_id=1, source_target_pairs={{0,4},{1,5},{2,6},{3,7},{4,8},{5,9},{6,10},{7,11},{8,12},{9,13},{1... | collective-permute-start | bytes 1327112 | tf_op jit(solution)/shard_map/ppermute | solution.py:40
  69.9 6.2 %shard_map.74 = (f32[3,192,384]{2,1,0:T(8,128)S(1)}, bf16[3,192,384]{2,1,0:T(8,128)(2,1)S(1)}) custom-call(s32[6]{0:T(128)S(1)} %stack.63.here, s32[2,48]{1,0:T(2,128)S(1)} %bitcast.20, bf16[48,768,384]{2,1,0:T(8,128)(2,1)} %maps.7, bf16[2,128,768]{2,1,0:T(8,128)(2,1)} %copy-done.8, bf16[2,128,768]{2,1,0:T(8,128)(2,1)} %copy-done.10, ...), custom_call_target="tpu_custom_call" | custom-call | flops 2264924160 | bytes 3538944 | tf_op jit(solution)/shard_map/pallas_call | solution.py:262
  76.9 6.9 %shard_map.73 = (bf16[3,192,384]{2,1,0:T(8,128)(2,1)S(1)}, f32[3,192,384]{2,1,0:T(8,128)S(1)}) custom-call(s32[6]{0:T(128)S(1)} %stack.63.here, s32[2,48]{1,0:T(2,128)S(1)} %bitcast.21, bf16[48,768,384]{2,1,0:T(8,128)(2,1)} %maps.7, bf16[2,128,768]{2,1,0:T(8,128)(2,1)} %copy-done.8, bf16[2,128,768]{2,1,0:T(8,128)(2,1)} %copy-done.10, ...), custom_call_target="tpu_custom_call" | custom-call | flops 2264924160 | bytes 3538944 | tf_op jit(solution)/shard_map/pallas_call | solution.py:262
  83.8 1.6 %collective-permute-start.21 = (bf16[3,192,384]{2,1,0:T(8,128)(2,1)S(1)}, bf16[3,192,384]{2,1,0:T(8,128)(2,1)S(1)}, u32[]{:S(2)}, u32[]{:S(2)}) collective-permute-start(bf16[3,192,384]{2,1,0:T(8,128)(2,1)S(1)} %get-tuple-element.19), channel_id=1, source_target_pairs={{0,12},{1,13},{2,14},{3,15},{4,0},{5,1},{6,2},{7,3},{8,4},{9,5},{1... | collective-permute-start | bytes 1327112 | tf_op jit(solution)/shard_map/ppermute | solution.py:40
  85.9 2.6 %collective-permute-start.26 = (bf16[3,192,384]{2,1,0:T(8,128)(2,1)S(1)}, bf16[3,192,384]{2,1,0:T(8,128)(2,1)S(1)}, u32[]{:S(2)}, u32[]{:S(2)}) collective-permute-start(bf16[3,192,384]{2,1,0:T(8,128)(2,1)S(1)} %add_convert_fusion), channel_id=1, source_target_pairs={{0,12},{1,13},{2,14},{3,15},{4,0},{5,1},{6,2},{7,3},{8,4},{9,5},{1... | collective-permute-start | bytes 1327112 | tf_op jit(solution)/shard_map/ppermute | solution.py:40
  89.4 6.8 %collective-permute-done.21.refs_22_ = bf16[3,192,384]{2,1,0:T(8,128)(2,1)S(1)} collective-permute-done((bf16[3,192,384]{2,1,0:T(8,128)(2,1)S(1)}, bf16[3,192,384]{2,1,0:T(8,128)(2,1)S(1)}, u32[]{:S(2)}, u32[]{:S(2)}) %collective-permute-start.21) | collective-permute-done | bytes 442400 | tf_op jit(solution)/shard_map/ppermute | solution.py:40
  96.2 6.3 %shard_map.75.acc = f32[3,384,384]{2,1,0:T(8,128)S(1)} custom-call(s32[6]{0:T(128)S(1)} %stack.63.here, s32[2,48]{1,0:T(2,128)S(1)} %bitcast.22, bf16[48,768,384]{2,1,0:T(8,128)(2,1)} %maps.7, bf16[2,128,768]{2,1,0:T(8,128)(2,1)} %copy-done.8, bf16[2,128,768]{2,1,0:T(8,128)(2,1)} %copy-done.10, bf16[2,128,768]{2,1,0:T(8,128)(2,1)} %copy-done.9, ...), custom_call_target="tpu_custom_call" | custom-call | flops 2264924160 | bytes 3538944 | tf_op jit(solution)/shard_map/pallas_call | solution.py:262
  102.5 3.1 %collective-permute-done.26.low = bf16[3,192,384]{2,1,0:T(8,128)(2,1)S(1)} collective-permute-done((bf16[3,192,384]{2,1,0:T(8,128)(2,1)S(1)}, bf16[3,192,384]{2,1,0:T(8,128)(2,1)S(1)}, u32[]{:S(2)}, u32[]{:S(2)}) %collective-permute-start.26) | collective-permute-done | bytes 442400 | tf_op jit(solution)/shard_map/ppermute | solution.py:40
  105.7 1.9 %shard_map.77 = f32[3,384,384]{2,1,0:T(8,128)} custom-call(s32[3]{0:T(128)S(1)} %copy-done.3, f32[3,384,384]{2,1,0:T(8,128)S(1)} %shard_map.75.acc, bf16[3,192,384]{2,1,0:T(8,128)(2,1)S(1)} %collective-permute-done.24.high, bf16[3,192,384]{2,1,0:T(8,128)(2,1)S(1)} %collective-permute-done.26.low), custom_call_target="tpu_custom_call" | custom-call | tf_op jit(solution)/shard_map/pallas_call | solution.py:296
  (100 shorter events, 17.8 us)
Async XLA Ops:
  0.0 9.1 %collective-permute-start = (bf16[2,128,768]{2,1,0:T(8,128)(2,1)}, bf16[2,128,768]{2,1,0:T(8,128)(2,1)S(1)}, u32[]{:S(2)}, u32[]{:S(2)}) collective-permute-start(bf16[2,128,768]{2,1,0:T(8,128)(2,1)} %param.7), channel_id=1, source_target_pairs={{0,16},{1,17},{2,18},{3,19},{4,20},{5,21},{6,22},{7,23},{8,24},{9,... | collective-permute-start | bytes 1179656 | tf_op jit(solution)/shard_map/ppermute | solution.py:40
  1.4 13.4 %collective-permute-start.8 = (bf16[2,128,768]{2,1,0:T(8,128)(2,1)}, bf16[2,128,768]{2,1,0:T(8,128)(2,1)S(1)}, u32[]{:S(2)}, u32[]{:S(2)}) collective-permute-start(bf16[2,128,768]{2,1,0:T(8,128)(2,1)} %param.7), channel_id=1, source_target_pairs={{0,2},{1,3},{2,0},{3,1},{4,6},{5,7},{6,4},{7,5},{8,10},{9,11},{10,... | collective-permute-start | bytes 1179656 | tf_op jit(solution)/shard_map/ppermute | solution.py:40
  5.1 12.2 %collective-permute-start.5 = (bf16[2,128,768]{2,1,0:T(8,128)(2,1)}, bf16[2,128,768]{2,1,0:T(8,128)(2,1)S(1)}, u32[]{:S(2)}, u32[]{:S(2)}) collective-permute-start(bf16[2,128,768]{2,1,0:T(8,128)(2,1)} %param.7), channel_id=1, source_target_pairs={{0,64},{1,65},{2,66},{3,67},{4,68},{5,69},{6,70},{7,71},{8,72},{9,... | collective-permute-start | bytes 1179656 | tf_op jit(solution)/shard_map/ppermute | solution.py:40
  9.2 13.1 %collective-permute-start.1 = (bf16[2,128,768]{2,1,0:T(8,128)(2,1)S(1)}, bf16[2,128,768]{2,1,0:T(8,128)(2,1)S(1)}, u32[]{:S(2)}, u32[]{:S(2)}) collective-permute-start(bf16[2,128,768]{2,1,0:T(8,128)(2,1)S(1)} %pad_maximum_fusion.2.refs_0_), channel_id=1, source_target_pairs={{0,32},{1,33},{2,34},{3,35},{4,36},{5,37},{6,38},{7,39},{8,40},{9,... | collective-permute-start | bytes 1179656 | tf_op jit(solution)/shard_map/ppermute | solution.py:40
  10.1 12.5 %collective-permute-start.3 = (bf16[2,128,768]{2,1,0:T(8,128)(2,1)S(1)}, bf16[2,128,768]{2,1,0:T(8,128)(2,1)S(1)}, u32[]{:S(2)}, u32[]{:S(2)}) collective-permute-start(bf16[2,128,768]{2,1,0:T(8,128)(2,1)S(1)} %pad_maximum_fusion.3.refs_1_), channel_id=1, source_target_pairs={{0,1},{1,2},{2,3},{3,0},{4,5},{5,6},{6,7},{7,4},{8,9},{9,10},{10,1... | collective-permute-start | bytes 1179656 | tf_op jit(solution)/shard_map/ppermute | solution.py:40
  14.8 8.0 %collective-permute-start.9 = (bf16[2,128,768]{2,1,0:T(8,128)(2,1)S(1)}, bf16[2,128,768]{2,1,0:T(8,128)(2,1)S(1)}, u32[]{:S(2)}, u32[]{:S(2)}) collective-permute-start(bf16[2,128,768]{2,1,0:T(8,128)(2,1)S(1)} %collective-permute-done.8.refs_12_), channel_id=1, source_target_pairs={{0,16},{1,17},{2,18},{3,19},{4,20},{5,21},{6,22},{7,23},{8,24},{9,... | collective-permute-start | bytes 1179656 | tf_op jit(solution)/shard_map/ppermute | solution.py:40
  17.3 5.5 %collective-permute-start.6 = (bf16[2,128,768]{2,1,0:T(8,128)(2,1)S(1)}, bf16[2,128,768]{2,1,0:T(8,128)(2,1)S(1)}, u32[]{:S(2)}, u32[]{:S(2)}) collective-permute-start(bf16[2,128,768]{2,1,0:T(8,128)(2,1)S(1)} %collective-permute-done.5.refs_10_), channel_id=1, source_target_pairs={{0,16},{1,17},{2,18},{3,19},{4,20},{5,21},{6,22},{7,23},{8,24},{9,... | collective-permute-start | bytes 1179656 | tf_op jit(solution)/shard_map/ppermute | solution.py:40
  25.9 15.4 %collective-permute-start.13 = (bf16[2,3,128,768]{3,2,1,0:T(8,128)(2,1)S(1)}, bf16[2,3,128,768]{3,2,1,0:T(8,128)(2,1)S(1)}, u32[]{:S(2)}, u32[]{:S(2)}) collective-permute-start(bf16[2,3,128,768]{3,2,1,0:T(8,128)(2,1)S(1)} %pad_maximum_fusion), channel_id=1, source_target_pairs={{0,1},{1,2},{2,3},{3,0},{4,5},{5,6},{6,7},{7,4},{8,9},{9,10},{10,1... | collective-permute-start | bytes 3538952 | tf_op jit(solution)/shard_map/ppermute | solution.py:40
  27.3 15.8 %collective-permute-start.17 = (bf16[2,3,128,768]{3,2,1,0:T(8,128)(2,1)S(1)}, bf16[2,3,128,768]{3,2,1,0:T(8,128)(2,1)S(1)}, u32[]{:S(2)}, u32[]{:S(2)}) collective-permute-start(bf16[2,3,128,768]{3,2,1,0:T(8,128)(2,1)S(1)} %pad_maximum_fusion.1), channel_id=1, source_target_pairs={{0,32},{1,33},{2,34},{3,35},{4,36},{5,37},{6,38},{7,39},{8,40},{9,... | collective-permute-start | bytes 3538952 | tf_op jit(solution)/shard_map/ppermute | solution.py:40
  29.8 17.4 %collective-permute-start.4 = (bf16[2,128,768]{2,1,0:T(8,128)(2,1)S(1)}, bf16[2,128,768]{2,1,0:T(8,128)(2,1)S(1)}, u32[]{:S(2)}, u32[]{:S(2)}) collective-permute-start(bf16[2,128,768]{2,1,0:T(8,128)(2,1)S(1)} %pad_maximum_fusion.3.refs_1_), channel_id=1, source_target_pairs={{0,32},{1,33},{2,34},{3,35},{4,36},{5,37},{6,38},{7,39},{8,40},{9,... | collective-permute-start | bytes 1179656 | tf_op jit(solution)/shard_map/ppermute | solution.py:40
  30.5 19.4 %collective-permute-start.11 = (bf16[2,128,768]{2,1,0:T(8,128)(2,1)S(1)}, bf16[2,128,768]{2,1,0:T(8,128)(2,1)}, u32[]{:S(2)}, u32[]{:S(2)}) collective-permute-start(bf16[2,128,768]{2,1,0:T(8,128)(2,1)S(1)} %pad_maximum_fusion.2.refs_0_), channel_id=1, source_target_pairs={{0,1},{1,2},{2,3},{3,0},{4,5},{5,6},{6,7},{7,4},{8,9},{9,10},{10,1... | collective-permute-start | bytes 1179656 | tf_op jit(solution)/shard_map/ppermute | solution.py:40
  41.4 10.6 %collective-permute-start.15 = (bf16[3,128,768]{2,1,0:T(8,128)(2,1)S(1)}, bf16[3,128,768]{2,1,0:T(8,128)(2,1)}, u32[]{:S(2)}, u32[]{:S(2)}) collective-permute-start(bf16[3,128,768]{2,1,0:T(8,128)(2,1)S(1)} %slice_bitcast_fusion.1), channel_id=1, source_target_pairs={{0,1},{1,2},{2,3},{3,0},{4,5},{5,6},{6,7},{7,4},{8,9},{9,10},{10,1... | collective-permute-start | bytes 1769480 | tf_op jit(solution)/shard_map/ppermute | solution.py:40
  43.2 11.9 %collective-permute-start.19 = (bf16[3,128,768]{2,1,0:T(8,128)(2,1)S(1)}, bf16[3,128,768]{2,1,0:T(8,128)(2,1)}, u32[]{:S(2)}, u32[]{:S(2)}) collective-permute-start(bf16[3,128,768]{2,1,0:T(8,128)(2,1)S(1)} %slice_bitcast_fusion), channel_id=1, source_target_pairs={{0,32},{1,33},{2,34},{3,35},{4,36},{5,37},{6,38},{7,39},{8,40},{9,... | collective-permute-start | bytes 1769480 | tf_op jit(solution)/shard_map/ppermute | solution.py:40
  46.5 13.4 %collective-permute-start.14 = (bf16[2,3,128,768]{3,2,1,0:T(8,128)(2,1)S(1)}, bf16[2,3,128,768]{3,2,1,0:T(8,128)(2,1)S(1)}, u32[]{:S(2)}, u32[]{:S(2)}) collective-permute-start(bf16[2,3,128,768]{3,2,1,0:T(8,128)(2,1)S(1)} %collective-permute-done.13.refs_14_), channel_id=1, source_target_pairs={{0,16},{1,17},{2,18},{3,19},{4,20},{5,21},{6,22},{7,23},{8,24},{9,... | collective-permute-start | bytes 3538952 | tf_op jit(solution)/shard_map/ppermute | solution.py:40
  47.1 12.8 %collective-permute-start.18 = (bf16[2,3,128,768]{3,2,1,0:T(8,128)(2,1)S(1)}, bf16[2,3,128,768]{3,2,1,0:T(8,128)(2,1)}, u32[]{:S(2)}, u32[]{:S(2)}) collective-permute-start(bf16[2,3,128,768]{3,2,1,0:T(8,128)(2,1)S(1)} %collective-permute-done.17.refs_18_), channel_id=1, source_target_pairs={{0,16},{1,17},{2,18},{3,19},{4,20},{5,21},{6,22},{7,23},{8,24},{9,... | collective-permute-start | bytes 3538952 | tf_op jit(solution)/shard_map/ppermute | solution.py:40
  50.0 7.1 %collective-permute-start.10 = (bf16[2,128,768]{2,1,0:T(8,128)(2,1)S(1)}, bf16[2,128,768]{2,1,0:T(8,128)(2,1)S(1)}, u32[]{:S(2)}, u32[]{:S(2)}) collective-permute-start(bf16[2,128,768]{2,1,0:T(8,128)(2,1)S(1)} %collective-permute-done.4.refs_4_), channel_id=1, source_target_pairs={{0,16},{1,17},{2,18},{3,19},{4,20},{5,21},{6,22},{7,23},{8,24},{9,... | collective-permute-start | bytes 1179656 | tf_op jit(solution)/shard_map/ppermute | solution.py:40
  52.0 7.9 %collective-permute-start.16 = (bf16[3,128,768]{2,1,0:T(8,128)(2,1)}, bf16[3,128,768]{2,1,0:T(8,128)(2,1)}, u32[]{:S(2)}, u32[]{:S(2)}) collective-permute-start(bf16[3,128,768]{2,1,0:T(8,128)(2,1)} %collective-permute-done.15.refs_16_), channel_id=1, source_target_pairs={{0,16},{1,17},{2,18},{3,19},{4,20},{5,21},{6,22},{7,23},{8,24},{9,... | collective-permute-start | bytes 1769480 | tf_op jit(solution)/shard_map/ppermute | solution.py:40
  55.1 4.9 %collective-permute-start.20 = (bf16[3,128,768]{2,1,0:T(8,128)(2,1)}, bf16[3,128,768]{2,1,0:T(8,128)(2,1)}, u32[]{:S(2)}, u32[]{:S(2)}) collective-permute-start(bf16[3,128,768]{2,1,0:T(8,128)(2,1)} %collective-permute-done.19.refs_20_), channel_id=1, source_target_pairs={{0,16},{1,17},{2,18},{3,19},{4,20},{5,21},{6,22},{7,23},{8,24},{9,... | collective-permute-start | bytes 1769480 | tf_op jit(solution)/shard_map/ppermute | solution.py:40
  67.2 18.2 %collective-permute-start.23 = (bf16[3,192,384]{2,1,0:T(8,128)(2,1)S(1)}, bf16[3,192,384]{2,1,0:T(8,128)(2,1)S(1)}, u32[]{:S(2)}, u32[]{:S(2)}) collective-permute-start(bf16[3,192,384]{2,1,0:T(8,128)(2,1)S(1)} %get-tuple-element.22), channel_id=1, source_target_pairs={{0,4},{1,5},{2,6},{3,7},{4,8},{5,9},{6,10},{7,11},{8,12},{9,13},{1... | collective-permute-start | bytes 1327112 | tf_op jit(solution)/shard_map/ppermute | solution.py:40
  69.2 16.6 %collective-permute-start.25 = (bf16[3,192,384]{2,1,0:T(8,128)(2,1)S(1)}, bf16[3,192,384]{2,1,0:T(8,128)(2,1)S(1)}, u32[]{:S(2)}, u32[]{:S(2)}) collective-permute-start(bf16[3,192,384]{2,1,0:T(8,128)(2,1)S(1)} %get-tuple-element.24), channel_id=1, source_target_pairs={{0,12},{1,13},{2,14},{3,15},{4,0},{5,1},{6,2},{7,3},{8,4},{9,5},{1... | collective-permute-start | bytes 1327112 | tf_op jit(solution)/shard_map/ppermute | solution.py:40
  76.2 13.3 %collective-permute-start.22 = (bf16[3,192,384]{2,1,0:T(8,128)(2,1)S(1)}, bf16[3,192,384]{2,1,0:T(8,128)(2,1)S(1)}, u32[]{:S(2)}, u32[]{:S(2)}) collective-permute-start(bf16[3,192,384]{2,1,0:T(8,128)(2,1)S(1)} %get-tuple-element.20), channel_id=1, source_target_pairs={{0,4},{1,5},{2,6},{3,7},{4,8},{5,9},{6,10},{7,11},{8,12},{9,13},{1... | collective-permute-start | bytes 1327112 | tf_op jit(solution)/shard_map/ppermute | solution.py:40
  83.8 12.4 %collective-permute-start.21 = (bf16[3,192,384]{2,1,0:T(8,128)(2,1)S(1)}, bf16[3,192,384]{2,1,0:T(8,128)(2,1)S(1)}, u32[]{:S(2)}, u32[]{:S(2)}) collective-permute-start(bf16[3,192,384]{2,1,0:T(8,128)(2,1)S(1)} %get-tuple-element.19), channel_id=1, source_target_pairs={{0,12},{1,13},{2,14},{3,15},{4,0},{5,1},{6,2},{7,3},{8,4},{9,5},{1... | collective-permute-start | bytes 1327112 | tf_op jit(solution)/shard_map/ppermute | solution.py:40
  85.6 17.0 %collective-permute-start.24 = (bf16[3,192,384]{2,1,0:T(8,128)(2,1)S(1)}, bf16[3,192,384]{2,1,0:T(8,128)(2,1)S(1)}, u32[]{:S(2)}, u32[]{:S(2)}) collective-permute-start(bf16[3,192,384]{2,1,0:T(8,128)(2,1)S(1)} %add_convert_fusion.1), channel_id=1, source_target_pairs={{0,4},{1,5},{2,6},{3,7},{4,8},{5,9},{6,10},{7,11},{8,12},{9,13},{1... | collective-permute-start | bytes 1327112 | tf_op jit(solution)/shard_map/ppermute | solution.py:40
  85.9 19.8 %collective-permute-start.26 = (bf16[3,192,384]{2,1,0:T(8,128)(2,1)S(1)}, bf16[3,192,384]{2,1,0:T(8,128)(2,1)S(1)}, u32[]{:S(2)}, u32[]{:S(2)}) collective-permute-start(bf16[3,192,384]{2,1,0:T(8,128)(2,1)S(1)} %add_convert_fusion), channel_id=1, source_target_pairs={{0,12},{1,13},{2,14},{3,15},{4,0},{5,1},{6,2},{7,3},{8,4},{9,5},{1... | collective-permute-start | bytes 1327112 | tf_op jit(solution)/shard_map/ppermute | solution.py:40
  (25 other events, 182.2 us)

commit v3 on v2

--- a/solution.py
+++ b/solution.py
@@ -32,8 +32,8 @@
 Y_FAR = route(lambda y, c, x, z: (y + 2, c, x, z))
 Z_FAR = route(lambda y, c, x, z: (y, c, x, z + 2))
 SWAP = route(lambda y, c, x, z: (y, 1 - c, x, z))
-X_UP = route(lambda y, c, x, z: (y, c, x + 1, z))
-X_DOWN = route(lambda y, c, x, z: (y, c, x - 1, z))
+X_AHEAD = route(lambda y, c, x, z: (y, c, x + 1 - 2 * c, z))
+X_BEHIND = route(lambda y, c, x, z: (y, c, x - 1 + 2 * c, z))
 
 
 def send(value, way):
@@ -145,27 +145,23 @@
                 copy(sry5.at[FLIP[dz] - 1], dz)
 
 
-def products(groups, here, orbs, maps, pieces, rows_of, dmaps, row_sems, sems, act):
-    owned = dmaps.shape[0] // len(groups)
-    pairs = owned * len(groups)
-
-    def pair_of(n):
-        row = here[2 + groups[0]] + n
-        for i, group in enumerate(groups[1:], 1):
-            row = jnp.where(n >= i * owned, here[2 + group] + n - i * owned, row)
-        return row
-
-    def start(n):
-        pltpu.make_async_copy(maps.at[pair_of(n)], dmaps.at[n], sems.at[n]).start()
+def sweep(group, here, orbs, maps, pieces, scratch, act):
+    rows_of, dmaps, row_sems, map_sems = scratch
+    pairs = orbs.shape[1] // (X * Z)
+
+    def start(p):
+        row = here[2 + group] + p
+        slot = lax.rem(p, 2)
+        pltpu.make_async_copy(maps.at[row], dmaps.at[slot], map_sems.at[slot]).start()
 
         @pl.loop(0, 2)
         def _(side):
-            k = orbs[side, pair_of(n)]
+            k = orbs[side, row]
             away = lax.rem(k // (2 * C) + Y - here[0], Y)
             near = jnp.where((away == 3) == (here[1] == 0), 1, 2)
             dy = jnp.where(away == 0, 0, jnp.where(away == 2, 3, near))
-            slot = lax.rem(n, 2)
-            fetch(pieces, dy, lax.rem(k, 2), lax.rem(k // 2 + here[1], 2), rows_of.at[slot, side], row_sems.at[slot, side])
+            dc = lax.rem(k // 2 + here[1], 2)
+            fetch(pieces, dy, lax.rem(k, 2), dc, rows_of.at[slot, side], row_sems.at[slot, side])
 
     @pl.loop(0, pairs + 1)
     def _(n):
@@ -175,66 +171,65 @@
 
         @pl.when(n > 0)
         def _():
-            m = n - 1
-            slot = lax.rem(m, 2)
+            p = n - 1
+            slot = lax.rem(p, 2)
+            pltpu.make_async_copy(dmaps.at[slot], dmaps.at[slot], map_sems.at[slot]).wait()
             for side in range(2):
                 rows = rows_of.at[slot, side]
                 pltpu.make_async_copy(rows, rows, row_sems.at[slot, side]).wait()
-            pltpu.make_async_copy(maps.at[0], dmaps.at[m], sems.at[m]).wait()
             q, v = rows_of.shape[2] * rows_of.shape[3], rows_of.shape[4]
-            dmap = dmaps[m]
-            half = [
-                jnp.dot(rows_of[slot, side].reshape(q, v), dmap, preferred_element_type=jnp.float32).astype(jnp.bfloat16)
-                for side in range(2)
-            ]
-            exchange = lax.dot_general(half[0], half[1], (((0,), (0,)), ((), ())), preferred_element_type=jnp.float32)
-            for i, group in enumerate(groups):
-                if len(groups) == 1:
-                    act(group, m, exchange)
-                else:
-
-                    @pl.when((m >= i * owned) & (m < (i + 1) * owned))
-                    def _(i=i, group=group):
-                        act(group, m - i * owned, exchange)
-
-
-def partial_kernel(groups, here, orbs, maps, *refs):
-    pieces, outs, scratch = refs[:N_PIECES], refs[N_PIECES : N_PIECES + 2 * len(groups)], refs[-4:]
-
-    def act(group, p, exchange):
-        top, bottom = outs[2 * groups.index(group) :][:2]
-        rows = top.shape[1]
+            act(p, dmaps[slot], *(rows_of[slot, side].reshape(q, v) for side in range(2)))
+
+
+def left_t(dmap, rows):
+    product = lax.dot_general(dmap, rows, (((0,), (1,)), ((), ())), preferred_element_type=jnp.float32)
+    return product.astype(jnp.bfloat16)
+
+
+def right(dmap, rows):
+    return jnp.dot(rows, dmap, preferred_element_type=jnp.float32).astype(jnp.bfloat16)
+
+
+def meet(lt, r):
+    return jnp.dot(lt, r, preferred_element_type=jnp.float32)
+
+
+def partial_kernel(group, here, orbs, maps, *refs):
+    pieces, (top, bottom), scratch = refs[:N_PIECES], refs[N_PIECES : N_PIECES + 2], refs[N_PIECES + 2 :]
+    rows = top.shape[1]
+
+    def act(p, dmap, left_rows, right_rows):
+        exchange = meet(left_t(dmap, left_rows), right(dmap, right_rows))
         top[p] = exchange[:rows].astype(top.dtype)
         bottom[p] = exchange[rows:].astype(bottom.dtype)
 
-    products(groups, here, orbs, maps, pieces, *scratch, act)
+    sweep(group, here, orbs, maps, pieces, scratch, act)
 
 
 def own_kernel(here, orbs, maps, *refs):
-    pieces, (high, low, orbital_energy, energy, amp, out) = refs[:N_PIECES], refs[N_PIECES : N_PIECES + 6]
-
-    def act(_, p, exchange):
+    pieces, (orbital_energy, energy, amp, out) = refs[:N_PIECES], refs[N_PIECES : N_PIECES + 4]
+
+    def act(p, dmap, left_rows, right_rows):
         row = here[2] + p
         occupied = orbital_energy[orbs[0, row]] + orbital_energy[orbs[1, row]]
+        exchange = meet(left_t(dmap, left_rows), right(dmap, right_rows))
         along = jnp.broadcast_to(energy[pl.ds(p, 1), :], exchange.shape)
-        total = exchange + (along.T + along - occupied) * amp[p]
-        rows = high.shape[1]
-        out[p, :rows] = total[:rows] + high[p].astype(jnp.float32)
-        out[p, rows:] = total[rows:] + low[p].astype(jnp.float32)
-
-    products((0,), here, orbs, maps, pieces, *refs[-4:], act)
-
-
-def last_kernel(kinds, acc, high, low, out, staged, sems):
-    owned, rows, width = high.shape
+        out[p] = exchange + (along.T + along - occupied) * amp[p]
+
+    sweep(0, here, orbs, maps, pieces, refs[N_PIECES + 4 :], act)
+
+
+def last_kernel(kinds, acc, up_top, up_bottom, down_top, down_bottom, out, staged, sems):
+    owned, rows, width = up_top.shape
     b = lax.broadcasted_iota(jnp.int32, (rows, width), 1)
     copies = []
     for p in range(owned):
         size = NSMALL + kinds[p] * (width - NSMALL)
-        for begin, late in ((0, high), (rows, low)):
+        for begin, near, late in ((0, down_top, up_top), (rows, up_bottom, down_bottom)):
             a = lax.broadcasted_iota(jnp.int32, (rows, width), 0) + begin
             part = pl.ds(begin, rows)
-            staged[p, part] = jnp.where((a < size) & (b < size), acc[p, part] + late[p].astype(jnp.float32), 0.0)
+            total = acc[p, part] + near[p].astype(jnp.float32) + late[p].astype(jnp.float32)
+            staged[p, part] = jnp.where((a < size) & (b < size), total, 0.0)
         copies.append(pltpu.make_async_copy(staged.at[p], out.at[p], sems.at[p]))
         copies[-1].start()
     for copy in copies:
@@ -247,7 +242,9 @@
     rows = width // 2
     orb, spot = lax.axis_index("orb"), lax.axis_index("pair")
     x, z = spot // Z, spot % Z
-    here = jnp.stack([orb // C, orb % C] + [owned * ((x + k) % X * Z + z) for k in range(X)]).astype(jnp.int32)
+    c = orb % C
+    ahead = 1 - 2 * c
+    here = jnp.stack([orb // C, c] + [owned * ((x + k * ahead + 4 * X) % X * Z + z) for k in range(X)]).astype(jnp.int32)
     orbs = pair_orbs.T
     pno_maps = pltpu.with_memory_space_constraint(pno_maps, pltpu.HBM)
 
@@ -257,50 +254,49 @@
     params = pltpu.CompilerParams(vmem_limit_bytes=VMEM)
     bf, f32 = jnp.bfloat16, jnp.float32
 
-    def call(kernel, n_groups, shapes, *late):
-        pairs = owned * n_groups
+    def call(kernel, *shapes, more_specs=(), more=()):
         return pl.pallas_call(
             kernel,
-            in_specs=[smem, smem, anywhere] + [anywhere] * N_PIECES + [vmem, vmem, smem, vmem, vmem][: len(late)],
+            in_specs=[smem, smem, anywhere] + [anywhere] * N_PIECES + list(more_specs),
             out_specs=[vmem] * len(shapes),
             out_shape=shapes,
             scratch_shapes=[
                 pltpu.VMEM((2, 2, Z, q, vectors), bf),
-                pltpu.VMEM((pairs, vectors, width), bf),
+                pltpu.VMEM((2, vectors, width), bf),
                 pltpu.SemaphoreType.DMA((2, 2)),
-                pltpu.SemaphoreType.DMA((pairs,)),
+                pltpu.SemaphoreType.DMA((2,)),
             ],
             compiler_params=params,
             cost_estimate=pl.CostEstimate(
-                flops=pairs * (4 * Z * q * vectors * width + 2 * Z * q * width * width),
-                bytes_accessed=pairs * (2 * vectors * width + 4 * width * width),
+                flops=owned * (4 * Z * q * vectors * width + 2 * Z * q * width * width),
+                bytes_accessed=owned * (4 * Z * q * vectors + 2 * vectors * width + 4 * width * width),
                 transcendentals=0,
             ),
-        )(here, orbs, pno_maps, *pieces, *late)
-
-    def partial(groups, *kinds):
+        )(here, orbs, pno_maps, *pieces, *more)
+
+    def partial(group, *kinds):
         shapes = [jax.ShapeDtypeStruct((owned, rows, width), kind) for kind in kinds]
-        return call(functools.partial(partial_kernel, groups), len(groups), shapes)
-
-    far_top, far_bottom = partial((2,), bf, bf)
-    far_top, far_bottom = send(far_top, X_UP), send(far_bottom, X_DOWN)
-    up_top, up_bottom = partial((1,), f32, bf)
-    up_bottom = send(up_bottom, X_UP)
-    down_top, down_bottom = partial((3,), bf, f32)
-    down_top = send(down_top, X_DOWN)
-    up_top = send((up_top + far_top.astype(f32)).astype(bf), X_UP)
-    down_bottom = send((down_bottom + far_bottom.astype(f32)).astype(bf), X_DOWN)
+        return call(functools.partial(partial_kernel, group), *shapes)
+
+    far_top, far_bottom = partial(2, bf, bf)
+    far_top, far_bottom = send(far_top, X_AHEAD), send(far_bottom, X_BEHIND)
+    up_top, up_bottom = partial(1, f32, bf)
+    up_bottom = send(up_bottom, X_AHEAD)
+    down_top, down_bottom = partial(3, bf, f32)
+    down_top = send(down_top, X_BEHIND)
+    up_top = send((up_top + far_top.astype(f32)).astype(bf), X_AHEAD)
+    down_bottom = send((down_bottom + far_bottom.astype(f32)).astype(bf), X_BEHIND)
 
     whole = jax.ShapeDtypeStruct((owned, width, width), f32)
-    (acc,) = call(own_kernel, 1, [whole], down_top, up_bottom, orbital_energy, pno_energy, amplitudes)
+    (acc,) = call(own_kernel, whole, more_specs=[smem, vmem, vmem], more=(orbital_energy, pno_energy, amplitudes))
     return pl.pallas_call(
         last_kernel,
-        in_specs=[smem, vmem, vmem, vmem],
+        in_specs=[smem, vmem, vmem, vmem, vmem, vmem],
         out_specs=anywhere,
         out_shape=whole,
         scratch_shapes=[pltpu.VMEM((owned, width, width), f32), pltpu.SemaphoreType.DMA((owned,))],
         compiler_params=params,
-    )(pair_class, acc, up_top, down_bottom)
+    )(pair_class, acc, up_top, up_bottom, down_top, down_bottom)
 
 
 def solution(mesh):

time: 108 us -> 104 us (0.963)
  waiting for transfers between devices: 35.7 us -> 31.8 us
  starting transfers between devices: 37.1 us -> 39 us
  Pallas kernels: 27.5 us -> 26.4 us
    ppermute x27, waiting for transfers between devices: 35.7 us -> 31.8 us  [send(): return lax.ppermute(value, AXES, way)]
    ppermute x27, starting transfers between devices: 37.1 us -> 39 us  [send(): return lax.ppermute(value, AXES, way)]
    pallas_call x4, Pallas kernels: 25.7 us -> 24.5 us  [call(): pl.pallas_call(kernel, in_specs=[smem, smem, anywhere] + [anywhere] * N_P...]
where the time goes in v3:
time: 104 us
  starting transfers between devices  39 us (38%)
  waiting for transfers between devices  31.8 us (31%)
  Pallas kernels  26.4 us (25%)
  local copies, waits for them, and re-layouts  5.21 us (5%)
    ppermute x27, starting transfers between devices, send(): return lax.ppermute(value, AXES, way)  39 us
    ppermute x27, waiting for transfers between devices, send(): return lax.ppermute(value, AXES, way)  31.8 us
    pallas_call x4, Pallas kernels, call(): pl.pallas_call(kernel, in_specs=[smem, smem, anywhere] + [anywhere] * N_P...  24.5 us
    unnamed x40, local copies, waits for them, and re-layouts  3.82 us
  transfers between devices with their start and end apart: 27, of which 11 were waited for; matrix products, arithmetic and copies ran while one was open for 2% of the time, Pallas kernels for 18%

profile of v3, /device:TPU:1, one launch (start us, length us, event | category | flops | bytes accessed | tf_op | source)
XLA Modules:
  0.0 103.6 jit_solution(5694294880452015130)
XLA Ops:
  1.4 3.7 %collective-permute-start.8 = (bf16[2,128,768]{2,1,0:T(8,128)(2,1)}, bf16[2,128,768]{2,1,0:T(8,128)(2,1)S(1)}, u32[]{:S(2)}, u32[]{:S(2)}) collective-permute-start(bf16[2,128,768]{2,1,0:T(8,128)(2,1)} %param.7), channel_id=1, source_target_pairs={{0,2},{1,3},{2,0},{3,1},{4,6},{5,7},{6,4},{7,5},{8,10},{9,11},{10,... | collective-permute-start | bytes 1179656 | tf_op jit(solution)/shard_map/ppermute | solution.py:40
  5.1 2.9 %collective-permute-start.5 = (bf16[2,128,768]{2,1,0:T(8,128)(2,1)}, bf16[2,128,768]{2,1,0:T(8,128)(2,1)S(1)}, u32[]{:S(2)}, u32[]{:S(2)}) collective-permute-start(bf16[2,128,768]{2,1,0:T(8,128)(2,1)} %param.7), channel_id=1, source_target_pairs={{0,64},{1,65},{2,66},{3,67},{4,68},{5,69},{6,70},{7,71},{8,72},{9,... | collective-permute-start | bytes 1179656 | tf_op jit(solution)/shard_map/ppermute | solution.py:40
  9.7 5.1 %collective-permute-done.8.refs_12_ = bf16[2,128,768]{2,1,0:T(8,128)(2,1)S(1)} collective-permute-done((bf16[2,128,768]{2,1,0:T(8,128)(2,1)}, bf16[2,128,768]{2,1,0:T(8,128)(2,1)S(1)}, u32[]{:S(2)}, u32[]{:S(2)}) %collective-permute-start.8) | collective-permute-done | bytes 393248 | tf_op jit(solution)/shard_map/ppermute | solution.py:40
  15.5 2.8 %collective-permute-start.1 = (bf16[2,128,768]{2,1,0:T(8,128)(2,1)S(1)}, bf16[2,128,768]{2,1,0:T(8,128)(2,1)S(1)}, u32[]{:S(2)}, u32[]{:S(2)}) collective-permute-start(bf16[2,128,768]{2,1,0:T(8,128)(2,1)S(1)} %pad_maximum_fusion.2.refs_0_), channel_id=1, source_target_pairs={{0,32},{1,33},{2,34},{3,35},{4,36},{5,37},{6,38},{7,39},{8,40},{9,... | collective-permute-start | bytes 1179656 | tf_op jit(solution)/shard_map/ppermute | solution.py:40
  18.4 1.6 %collective-permute-done.3.refs_8_ = bf16[2,128,768]{2,1,0:T(8,128)(2,1)S(1)} collective-permute-done((bf16[2,128,768]{2,1,0:T(8,128)(2,1)S(1)}, bf16[2,128,768]{2,1,0:T(8,128)(2,1)S(1)}, u32[]{:S(2)}, u32[]{:S(2)}) %collective-permute-start.3) | collective-permute-done | bytes 393248 | tf_op jit(solution)/shard_map/ppermute | solution.py:40
  20.0 3.0 %collective-permute-done.1.refs_2_ = bf16[2,128,768]{2,1,0:T(8,128)(2,1)S(1)} collective-permute-done((bf16[2,128,768]{2,1,0:T(8,128)(2,1)S(1)}, bf16[2,128,768]{2,1,0:T(8,128)(2,1)S(1)}, u32[]{:S(2)}, u32[]{:S(2)}) %collective-permute-start.1) | collective-permute-done | bytes 393248 | tf_op jit(solution)/shard_map/ppermute | solution.py:40
  23.1 1.5 %collective-permute-start.2 = (bf16[2,128,768]{2,1,0:T(8,128)(2,1)S(1)}, bf16[2,128,768]{2,1,0:T(8,128)(2,1)S(1)}, u32[]{:S(2)}, u32[]{:S(2)}) collective-permute-start(bf16[2,128,768]{2,1,0:T(8,128)(2,1)S(1)} %collective-permute-done.1.refs_2_), channel_id=1, source_target_pairs={{0,16},{1,17},{2,18},{3,19},{4,20},{5,21},{6,22},{7,23},{8,24},{9,... | collective-permute-start | bytes 1179656 | tf_op jit(solution)/shard_map/ppermute | solution.py:40
  25.8 1.8 %collective-permute-start.17 = (bf16[2,3,128,768]{3,2,1,0:T(8,128)(2,1)S(1)}, bf16[2,3,128,768]{3,2,1,0:T(8,128)(2,1)S(1)}, u32[]{:S(2)}, u32[]{:S(2)}) collective-permute-start(bf16[2,3,128,768]{3,2,1,0:T(8,128)(2,1)S(1)} %pad_maximum_fusion.1), channel_id=1, source_target_pairs={{0,32},{1,33},{2,34},{3,35},{4,36},{5,37},{6,38},{7,39},{8,40},{9,... | collective-permute-start | bytes 3538952 | tf_op jit(solution)/shard_map/ppermute | solution.py:40
  28.5 3.5 %collective-permute-start.13 = (bf16[2,3,128,768]{3,2,1,0:T(8,128)(2,1)S(1)}, bf16[2,3,128,768]{3,2,1,0:T(8,128)(2,1)S(1)}, u32[]{:S(2)}, u32[]{:S(2)}) collective-permute-start(bf16[2,3,128,768]{3,2,1,0:T(8,128)(2,1)S(1)} %pad_maximum_fusion), channel_id=1, source_target_pairs={{0,1},{1,2},{2,3},{3,0},{4,5},{5,6},{6,7},{7,4},{8,9},{9,10},{10,1... | collective-permute-start | bytes 3538952 | tf_op jit(solution)/shard_map/ppermute | solution.py:40
  32.4 8.8 %collective-permute-done.17.refs_18_ = bf16[2,3,128,768]{3,2,1,0:T(8,128)(2,1)S(1)} collective-permute-done((bf16[2,3,128,768]{3,2,1,0:T(8,128)(2,1)S(1)}, bf16[2,3,128,768]{3,2,1,0:T(8,128)(2,1)S(1)}, u32[]{:S(2)}, u32[]{:S(2)}) %collective-permute-start.17) | collective-permute-done | bytes 1179680 | tf_op jit(solution)/shard_map/ppermute | solution.py:40
  41.2 3.0 %collective-permute-start.19 = (bf16[3,128,768]{2,1,0:T(8,128)(2,1)S(1)}, bf16[3,128,768]{2,1,0:T(8,128)(2,1)}, u32[]{:S(2)}, u32[]{:S(2)}) collective-permute-start(bf16[3,128,768]{2,1,0:T(8,128)(2,1)S(1)} %slice_bitcast_fusion), channel_id=1, source_target_pairs={{0,32},{1,33},{2,34},{3,35},{4,36},{5,37},{6,38},{7,39},{8,40},{9,... | collective-permute-start | bytes 1769480 | tf_op jit(solution)/shard_map/ppermute | solution.py:40
  45.2 3.6 %collective-permute-start.15 = (bf16[3,128,768]{2,1,0:T(8,128)(2,1)S(1)}, bf16[3,128,768]{2,1,0:T(8,128)(2,1)}, u32[]{:S(2)}, u32[]{:S(2)}) collective-permute-start(bf16[3,128,768]{2,1,0:T(8,128)(2,1)S(1)} %slice_bitcast_fusion.1), channel_id=1, source_target_pairs={{0,1},{1,2},{2,3},{3,0},{4,5},{5,6},{6,7},{7,4},{8,9},{9,10},{10,1... | collective-permute-start | bytes 1769480 | tf_op jit(solution)/shard_map/ppermute | solution.py:40
  50.2 1.6 %collective-permute-done.19.refs_20_ = bf16[3,128,768]{2,1,0:T(8,128)(2,1)} collective-permute-done((bf16[3,128,768]{2,1,0:T(8,128)(2,1)S(1)}, bf16[3,128,768]{2,1,0:T(8,128)(2,1)}, u32[]{:S(2)}, u32[]{:S(2)}) %collective-permute-start.19) | collective-permute-done | bytes 589856 | tf_op jit(solution)/shard_map/ppermute | solution.py:40
  51.8 2.9 %collective-permute-start.20 = (bf16[3,128,768]{2,1,0:T(8,128)(2,1)}, bf16[3,128,768]{2,1,0:T(8,128)(2,1)}, u32[]{:S(2)}, u32[]{:S(2)}) collective-permute-start(bf16[3,128,768]{2,1,0:T(8,128)(2,1)} %collective-permute-done.19.refs_20_), channel_id=1, source_target_pairs={{0,16},{1,17},{2,18},{3,19},{4,20},{5,21},{6,22},{7,23},{8,24},{9,... | collective-permute-start | bytes 1769480 | tf_op jit(solution)/shard_map/ppermute | solution.py:40
  57.4 2.0 %collective-permute-done.10.refs_5_ = bf16[2,128,768]{2,1,0:T(8,128)(2,1)} collective-permute-done((bf16[2,128,768]{2,1,0:T(8,128)(2,1)}, bf16[2,128,768]{2,1,0:T(8,128)(2,1)}, u32[]{:S(2)}, u32[]{:S(2)}) %collective-permute-start.10) | collective-permute-done | bytes 393248 | tf_op jit(solution)/shard_map/ppermute | solution.py:40
  60.4 6.1 %shard_map.75 = (bf16[3,192,384]{2,1,0:T(8,128)(2,1)S(1)}, bf16[3,192,384]{2,1,0:T(8,128)(2,1)S(1)}) custom-call(s32[6]{0:T(128)S(1)} %stack.63.here, s32[2,48]{1,0:T(2,128)S(1)} %bitcast.19, bf16[48,768,384]{2,1,0:T(8,128)(2,1)} %maps.7, bf16[2,128,768]{2,1,0:T(8,128)(2,1)} %copy-done.10, bf16[2,128,768]{2,1,0:T(8,128)(2,1)} %copy-done.8, ...), custom_call_target="tpu_custom_call" | custom-call | flops 2264924160 | bytes 8257536 | tf_op jit(solution)/shard_map/pallas_call | solution.py:258
  67.9 6.1 %shard_map.76 = (bf16[3,192,384]{2,1,0:T(8,128)(2,1)S(1)}, f32[3,192,384]{2,1,0:T(8,128)S(1)}) custom-call(s32[6]{0:T(128)S(1)} %stack.63.here, s32[2,48]{1,0:T(2,128)S(1)} %bitcast.20, bf16[48,768,384]{2,1,0:T(8,128)(2,1)} %maps.7, bf16[2,128,768]{2,1,0:T(8,128)(2,1)} %copy-done.10, bf16[2,128,768]{2,1,0:T(8,128)(2,1)} %copy-done.8, ...), custom_call_target="tpu_custom_call" | custom-call | flops 2264924160 | bytes 8257536 | tf_op jit(solution)/shard_map/pallas_call | solution.py:258
  75.2 1.5 %collective-permute-start.21 = (bf16[3,192,384]{2,1,0:T(8,128)(2,1)S(1)}, bf16[3,192,384]{2,1,0:T(8,128)(2,1)S(1)}, u32[]{:S(2)}, u32[]{:S(2)}) collective-permute-start(bf16[3,192,384]{2,1,0:T(8,128)(2,1)S(1)} %get-tuple-element.20), channel_id=1, source_target_pairs={{0,4},{1,5},{2,6},{3,7},{4,8},{5,9},{6,10},{7,11},{8,12},{9,13},{1... | collective-permute-start | bytes 1327112 | tf_op jit(solution)/shard_map/ppermute | solution.py:40
  76.7 6.1 %shard_map.74 = (f32[3,192,384]{2,1,0:T(8,128)S(1)}, bf16[3,192,384]{2,1,0:T(8,128)(2,1)S(1)}) custom-call(s32[6]{0:T(128)S(1)} %stack.63.here, s32[2,48]{1,0:T(2,128)S(1)} %bitcast.21, bf16[48,768,384]{2,1,0:T(8,128)(2,1)} %maps.7, bf16[2,128,768]{2,1,0:T(8,128)(2,1)} %copy-done.10, bf16[2,128,768]{2,1,0:T(8,128)(2,1)} %copy-done.8, ...), custom_call_target="tpu_custom_call" | custom-call | flops 2264924160 | bytes 8257536 | tf_op jit(solution)/shard_map/pallas_call | solution.py:258
  84.8 1.9 %collective-permute-done.21 = bf16[3,192,384]{2,1,0:T(8,128)(2,1)S(1)} collective-permute-done((bf16[3,192,384]{2,1,0:T(8,128)(2,1)S(1)}, bf16[3,192,384]{2,1,0:T(8,128)(2,1)S(1)}, u32[]{:S(2)}, u32[]{:S(2)}) %collective-permute-start.21) | collective-permute-done | bytes 442400 | tf_op jit(solution)/shard_map/ppermute | solution.py:40
  86.8 3.3 %collective-permute-start.22 = (bf16[3,192,384]{2,1,0:T(8,128)(2,1)S(1)}, bf16[3,192,384]{2,1,0:T(8,128)(2,1)S(1)}, u32[]{:S(2)}, u32[]{:S(2)}) collective-permute-start(bf16[3,192,384]{2,1,0:T(8,128)(2,1)S(1)} %add_convert_fusion.1), channel_id=1, source_target_pairs={{0,4},{1,5},{2,6},{3,7},{4,8},{5,9},{6,10},{7,11},{8,12},{9,13},{1... | collective-permute-start | bytes 1327112 | tf_op jit(solution)/shard_map/ppermute | solution.py:40
  90.1 6.1 %shard_map.73.acc = f32[3,384,384]{2,1,0:T(8,128)S(1)} custom-call(s32[6]{0:T(128)S(1)} %stack.63.here, s32[2,48]{1,0:T(2,128)S(1)} %bitcast.22, bf16[48,768,384]{2,1,0:T(8,128)(2,1)} %maps.7, bf16[2,128,768]{2,1,0:T(8,128)(2,1)} %copy-done.10, bf16[2,128,768]{2,1,0:T(8,128)(2,1)} %copy-done.8, bf16[2,128,768]{2,1,0:T(8,128)(2,1)} %copy-done.11, ...), custom_call_target="tpu_custom_call" | custom-call | flops 2264924160 | bytes 8257536 | tf_op jit(solution)/shard_map/pallas_call | solution.py:258
  96.3 5.3 %collective-permute-done.22.up_top = bf16[3,192,384]{2,1,0:T(8,128)(2,1)S(1)} collective-permute-done((bf16[3,192,384]{2,1,0:T(8,128)(2,1)S(1)}, bf16[3,192,384]{2,1,0:T(8,128)(2,1)S(1)}, u32[]{:S(2)}, u32[]{:S(2)}) %collective-permute-start.22) | collective-permute-done | bytes 442400 | tf_op jit(solution)/shard_map/ppermute | solution.py:40
  101.6 1.9 %shard_map.77 = f32[3,384,384]{2,1,0:T(8,128)} custom-call(s32[3]{0:T(128)S(1)} %copy-done.4, f32[3,384,384]{2,1,0:T(8,128)S(1)} %shard_map.73.acc, bf16[3,192,384]{2,1,0:T(8,128)(2,1)S(1)} %collective-permute-done.22.up_top, bf16[3,192,384]{2,1,0:T(8,128)(2,1)S(1)} %collective-permute-done.23.up_bottom, ...), custom_call_target="tpu_custom_call" | custom-call | tf_op jit(solution)/shard_map/pallas_call | solution.py:292
  (99 shorter events, 16.9 us)
Async XLA Ops:
  0.0 9.1 %collective-permute-start = (bf16[2,128,768]{2,1,0:T(8,128)(2,1)}, bf16[2,128,768]{2,1,0:T(8,128)(2,1)S(1)}, u32[]{:S(2)}, u32[]{:S(2)}) collective-permute-start(bf16[2,128,768]{2,1,0:T(8,128)(2,1)} %param.7), channel_id=1, source_target_pairs={{0,16},{1,17},{2,18},{3,19},{4,20},{5,21},{6,22},{7,23},{8,24},{9,... | collective-permute-start | bytes 1179656 | tf_op jit(solution)/shard_map/ppermute | solution.py:40
  1.4 13.4 %collective-permute-start.8 = (bf16[2,128,768]{2,1,0:T(8,128)(2,1)}, bf16[2,128,768]{2,1,0:T(8,128)(2,1)S(1)}, u32[]{:S(2)}, u32[]{:S(2)}) collective-permute-start(bf16[2,128,768]{2,1,0:T(8,128)(2,1)} %param.7), channel_id=1, source_target_pairs={{0,2},{1,3},{2,0},{3,1},{4,6},{5,7},{6,4},{7,5},{8,10},{9,11},{10,... | collective-permute-start | bytes 1179656 | tf_op jit(solution)/shard_map/ppermute | solution.py:40
  5.1 13.2 %collective-permute-start.5 = (bf16[2,128,768]{2,1,0:T(8,128)(2,1)}, bf16[2,128,768]{2,1,0:T(8,128)(2,1)S(1)}, u32[]{:S(2)}, u32[]{:S(2)}) collective-permute-start(bf16[2,128,768]{2,1,0:T(8,128)(2,1)} %param.7), channel_id=1, source_target_pairs={{0,64},{1,65},{2,66},{3,67},{4,68},{5,69},{6,70},{7,71},{8,72},{9,... | collective-permute-start | bytes 1179656 | tf_op jit(solution)/shard_map/ppermute | solution.py:40
  9.2 10.8 %collective-permute-start.3 = (bf16[2,128,768]{2,1,0:T(8,128)(2,1)S(1)}, bf16[2,128,768]{2,1,0:T(8,128)(2,1)S(1)}, u32[]{:S(2)}, u32[]{:S(2)}) collective-permute-start(bf16[2,128,768]{2,1,0:T(8,128)(2,1)S(1)} %pad_maximum_fusion.3.refs_1_), channel_id=1, source_target_pairs={{0,1},{1,2},{2,3},{3,0},{4,5},{5,6},{6,7},{7,4},{8,9},{9,10},{10,1... | collective-permute-start | bytes 1179656 | tf_op jit(solution)/shard_map/ppermute | solution.py:40
  14.8 5.2 %collective-permute-start.9 = (bf16[2,128,768]{2,1,0:T(8,128)(2,1)S(1)}, bf16[2,128,768]{2,1,0:T(8,128)(2,1)S(1)}, u32[]{:S(2)}, u32[]{:S(2)}) collective-permute-start(bf16[2,128,768]{2,1,0:T(8,128)(2,1)S(1)} %collective-permute-done.8.refs_12_), channel_id=1, source_target_pairs={{0,16},{1,17},{2,18},{3,19},{4,20},{5,21},{6,22},{7,23},{8,24},{9,... | collective-permute-start | bytes 1179656 | tf_op jit(solution)/shard_map/ppermute | solution.py:40
  15.5 7.5 %collective-permute-start.1 = (bf16[2,128,768]{2,1,0:T(8,128)(2,1)S(1)}, bf16[2,128,768]{2,1,0:T(8,128)(2,1)S(1)}, u32[]{:S(2)}, u32[]{:S(2)}) collective-permute-start(bf16[2,128,768]{2,1,0:T(8,128)(2,1)S(1)} %pad_maximum_fusion.2.refs_0_), channel_id=1, source_target_pairs={{0,32},{1,33},{2,34},{3,35},{4,36},{5,37},{6,38},{7,39},{8,40},{9,... | collective-permute-start | bytes 1179656 | tf_op jit(solution)/shard_map/ppermute | solution.py:40
  18.3 6.2 %collective-permute-start.6 = (bf16[2,128,768]{2,1,0:T(8,128)(2,1)S(1)}, bf16[2,128,768]{2,1,0:T(8,128)(2,1)S(1)}, u32[]{:S(2)}, u32[]{:S(2)}) collective-permute-start(bf16[2,128,768]{2,1,0:T(8,128)(2,1)S(1)} %collective-permute-done.5.refs_10_), channel_id=1, source_target_pairs={{0,16},{1,17},{2,18},{3,19},{4,20},{5,21},{6,22},{7,23},{8,24},{9,... | collective-permute-start | bytes 1179656 | tf_op jit(solution)/shard_map/ppermute | solution.py:40
  20.0 4.7 %collective-permute-start.7 = (bf16[2,128,768]{2,1,0:T(8,128)(2,1)S(1)}, bf16[2,128,768]{2,1,0:T(8,128)(2,1)S(1)}, u32[]{:S(2)}, u32[]{:S(2)}) collective-permute-start(bf16[2,128,768]{2,1,0:T(8,128)(2,1)S(1)} %collective-permute-done.3.refs_8_), channel_id=1, source_target_pairs={{0,16},{1,17},{2,18},{3,19},{4,20},{5,21},{6,22},{7,23},{8,24},{9,... | collective-permute-start | bytes 1179656 | tf_op jit(solution)/shard_map/ppermute | solution.py:40
  25.8 15.4 %collective-permute-start.17 = (bf16[2,3,128,768]{3,2,1,0:T(8,128)(2,1)S(1)}, bf16[2,3,128,768]{3,2,1,0:T(8,128)(2,1)S(1)}, u32[]{:S(2)}, u32[]{:S(2)}) collective-permute-start(bf16[2,3,128,768]{3,2,1,0:T(8,128)(2,1)S(1)} %pad_maximum_fusion.1), channel_id=1, source_target_pairs={{0,32},{1,33},{2,34},{3,35},{4,36},{5,37},{6,38},{7,39},{8,40},{9,... | collective-permute-start | bytes 3538952 | tf_op jit(solution)/shard_map/ppermute | solution.py:40
  28.5 16.7 %collective-permute-start.13 = (bf16[2,3,128,768]{3,2,1,0:T(8,128)(2,1)S(1)}, bf16[2,3,128,768]{3,2,1,0:T(8,128)(2,1)S(1)}, u32[]{:S(2)}, u32[]{:S(2)}) collective-permute-start(bf16[2,3,128,768]{3,2,1,0:T(8,128)(2,1)S(1)} %pad_maximum_fusion), channel_id=1, source_target_pairs={{0,1},{1,2},{2,3},{3,0},{4,5},{5,6},{6,7},{7,4},{8,9},{9,10},{10,1... | collective-permute-start | bytes 3538952 | tf_op jit(solution)/shard_map/ppermute | solution.py:40
  32.0 17.4 %collective-permute-start.11 = (bf16[2,128,768]{2,1,0:T(8,128)(2,1)S(1)}, bf16[2,128,768]{2,1,0:T(8,128)(2,1)S(1)}, u32[]{:S(2)}, u32[]{:S(2)}) collective-permute-start(bf16[2,128,768]{2,1,0:T(8,128)(2,1)S(1)} %pad_maximum_fusion.2.refs_0_), channel_id=1, source_target_pairs={{0,1},{1,2},{2,3},{3,0},{4,5},{5,6},{6,7},{7,4},{8,9},{9,10},{10,1... | collective-permute-start | bytes 1179656 | tf_op jit(solution)/shard_map/ppermute | solution.py:40
  32.1 17.4 %collective-permute-start.4 = (bf16[2,128,768]{2,1,0:T(8,128)(2,1)S(1)}, bf16[2,128,768]{2,1,0:T(8,128)(2,1)}, u32[]{:S(2)}, u32[]{:S(2)}) collective-permute-start(bf16[2,128,768]{2,1,0:T(8,128)(2,1)S(1)} %pad_maximum_fusion.3.refs_1_), channel_id=1, source_target_pairs={{0,32},{1,33},{2,34},{3,35},{4,36},{5,37},{6,38},{7,39},{8,40},{9,... | collective-permute-start | bytes 1179656 | tf_op jit(solution)/shard_map/ppermute | solution.py:40
  41.2 10.6 %collective-permute-start.19 = (bf16[3,128,768]{2,1,0:T(8,128)(2,1)S(1)}, bf16[3,128,768]{2,1,0:T(8,128)(2,1)}, u32[]{:S(2)}, u32[]{:S(2)}) collective-permute-start(bf16[3,128,768]{2,1,0:T(8,128)(2,1)S(1)} %slice_bitcast_fusion), channel_id=1, source_target_pairs={{0,32},{1,33},{2,34},{3,35},{4,36},{5,37},{6,38},{7,39},{8,40},{9,... | collective-permute-start | bytes 1769480 | tf_op jit(solution)/shard_map/ppermute | solution.py:40
  45.2 10.5 %collective-permute-start.15 = (bf16[3,128,768]{2,1,0:T(8,128)(2,1)S(1)}, bf16[3,128,768]{2,1,0:T(8,128)(2,1)}, u32[]{:S(2)}, u32[]{:S(2)}) collective-permute-start(bf16[3,128,768]{2,1,0:T(8,128)(2,1)S(1)} %slice_bitcast_fusion.1), channel_id=1, source_target_pairs={{0,1},{1,2},{2,3},{3,0},{4,5},{5,6},{6,7},{7,4},{8,9},{9,10},{10,1... | collective-permute-start | bytes 1769480 | tf_op jit(solution)/shard_map/ppermute | solution.py:40
  48.8 10.6 %collective-permute-start.18 = (bf16[2,3,128,768]{3,2,1,0:T(8,128)(2,1)S(1)}, bf16[2,3,128,768]{3,2,1,0:T(8,128)(2,1)S(1)}, u32[]{:S(2)}, u32[]{:S(2)}) collective-permute-start(bf16[2,3,128,768]{3,2,1,0:T(8,128)(2,1)S(1)} %collective-permute-done.17.refs_18_), channel_id=1, source_target_pairs={{0,16},{1,17},{2,18},{3,19},{4,20},{5,21},{6,22},{7,23},{8,24},{9,... | collective-permute-start | bytes 3538952 | tf_op jit(solution)/shard_map/ppermute | solution.py:40
  49.3 10.0 %collective-permute-start.14 = (bf16[2,3,128,768]{3,2,1,0:T(8,128)(2,1)S(1)}, bf16[2,3,128,768]{3,2,1,0:T(8,128)(2,1)}, u32[]{:S(2)}, u32[]{:S(2)}) collective-permute-start(bf16[2,3,128,768]{3,2,1,0:T(8,128)(2,1)S(1)} %collective-permute-done.13.refs_14_), channel_id=1, source_target_pairs={{0,16},{1,17},{2,18},{3,19},{4,20},{5,21},{6,22},{7,23},{8,24},{9,... | collective-permute-start | bytes 3538952 | tf_op jit(solution)/shard_map/ppermute | solution.py:40
  50.1 6.4 %collective-permute-start.12 = (bf16[2,128,768]{2,1,0:T(8,128)(2,1)S(1)}, bf16[2,128,768]{2,1,0:T(8,128)(2,1)S(1)}, u32[]{:S(2)}, u32[]{:S(2)}) collective-permute-start(bf16[2,128,768]{2,1,0:T(8,128)(2,1)S(1)} %collective-permute-done.11.refs_6_), channel_id=1, source_target_pairs={{0,16},{1,17},{2,18},{3,19},{4,20},{5,21},{6,22},{7,23},{8,24},{9,... | collective-permute-start | bytes 1179656 | tf_op jit(solution)/shard_map/ppermute | solution.py:40
  51.8 7.5 %collective-permute-start.20 = (bf16[3,128,768]{2,1,0:T(8,128)(2,1)}, bf16[3,128,768]{2,1,0:T(8,128)(2,1)}, u32[]{:S(2)}, u32[]{:S(2)}) collective-permute-start(bf16[3,128,768]{2,1,0:T(8,128)(2,1)} %collective-permute-done.19.refs_20_), channel_id=1, source_target_pairs={{0,16},{1,17},{2,18},{3,19},{4,20},{5,21},{6,22},{7,23},{8,24},{9,... | collective-permute-start | bytes 1769480 | tf_op jit(solution)/shard_map/ppermute | solution.py:40
  66.5 16.7 %collective-permute-start.25 = (bf16[3,192,384]{2,1,0:T(8,128)(2,1)S(1)}, bf16[3,192,384]{2,1,0:T(8,128)(2,1)S(1)}, u32[]{:S(2)}, u32[]{:S(2)}) collective-permute-start(bf16[3,192,384]{2,1,0:T(8,128)(2,1)S(1)} %get-tuple-element.24), channel_id=1, source_target_pairs={{0,12},{1,13},{2,14},{3,15},{4,0},{5,1},{6,2},{7,3},{8,4},{9,5},{1... | collective-permute-start | bytes 1327112 | tf_op jit(solution)/shard_map/ppermute | solution.py:40
  73.9 22.3 %collective-permute-start.24 = (bf16[3,192,384]{2,1,0:T(8,128)(2,1)S(1)}, bf16[3,192,384]{2,1,0:T(8,128)(2,1)S(1)}, u32[]{:S(2)}, u32[]{:S(2)}) collective-permute-start(bf16[3,192,384]{2,1,0:T(8,128)(2,1)S(1)} %get-tuple-element.22), channel_id=1, source_target_pairs={{0,12},{1,13},{2,14},{3,15},{4,0},{5,1},{6,2},{7,3},{8,4},{9,5},{1... | collective-permute-start | bytes 1327112 | tf_op jit(solution)/shard_map/ppermute | solution.py:40
  75.2 11.5 %collective-permute-start.21 = (bf16[3,192,384]{2,1,0:T(8,128)(2,1)S(1)}, bf16[3,192,384]{2,1,0:T(8,128)(2,1)S(1)}, u32[]{:S(2)}, u32[]{:S(2)}) collective-permute-start(bf16[3,192,384]{2,1,0:T(8,128)(2,1)S(1)} %get-tuple-element.20), channel_id=1, source_target_pairs={{0,4},{1,5},{2,6},{3,7},{4,8},{5,9},{6,10},{7,11},{8,12},{9,13},{1... | collective-permute-start | bytes 1327112 | tf_op jit(solution)/shard_map/ppermute | solution.py:40
  82.8 13.4 %collective-permute-start.23 = (bf16[3,192,384]{2,1,0:T(8,128)(2,1)S(1)}, bf16[3,192,384]{2,1,0:T(8,128)(2,1)S(1)}, u32[]{:S(2)}, u32[]{:S(2)}) collective-permute-start(bf16[3,192,384]{2,1,0:T(8,128)(2,1)S(1)} %get-tuple-element.21), channel_id=1, source_target_pairs={{0,4},{1,5},{2,6},{3,7},{4,8},{5,9},{6,10},{7,11},{8,12},{9,13},{1... | collective-permute-start | bytes 1327112 | tf_op jit(solution)/shard_map/ppermute | solution.py:40
  83.4 12.9 %collective-permute-start.26 = (bf16[3,192,384]{2,1,0:T(8,128)(2,1)S(1)}, bf16[3,192,384]{2,1,0:T(8,128)(2,1)S(1)}, u32[]{:S(2)}, u32[]{:S(2)}) collective-permute-start(bf16[3,192,384]{2,1,0:T(8,128)(2,1)S(1)} %add_convert_fusion), channel_id=1, source_target_pairs={{0,12},{1,13},{2,14},{3,15},{4,0},{5,1},{6,2},{7,3},{8,4},{9,5},{1... | collective-permute-start | bytes 1327112 | tf_op jit(solution)/shard_map/ppermute | solution.py:40
  86.8 14.8 %collective-permute-start.22 = (bf16[3,192,384]{2,1,0:T(8,128)(2,1)S(1)}, bf16[3,192,384]{2,1,0:T(8,128)(2,1)S(1)}, u32[]{:S(2)}, u32[]{:S(2)}) collective-permute-start(bf16[3,192,384]{2,1,0:T(8,128)(2,1)S(1)} %add_convert_fusion.1), channel_id=1, source_target_pairs={{0,4},{1,5},{2,6},{3,7},{4,8},{5,9},{6,10},{7,11},{8,12},{9,13},{1... | collective-permute-start | bytes 1327112 | tf_op jit(solution)/shard_map/ppermute | solution.py:40
  (24 other events, 172.7 us)

commit v4 on v3

--- a/solution.py
+++ b/solution.py
@@ -45,27 +45,40 @@
 
 
 def gather(own):
-    ry2, rz2 = send(own, Y_FAR), send(own, Z_FAR)
+    rz2 = send(own, Z_FAR)
     other = send(own, SWAP)
-    wa, wb = jnp.stack([own[0], other[0]]), jnp.stack([own[1], other[1]])
-    ya, zb = send(wa, Y_ROUTE), send(wb, Z_ROUTE)
-    yb, za = send(after(wb, ya, zb), Y_ROUTE), send(after(wa, ya, zb), Z_ROUTE)
-    sya, szb, sry2, srz2 = (send(v, SWAP) for v in (ya, zb, ry2, rz2))
+    wb = jnp.stack([own[1], other[1]])
+    ry2 = send(own, Y_FAR)
+    srz2 = send(rz2, SWAP)
+    zb = send(wb, Z_ROUTE)
+    sry2 = send(ry2, SWAP)
+    wa = jnp.stack([own[0], other[0]])
+    ya = send(wa, Y_ROUTE)
+    za = send(after(wa, ya, zb), Z_ROUTE)
+    yb = send(after(wb, ya, zb), Y_ROUTE)
+    sya = send(ya, SWAP)
     on_z = jnp.stack([jnp.stack([ya[0], sya[1], ry2[0]]), jnp.stack([ya[1], sya[0], sry2[0]])])
+    rz3 = send(on_z, Z_ROUTE)
+    srz3 = send(rz3, SWAP)
+    rz5 = send(rz3[0], Z_ROUTE)
+    srz5 = send(rz5, SWAP)
+    szb = send(zb, SWAP)
     on_y = jnp.stack([jnp.stack([zb[0], szb[1], rz2[1]]), jnp.stack([zb[1], szb[0], srz2[1]])])
-    rz3, ry3 = send(on_z, Z_ROUTE), send(on_y, Y_ROUTE)
-    rz5, ry5 = send(rz3[0], Z_ROUTE), send(ry3[0], Y_ROUTE)
-    syb, sza = send(after(yb, on_z, on_y), SWAP), send(after(za, on_z, on_y), SWAP)
-    srz3, sry3, srz5, sry5 = (send(v, SWAP) for v in (rz3, ry3, rz5, ry5))
-    return wa, wb, ya, sya, yb, syb, za, sza, zb, szb, ry2, sry2, rz2, srz2, rz3, srz3, rz5, srz5, ry3, sry3, ry5, sry5
+    ry3 = send(on_y, Y_ROUTE)
+    sry3 = send(ry3, SWAP)
+    leaf = send(jnp.stack([after(yb, on_z, on_y), za]), SWAP)
+    ry5 = send(ry3[0], Y_ROUTE)
+    sry5 = send(ry5, SWAP)
+    return wa, wb, ya, sya, yb, za, leaf, zb, szb, ry2, sry2, rz2, srz2, rz3, srz3, rz5, srz5, ry3, sry3, ry5, sry5
 
 
 FLIP = (0, 2, 1, 3)
-N_PIECES = 22
+N_PIECES = 21
 
 
 def fetch(pieces, dy, l, dc, dst, sem):
-    wa, wb, ya, sya, yb, syb, za, sza, zb, szb, ry2, sry2, rz2, srz2, rz3, srz3, rz5, srz5, ry3, sry3, ry5, sry5 = pieces
+    wa, wb, ya, sya, yb, za, leaf, zb, szb, ry2, sry2, rz2, srz2, rz3, srz3, rz5, srz5, ry3, sry3, ry5, sry5 = pieces
+    syb, sza = leaf.at[0], leaf.at[1]
     def copy(src, dz):
         pltpu.make_async_copy(src, dst.at[dz], sem).start()
 

time: 104 us -> 103 us (level)
  local copies, waits for them, and re-layouts: 5.21 us -> 3.84 us
    unnamed x40, local copies, waits for them, and re-layouts: 3.82 us -> 2.45 us
    ppermute x27 -> x26, waiting for transfers between devices: 31.8 us -> 31.2 us  [send(): return lax.ppermute(value, AXES, way)]
    ppermute x27 -> x26, starting transfers between devices: 39 us -> 39.2 us  [send(): return lax.ppermute(value, AXES, way)]
  transfers between devices with their start and end apart: 27 -> 26, of which waited for: 11 -> 11; matrix products, arithmetic and copies ran while one was open for 2% -> 3% of each run, Pallas kernels for 18% -> 18%
where the time goes in v4:
time: 103 us
  starting transfers between devices  39.2 us (38%)
  waiting for transfers between devices  31.2 us (30%)
  Pallas kernels  26.3 us (26%)
  local copies, waits for them, and re-layouts  3.84 us (4%)
  other arithmetic  1.77 us (2%)
    ppermute x26, starting transfers between devices, send(): return lax.ppermute(value, AXES, way)  39.2 us
    ppermute x26, waiting for transfers between devices, send(): return lax.ppermute(value, AXES, way)  31.2 us
    pallas_call x4, Pallas kernels, call(): pl.pallas_call(kernel, in_specs=[smem, smem, anywhere] + [anywhere] * N_P...  24.4 us
    unnamed x40, local copies, waits for them, and re-layouts  2.45 us
  transfers between devices with their start and end apart: 26, of which 11 were waited for; matrix products, arithmetic and copies ran while one was open for 3% of the time, Pallas kernels for 18%

profile of v4, /device:TPU:1, one launch (start us, length us, event | category | flops | bytes accessed | tf_op | source)
XLA Modules:
  0.0 102.6 jit_solution(3523631261816594553)
XLA Ops:
  0.0 1.4 %collective-permute-start = (bf16[2,128,768]{2,1,0:T(8,128)(2,1)}, bf16[2,128,768]{2,1,0:T(8,128)(2,1)S(1)}, u32[]{:S(2)}, u32[]{:S(2)}) collective-permute-start(bf16[2,128,768]{2,1,0:T(8,128)(2,1)} %param.7), channel_id=1, source_target_pairs={{0,16},{1,17},{2,18},{3,19},{4,20},{5,21},{6,22},{7,23},{8,24},{9,... | collective-permute-start | bytes 1179656 | tf_op jit(solution)/shard_map/ppermute | solution.py:40
  1.4 3.7 %collective-permute-start.9 = (bf16[2,128,768]{2,1,0:T(8,128)(2,1)}, bf16[2,128,768]{2,1,0:T(8,128)(2,1)S(1)}, u32[]{:S(2)}, u32[]{:S(2)}) collective-permute-start(bf16[2,128,768]{2,1,0:T(8,128)(2,1)} %param.7), channel_id=1, source_target_pairs={{0,2},{1,3},{2,0},{3,1},{4,6},{5,7},{6,4},{7,5},{8,10},{9,11},{10,... | collective-permute-start | bytes 1179656 | tf_op jit(solution)/shard_map/ppermute | solution.py:40
  5.1 2.9 %collective-permute-start.6 = (bf16[2,128,768]{2,1,0:T(8,128)(2,1)}, bf16[2,128,768]{2,1,0:T(8,128)(2,1)S(1)}, u32[]{:S(2)}, u32[]{:S(2)}) collective-permute-start(bf16[2,128,768]{2,1,0:T(8,128)(2,1)} %param.7), channel_id=1, source_target_pairs={{0,64},{1,65},{2,66},{3,67},{4,68},{5,69},{6,70},{7,71},{8,72},{9,... | collective-permute-start | bytes 1179656 | tf_op jit(solution)/shard_map/ppermute | solution.py:40
  9.7 5.1 %collective-permute-done.9.refs_11_ = bf16[2,128,768]{2,1,0:T(8,128)(2,1)S(1)} collective-permute-done((bf16[2,128,768]{2,1,0:T(8,128)(2,1)}, bf16[2,128,768]{2,1,0:T(8,128)(2,1)S(1)}, u32[]{:S(2)}, u32[]{:S(2)}) %collective-permute-start.9) | collective-permute-done | bytes 393248 | tf_op jit(solution)/shard_map/ppermute | solution.py:40
  15.5 2.8 %collective-permute-start.1 = (bf16[2,128,768]{2,1,0:T(8,128)(2,1)S(1)}, bf16[2,128,768]{2,1,0:T(8,128)(2,1)S(1)}, u32[]{:S(2)}, u32[]{:S(2)}) collective-permute-start(bf16[2,128,768]{2,1,0:T(8,128)(2,1)S(1)} %pad_maximum_fusion.3.refs_0_), channel_id=1, source_target_pairs={{0,32},{1,33},{2,34},{3,35},{4,36},{5,37},{6,38},{7,39},{8,40},{9,... | collective-permute-start | bytes 1179656 | tf_op jit(solution)/shard_map/ppermute | solution.py:40
  18.4 1.6 %collective-permute-done.3.refs_7_ = bf16[2,128,768]{2,1,0:T(8,128)(2,1)S(1)} collective-permute-done((bf16[2,128,768]{2,1,0:T(8,128)(2,1)S(1)}, bf16[2,128,768]{2,1,0:T(8,128)(2,1)S(1)}, u32[]{:S(2)}, u32[]{:S(2)}) %collective-permute-start.3) | collective-permute-done | bytes 393248 | tf_op jit(solution)/shard_map/ppermute | solution.py:40
  20.0 3.0 %collective-permute-done.1.refs_2_ = bf16[2,128,768]{2,1,0:T(8,128)(2,1)S(1)} collective-permute-done((bf16[2,128,768]{2,1,0:T(8,128)(2,1)S(1)}, bf16[2,128,768]{2,1,0:T(8,128)(2,1)S(1)}, u32[]{:S(2)}, u32[]{:S(2)}) %collective-permute-start.1) | collective-permute-done | bytes 393248 | tf_op jit(solution)/shard_map/ppermute | solution.py:40
  23.1 1.5 %collective-permute-start.2 = (bf16[2,128,768]{2,1,0:T(8,128)(2,1)S(1)}, bf16[2,128,768]{2,1,0:T(8,128)(2,1)S(1)}, u32[]{:S(2)}, u32[]{:S(2)}) collective-permute-start(bf16[2,128,768]{2,1,0:T(8,128)(2,1)S(1)} %collective-permute-done.1.refs_2_), channel_id=1, source_target_pairs={{0,16},{1,17},{2,18},{3,19},{4,20},{5,21},{6,22},{7,23},{8,24},{9,... | collective-permute-start | bytes 1179656 | tf_op jit(solution)/shard_map/ppermute | solution.py:40
  25.8 1.8 %collective-permute-start.16 = (bf16[2,3,128,768]{3,2,1,0:T(8,128)(2,1)S(1)}, bf16[2,3,128,768]{3,2,1,0:T(8,128)(2,1)S(1)}, u32[]{:S(2)}, u32[]{:S(2)}) collective-permute-start(bf16[2,3,128,768]{3,2,1,0:T(8,128)(2,1)S(1)} %pad_maximum_fusion.1), channel_id=1, source_target_pairs={{0,32},{1,33},{2,34},{3,35},{4,36},{5,37},{6,38},{7,39},{8,40},{9,... | collective-permute-start | bytes 3538952 | tf_op jit(solution)/shard_map/ppermute | solution.py:40
  28.4 3.5 %collective-permute-start.12 = (bf16[2,3,128,768]{3,2,1,0:T(8,128)(2,1)S(1)}, bf16[2,3,128,768]{3,2,1,0:T(8,128)(2,1)S(1)}, u32[]{:S(2)}, u32[]{:S(2)}) collective-permute-start(bf16[2,3,128,768]{3,2,1,0:T(8,128)(2,1)S(1)} %pad_maximum_fusion), channel_id=1, source_target_pairs={{0,1},{1,2},{2,3},{3,0},{4,5},{5,6},{6,7},{7,4},{8,9},{9,10},{10,1... | collective-permute-start | bytes 3538952 | tf_op jit(solution)/shard_map/ppermute | solution.py:40
  32.4 8.8 %collective-permute-done.16.refs_17_ = bf16[2,3,128,768]{3,2,1,0:T(8,128)(2,1)S(1)} collective-permute-done((bf16[2,3,128,768]{3,2,1,0:T(8,128)(2,1)S(1)}, bf16[2,3,128,768]{3,2,1,0:T(8,128)(2,1)S(1)}, u32[]{:S(2)}, u32[]{:S(2)}) %collective-permute-start.16) | collective-permute-done | bytes 1179680 | tf_op jit(solution)/shard_map/ppermute | solution.py:40
  41.2 3.0 %collective-permute-start.18 = (bf16[3,128,768]{2,1,0:T(8,128)(2,1)S(1)}, bf16[3,128,768]{2,1,0:T(8,128)(2,1)}, u32[]{:S(2)}, u32[]{:S(2)}) collective-permute-start(bf16[3,128,768]{2,1,0:T(8,128)(2,1)S(1)} %slice_bitcast_fusion), channel_id=1, source_target_pairs={{0,32},{1,33},{2,34},{3,35},{4,36},{5,37},{6,38},{7,39},{8,40},{9,... | collective-permute-start | bytes 1769480 | tf_op jit(solution)/shard_map/ppermute | solution.py:40
  45.2 3.5 %collective-permute-start.14 = (bf16[3,128,768]{2,1,0:T(8,128)(2,1)S(1)}, bf16[3,128,768]{2,1,0:T(8,128)(2,1)}, u32[]{:S(2)}, u32[]{:S(2)}) collective-permute-start(bf16[3,128,768]{2,1,0:T(8,128)(2,1)S(1)} %slice_bitcast_fusion.1), channel_id=1, source_target_pairs={{0,1},{1,2},{2,3},{3,0},{4,5},{5,6},{6,7},{7,4},{8,9},{9,10},{10,1... | collective-permute-start | bytes 1769480 | tf_op jit(solution)/shard_map/ppermute | solution.py:40
  51.8 2.9 %collective-permute-start.19 = (bf16[3,128,768]{2,1,0:T(8,128)(2,1)}, bf16[3,128,768]{2,1,0:T(8,128)(2,1)}, u32[]{:S(2)}, u32[]{:S(2)}) collective-permute-start(bf16[3,128,768]{2,1,0:T(8,128)(2,1)} %collective-permute-done.18.refs_19_), channel_id=1, source_target_pairs={{0,16},{1,17},{2,18},{3,19},{4,20},{5,21},{6,22},{7,23},{8,24},{9,... | collective-permute-start | bytes 1769480 | tf_op jit(solution)/shard_map/ppermute | solution.py:40
  56.7 1.9 %collective-permute-done.15.refs_16_ = bf16[3,128,768]{2,1,0:T(8,128)(2,1)} collective-permute-done((bf16[3,128,768]{2,1,0:T(8,128)(2,1)}, bf16[3,128,768]{2,1,0:T(8,128)(2,1)}, u32[]{:S(2)}, u32[]{:S(2)}) %collective-permute-start.15) | collective-permute-done | bytes 589856 | tf_op jit(solution)/shard_map/ppermute | solution.py:40
  59.6 6.1 %shard_map.75 = (bf16[3,192,384]{2,1,0:T(8,128)(2,1)S(1)}, bf16[3,192,384]{2,1,0:T(8,128)(2,1)S(1)}) custom-call(s32[6]{0:T(128)S(1)} %stack.72.here, s32[2,48]{1,0:T(2,128)S(1)} %bitcast.21, bf16[48,768,384]{2,1,0:T(8,128)(2,1)} %maps.7, bf16[2,128,768]{2,1,0:T(8,128)(2,1)} %copy-done.10, bf16[2,128,768]{2,1,0:T(8,128)(2,1)} %copy-done.8, ...), custom_call_target="tpu_custom_call" | custom-call | flops 2264924160 | bytes 8257536 | tf_op jit(solution)/shard_map/pallas_call | solution.py:271
  67.0 6.1 %shard_map.76 = (bf16[3,192,384]{2,1,0:T(8,128)(2,1)S(1)}, f32[3,192,384]{2,1,0:T(8,128)S(1)}) custom-call(s32[6]{0:T(128)S(1)} %stack.72.here, s32[2,48]{1,0:T(2,128)S(1)} %bitcast.22, bf16[48,768,384]{2,1,0:T(8,128)(2,1)} %maps.7, bf16[2,128,768]{2,1,0:T(8,128)(2,1)} %copy-done.10, bf16[2,128,768]{2,1,0:T(8,128)(2,1)} %copy-done.8, ...), custom_call_target="tpu_custom_call" | custom-call | flops 2264924160 | bytes 8257536 | tf_op jit(solution)/shard_map/pallas_call | solution.py:271
  74.3 1.5 %collective-permute-start.20 = (bf16[3,192,384]{2,1,0:T(8,128)(2,1)S(1)}, bf16[3,192,384]{2,1,0:T(8,128)(2,1)S(1)}, u32[]{:S(2)}, u32[]{:S(2)}) collective-permute-start(bf16[3,192,384]{2,1,0:T(8,128)(2,1)S(1)} %get-tuple-element.18), channel_id=1, source_target_pairs={{0,4},{1,5},{2,6},{3,7},{4,8},{5,9},{6,10},{7,11},{8,12},{9,13},{1... | collective-permute-start | bytes 1327112 | tf_op jit(solution)/shard_map/ppermute | solution.py:40
  75.8 6.1 %shard_map.74 = (f32[3,192,384]{2,1,0:T(8,128)S(1)}, bf16[3,192,384]{2,1,0:T(8,128)(2,1)S(1)}) custom-call(s32[6]{0:T(128)S(1)} %stack.72.here, s32[2,48]{1,0:T(2,128)S(1)} %bitcast.23, bf16[48,768,384]{2,1,0:T(8,128)(2,1)} %maps.7, bf16[2,128,768]{2,1,0:T(8,128)(2,1)} %copy-done.10, bf16[2,128,768]{2,1,0:T(8,128)(2,1)} %copy-done.8, ...), custom_call_target="tpu_custom_call" | custom-call | flops 2264924160 | bytes 8257536 | tf_op jit(solution)/shard_map/pallas_call | solution.py:271
  83.6 1.9 %collective-permute-done.20 = bf16[3,192,384]{2,1,0:T(8,128)(2,1)S(1)} collective-permute-done((bf16[3,192,384]{2,1,0:T(8,128)(2,1)S(1)}, bf16[3,192,384]{2,1,0:T(8,128)(2,1)S(1)}, u32[]{:S(2)}, u32[]{:S(2)}) %collective-permute-start.20) | collective-permute-done | bytes 442400 | tf_op jit(solution)/shard_map/ppermute | solution.py:40
  85.6 3.5 %collective-permute-start.21 = (bf16[3,192,384]{2,1,0:T(8,128)(2,1)S(1)}, bf16[3,192,384]{2,1,0:T(8,128)(2,1)S(1)}, u32[]{:S(2)}, u32[]{:S(2)}) collective-permute-start(bf16[3,192,384]{2,1,0:T(8,128)(2,1)S(1)} %add_convert_fusion.1), channel_id=1, source_target_pairs={{0,4},{1,5},{2,6},{3,7},{4,8},{5,9},{6,10},{7,11},{8,12},{9,13},{1... | collective-permute-start | bytes 1327112 | tf_op jit(solution)/shard_map/ppermute | solution.py:40
  89.1 6.1 %shard_map.73.acc = f32[3,384,384]{2,1,0:T(8,128)S(1)} custom-call(s32[6]{0:T(128)S(1)} %stack.72.here, s32[2,48]{1,0:T(2,128)S(1)} %bitcast.24, bf16[48,768,384]{2,1,0:T(8,128)(2,1)} %maps.7, bf16[2,128,768]{2,1,0:T(8,128)(2,1)} %copy-done.10, bf16[2,128,768]{2,1,0:T(8,128)(2,1)} %copy-done.8, bf16[2,128,768]{2,1,0:T(8,128)(2,1)} %copy-done.11, ...), custom_call_target="tpu_custom_call" | custom-call | flops 2264924160 | bytes 8257536 | tf_op jit(solution)/shard_map/pallas_call | solution.py:271
  95.3 5.4 %collective-permute-done.21.up_top = bf16[3,192,384]{2,1,0:T(8,128)(2,1)S(1)} collective-permute-done((bf16[3,192,384]{2,1,0:T(8,128)(2,1)S(1)}, bf16[3,192,384]{2,1,0:T(8,128)(2,1)S(1)}, u32[]{:S(2)}, u32[]{:S(2)}) %collective-permute-start.21) | collective-permute-done | bytes 442400 | tf_op jit(solution)/shard_map/ppermute | solution.py:40
  100.7 1.9 %shard_map.77 = f32[3,384,384]{2,1,0:T(8,128)} custom-call(s32[3]{0:T(128)S(1)} %copy-done.4, f32[3,384,384]{2,1,0:T(8,128)S(1)} %shard_map.73.acc, bf16[3,192,384]{2,1,0:T(8,128)(2,1)S(1)} %collective-permute-done.21.up_top, bf16[3,192,384]{2,1,0:T(8,128)(2,1)S(1)} %collective-permute-done.22.up_bottom, ...), custom_call_target="tpu_custom_call" | custom-call | tf_op jit(solution)/shard_map/pallas_call | solution.py:305
  (98 shorter events, 16.3 us)
Async XLA Ops:
  0.0 9.1 %collective-permute-start = (bf16[2,128,768]{2,1,0:T(8,128)(2,1)}, bf16[2,128,768]{2,1,0:T(8,128)(2,1)S(1)}, u32[]{:S(2)}, u32[]{:S(2)}) collective-permute-start(bf16[2,128,768]{2,1,0:T(8,128)(2,1)} %param.7), channel_id=1, source_target_pairs={{0,16},{1,17},{2,18},{3,19},{4,20},{5,21},{6,22},{7,23},{8,24},{9,... | collective-permute-start | bytes 1179656 | tf_op jit(solution)/shard_map/ppermute | solution.py:40
  1.4 13.4 %collective-permute-start.9 = (bf16[2,128,768]{2,1,0:T(8,128)(2,1)}, bf16[2,128,768]{2,1,0:T(8,128)(2,1)S(1)}, u32[]{:S(2)}, u32[]{:S(2)}) collective-permute-start(bf16[2,128,768]{2,1,0:T(8,128)(2,1)} %param.7), channel_id=1, source_target_pairs={{0,2},{1,3},{2,0},{3,1},{4,6},{5,7},{6,4},{7,5},{8,10},{9,11},{10,... | collective-permute-start | bytes 1179656 | tf_op jit(solution)/shard_map/ppermute | solution.py:40
  5.1 13.2 %collective-permute-start.6 = (bf16[2,128,768]{2,1,0:T(8,128)(2,1)}, bf16[2,128,768]{2,1,0:T(8,128)(2,1)S(1)}, u32[]{:S(2)}, u32[]{:S(2)}) collective-permute-start(bf16[2,128,768]{2,1,0:T(8,128)(2,1)} %param.7), channel_id=1, source_target_pairs={{0,64},{1,65},{2,66},{3,67},{4,68},{5,69},{6,70},{7,71},{8,72},{9,... | collective-permute-start | bytes 1179656 | tf_op jit(solution)/shard_map/ppermute | solution.py:40
  9.2 10.8 %collective-permute-start.3 = (bf16[2,128,768]{2,1,0:T(8,128)(2,1)S(1)}, bf16[2,128,768]{2,1,0:T(8,128)(2,1)S(1)}, u32[]{:S(2)}, u32[]{:S(2)}) collective-permute-start(bf16[2,128,768]{2,1,0:T(8,128)(2,1)S(1)} %pad_maximum_fusion.4.refs_1_), channel_id=1, source_target_pairs={{0,1},{1,2},{2,3},{3,0},{4,5},{5,6},{6,7},{7,4},{8,9},{9,10},{10,1... | collective-permute-start | bytes 1179656 | tf_op jit(solution)/shard_map/ppermute | solution.py:40
  14.8 5.2 %collective-permute-start.10 = (bf16[2,128,768]{2,1,0:T(8,128)(2,1)S(1)}, bf16[2,128,768]{2,1,0:T(8,128)(2,1)S(1)}, u32[]{:S(2)}, u32[]{:S(2)}) collective-permute-start(bf16[2,128,768]{2,1,0:T(8,128)(2,1)S(1)} %collective-permute-done.9.refs_11_), channel_id=1, source_target_pairs={{0,16},{1,17},{2,18},{3,19},{4,20},{5,21},{6,22},{7,23},{8,24},{9,... | collective-permute-start | bytes 1179656 | tf_op jit(solution)/shard_map/ppermute | solution.py:40
  15.5 7.5 %collective-permute-start.1 = (bf16[2,128,768]{2,1,0:T(8,128)(2,1)S(1)}, bf16[2,128,768]{2,1,0:T(8,128)(2,1)S(1)}, u32[]{:S(2)}, u32[]{:S(2)}) collective-permute-start(bf16[2,128,768]{2,1,0:T(8,128)(2,1)S(1)} %pad_maximum_fusion.3.refs_0_), channel_id=1, source_target_pairs={{0,32},{1,33},{2,34},{3,35},{4,36},{5,37},{6,38},{7,39},{8,40},{9,... | collective-permute-start | bytes 1179656 | tf_op jit(solution)/shard_map/ppermute | solution.py:40
  18.3 6.2 %collective-permute-start.7 = (bf16[2,128,768]{2,1,0:T(8,128)(2,1)S(1)}, bf16[2,128,768]{2,1,0:T(8,128)(2,1)S(1)}, u32[]{:S(2)}, u32[]{:S(2)}) collective-permute-start(bf16[2,128,768]{2,1,0:T(8,128)(2,1)S(1)} %collective-permute-done.6.refs_9_), channel_id=1, source_target_pairs={{0,16},{1,17},{2,18},{3,19},{4,20},{5,21},{6,22},{7,23},{8,24},{9,... | collective-permute-start | bytes 1179656 | tf_op jit(solution)/shard_map/ppermute | solution.py:40
  20.0 4.7 %collective-permute-start.8 = (bf16[2,128,768]{2,1,0:T(8,128)(2,1)S(1)}, bf16[2,128,768]{2,1,0:T(8,128)(2,1)S(1)}, u32[]{:S(2)}, u32[]{:S(2)}) collective-permute-start(bf16[2,128,768]{2,1,0:T(8,128)(2,1)S(1)} %collective-permute-done.3.refs_7_), channel_id=1, source_target_pairs={{0,16},{1,17},{2,18},{3,19},{4,20},{5,21},{6,22},{7,23},{8,24},{9,... | collective-permute-start | bytes 1179656 | tf_op jit(solution)/shard_map/ppermute | solution.py:40
  25.8 15.4 %collective-permute-start.16 = (bf16[2,3,128,768]{3,2,1,0:T(8,128)(2,1)S(1)}, bf16[2,3,128,768]{3,2,1,0:T(8,128)(2,1)S(1)}, u32[]{:S(2)}, u32[]{:S(2)}) collective-permute-start(bf16[2,3,128,768]{3,2,1,0:T(8,128)(2,1)S(1)} %pad_maximum_fusion.1), channel_id=1, source_target_pairs={{0,32},{1,33},{2,34},{3,35},{4,36},{5,37},{6,38},{7,39},{8,40},{9,... | collective-permute-start | bytes 3538952 | tf_op jit(solution)/shard_map/ppermute | solution.py:40
  28.4 16.7 %collective-permute-start.12 = (bf16[2,3,128,768]{3,2,1,0:T(8,128)(2,1)S(1)}, bf16[2,3,128,768]{3,2,1,0:T(8,128)(2,1)S(1)}, u32[]{:S(2)}, u32[]{:S(2)}) collective-permute-start(bf16[2,3,128,768]{3,2,1,0:T(8,128)(2,1)S(1)} %pad_maximum_fusion), channel_id=1, source_target_pairs={{0,1},{1,2},{2,3},{3,0},{4,5},{5,6},{6,7},{7,4},{8,9},{9,10},{10,1... | collective-permute-start | bytes 3538952 | tf_op jit(solution)/shard_map/ppermute | solution.py:40
  32.0 16.7 %collective-permute-start.4 = (bf16[2,128,768]{2,1,0:T(8,128)(2,1)S(1)}, bf16[2,128,768]{2,1,0:T(8,128)(2,1)S(1)}, u32[]{:S(2)}, u32[]{:S(2)}) collective-permute-start(bf16[2,128,768]{2,1,0:T(8,128)(2,1)S(1)} %pad_maximum_fusion.4.refs_1_), channel_id=1, source_target_pairs={{0,32},{1,33},{2,34},{3,35},{4,36},{5,37},{6,38},{7,39},{8,40},{9,... | collective-permute-start | bytes 1179656 | tf_op jit(solution)/shard_map/ppermute | solution.py:40
  32.3 17.0 %collective-permute-start.5 = (bf16[2,128,768]{2,1,0:T(8,128)(2,1)S(1)}, bf16[2,128,768]{2,1,0:T(8,128)(2,1)S(1)}, u32[]{:S(2)}, u32[]{:S(2)}) collective-permute-start(bf16[2,128,768]{2,1,0:T(8,128)(2,1)S(1)} %pad_maximum_fusion.3.refs_0_), channel_id=1, source_target_pairs={{0,1},{1,2},{2,3},{3,0},{4,5},{5,6},{6,7},{7,4},{8,9},{9,10},{10,1... | collective-permute-start | bytes 1179656 | tf_op jit(solution)/shard_map/ppermute | solution.py:40
  41.2 10.6 %collective-permute-start.18 = (bf16[3,128,768]{2,1,0:T(8,128)(2,1)S(1)}, bf16[3,128,768]{2,1,0:T(8,128)(2,1)}, u32[]{:S(2)}, u32[]{:S(2)}) collective-permute-start(bf16[3,128,768]{2,1,0:T(8,128)(2,1)S(1)} %slice_bitcast_fusion), channel_id=1, source_target_pairs={{0,32},{1,33},{2,34},{3,35},{4,36},{5,37},{6,38},{7,39},{8,40},{9,... | collective-permute-start | bytes 1769480 | tf_op jit(solution)/shard_map/ppermute | solution.py:40
  45.2 10.5 %collective-permute-start.14 = (bf16[3,128,768]{2,1,0:T(8,128)(2,1)S(1)}, bf16[3,128,768]{2,1,0:T(8,128)(2,1)}, u32[]{:S(2)}, u32[]{:S(2)}) collective-permute-start(bf16[3,128,768]{2,1,0:T(8,128)(2,1)S(1)} %slice_bitcast_fusion.1), channel_id=1, source_target_pairs={{0,1},{1,2},{2,3},{3,0},{4,5},{5,6},{6,7},{7,4},{8,9},{9,10},{10,1... | collective-permute-start | bytes 1769480 | tf_op jit(solution)/shard_map/ppermute | solution.py:40
  48.7 9.9 %collective-permute-start.17 = (bf16[2,3,128,768]{3,2,1,0:T(8,128)(2,1)S(1)}, bf16[2,3,128,768]{3,2,1,0:T(8,128)(2,1)S(1)}, u32[]{:S(2)}, u32[]{:S(2)}) collective-permute-start(bf16[2,3,128,768]{3,2,1,0:T(8,128)(2,1)S(1)} %collective-permute-done.16.refs_17_), channel_id=1, source_target_pairs={{0,16},{1,17},{2,18},{3,19},{4,20},{5,21},{6,22},{7,23},{8,24},{9,... | collective-permute-start | bytes 3538952 | tf_op jit(solution)/shard_map/ppermute | solution.py:40
  48.7 9.8 %collective-permute-start.13 = (bf16[2,3,128,768]{3,2,1,0:T(8,128)(2,1)S(1)}, bf16[2,3,128,768]{3,2,1,0:T(8,128)(2,1)}, u32[]{:S(2)}, u32[]{:S(2)}) collective-permute-start(bf16[2,3,128,768]{3,2,1,0:T(8,128)(2,1)S(1)} %collective-permute-done.12.refs_13_), channel_id=1, source_target_pairs={{0,16},{1,17},{2,18},{3,19},{4,20},{5,21},{6,22},{7,23},{8,24},{9,... | collective-permute-start | bytes 3538952 | tf_op jit(solution)/shard_map/ppermute | solution.py:40
  50.4 6.3 %collective-permute-start.11 = (bf16[2,2,128,768]{3,2,1,0:T(8,128)(2,1)}, bf16[2,2,128,768]{3,2,1,0:T(8,128)(2,1)}, u32[]{:S(2)}, u32[]{:S(2)}) collective-permute-start(bf16[2,2,128,768]{3,2,1,0:T(8,128)(2,1)} %pad_maximum_fusion.2), channel_id=1, source_target_pairs={{0,16},{1,17},{2,18},{3,19},{4,20},{5,21},{6,22},{7,23},{8,24},{9,... | collective-permute-start | bytes 2359304 | tf_op jit(solution)/shard_map/ppermute | solution.py:40
  51.8 4.8 %collective-permute-start.19 = (bf16[3,128,768]{2,1,0:T(8,128)(2,1)}, bf16[3,128,768]{2,1,0:T(8,128)(2,1)}, u32[]{:S(2)}, u32[]{:S(2)}) collective-permute-start(bf16[3,128,768]{2,1,0:T(8,128)(2,1)} %collective-permute-done.18.refs_19_), channel_id=1, source_target_pairs={{0,16},{1,17},{2,18},{3,19},{4,20},{5,21},{6,22},{7,23},{8,24},{9,... | collective-permute-start | bytes 1769480 | tf_op jit(solution)/shard_map/ppermute | solution.py:40
  65.7 16.5 %collective-permute-start.24 = (bf16[3,192,384]{2,1,0:T(8,128)(2,1)S(1)}, bf16[3,192,384]{2,1,0:T(8,128)(2,1)S(1)}, u32[]{:S(2)}, u32[]{:S(2)}) collective-permute-start(bf16[3,192,384]{2,1,0:T(8,128)(2,1)S(1)} %get-tuple-element.22), channel_id=1, source_target_pairs={{0,12},{1,13},{2,14},{3,15},{4,0},{5,1},{6,2},{7,3},{8,4},{9,5},{1... | collective-permute-start | bytes 1327112 | tf_op jit(solution)/shard_map/ppermute | solution.py:40
  73.0 22.2 %collective-permute-start.23 = (bf16[3,192,384]{2,1,0:T(8,128)(2,1)S(1)}, bf16[3,192,384]{2,1,0:T(8,128)(2,1)S(1)}, u32[]{:S(2)}, u32[]{:S(2)}) collective-permute-start(bf16[3,192,384]{2,1,0:T(8,128)(2,1)S(1)} %get-tuple-element.20), channel_id=1, source_target_pairs={{0,12},{1,13},{2,14},{3,15},{4,0},{5,1},{6,2},{7,3},{8,4},{9,5},{1... | collective-permute-start | bytes 1327112 | tf_op jit(solution)/shard_map/ppermute | solution.py:40
  74.3 11.2 %collective-permute-start.20 = (bf16[3,192,384]{2,1,0:T(8,128)(2,1)S(1)}, bf16[3,192,384]{2,1,0:T(8,128)(2,1)S(1)}, u32[]{:S(2)}, u32[]{:S(2)}) collective-permute-start(bf16[3,192,384]{2,1,0:T(8,128)(2,1)S(1)} %get-tuple-element.18), channel_id=1, source_target_pairs={{0,4},{1,5},{2,6},{3,7},{4,8},{5,9},{6,10},{7,11},{8,12},{9,13},{1... | collective-permute-start | bytes 1327112 | tf_op jit(solution)/shard_map/ppermute | solution.py:40
  81.9 13.4 %collective-permute-start.22 = (bf16[3,192,384]{2,1,0:T(8,128)(2,1)S(1)}, bf16[3,192,384]{2,1,0:T(8,128)(2,1)S(1)}, u32[]{:S(2)}, u32[]{:S(2)}) collective-permute-start(bf16[3,192,384]{2,1,0:T(8,128)(2,1)S(1)} %get-tuple-element.19), channel_id=1, source_target_pairs={{0,4},{1,5},{2,6},{3,7},{4,8},{5,9},{6,10},{7,11},{8,12},{9,13},{1... | collective-permute-start | bytes 1327112 | tf_op jit(solution)/shard_map/ppermute | solution.py:40
  82.3 13.0 %collective-permute-start.25 = (bf16[3,192,384]{2,1,0:T(8,128)(2,1)S(1)}, bf16[3,192,384]{2,1,0:T(8,128)(2,1)S(1)}, u32[]{:S(2)}, u32[]{:S(2)}) collective-permute-start(bf16[3,192,384]{2,1,0:T(8,128)(2,1)S(1)} %add_convert_fusion), channel_id=1, source_target_pairs={{0,12},{1,13},{2,14},{3,15},{4,0},{5,1},{6,2},{7,3},{8,4},{9,5},{1... | collective-permute-start | bytes 1327112 | tf_op jit(solution)/shard_map/ppermute | solution.py:40
  85.6 15.1 %collective-permute-start.21 = (bf16[3,192,384]{2,1,0:T(8,128)(2,1)S(1)}, bf16[3,192,384]{2,1,0:T(8,128)(2,1)S(1)}, u32[]{:S(2)}, u32[]{:S(2)}) collective-permute-start(bf16[3,192,384]{2,1,0:T(8,128)(2,1)S(1)} %add_convert_fusion.1), channel_id=1, source_target_pairs={{0,4},{1,5},{2,6},{3,7},{4,8},{5,9},{6,10},{7,11},{8,12},{9,13},{1... | collective-permute-start | bytes 1327112 | tf_op jit(solution)/shard_map/ppermute | solution.py:40
  (23 other events, 146.6 us)

commit v5 on v4

--- a/solution.py
+++ b/solution.py
@@ -281,8 +281,8 @@
             ],
             compiler_params=params,
             cost_estimate=pl.CostEstimate(
-                flops=owned * (4 * Z * q * vectors * width + 2 * Z * q * width * width),
-                bytes_accessed=owned * (4 * Z * q * vectors + 2 * vectors * width + 4 * width * width),
+                flops=10 * owned * (4 * Z * q * vectors * width + 2 * Z * q * width * width),
+                bytes_accessed=10 * owned * (4 * Z * q * vectors + 2 * vectors * width + 4 * width * width),
                 transcendentals=0,
             ),
         )(here, orbs, pno_maps, *pieces, *more)

time: 103 us -> 102 us (level)
  waiting for transfers between devices: 31.2 us -> 30 us
    unnamed x40 -> x36, local copies, waits for them, and re-layouts: 2.45 us -> 1.26 us
    ppermute x26, waiting for transfers between devices: 31.2 us -> 30 us  [send(): return lax.ppermute(value, AXES, way)]
    squeeze x1, local copies, waits for them, and re-layouts: 0.04 us -> 1.1 us  [gather(): ry5 = send(ry3[0], Y_ROUTE)]
  transfers between devices with their start and end apart: 26 -> 26, of which waited for: 11 -> 11; matrix products, arithmetic and copies ran while one was open for 3% -> 3% of each run, Pallas kernels for 18% -> 19%
where the time goes in v5:
time: 102 us
  starting transfers between devices  39.8 us (39%)
  waiting for transfers between devices  30 us (29%)
  Pallas kernels  26.9 us (26%)
  local copies, waits for them, and re-layouts  3.72 us (4%)
    ppermute x26, starting transfers between devices, send(): return lax.ppermute(value, AXES, way)  39.8 us
    ppermute x26, waiting for transfers between devices, send(): return lax.ppermute(value, AXES, way)  30 us
    pallas_call x4, Pallas kernels, call(): pl.pallas_call(kernel, in_specs=[smem, smem, anywhere] + [anywhere] * N_P...  25 us
  transfers between devices with their start and end apart: 26, of which 11 were waited for; matrix products, arithmetic and copies ran while one was open for 3% of the time, Pallas kernels for 19%

profile of v5, /device:TPU:1, one launch (start us, length us, event | category | flops | bytes accessed | tf_op | source)
XLA Modules:
  0.0 101.7 jit_solution(17326032096220612312)
XLA Ops:
  1.4 3.7 %collective-permute-start.9 = (bf16[2,128,768]{2,1,0:T(8,128)(2,1)}, bf16[2,128,768]{2,1,0:T(8,128)(2,1)S(1)}, u32[]{:S(2)}, u32[]{:S(2)}) collective-permute-start(bf16[2,128,768]{2,1,0:T(8,128)(2,1)} %param.7), channel_id=1, source_target_pairs={{0,2},{1,3},{2,0},{3,1},{4,6},{5,7},{6,4},{7,5},{8,10},{9,11},{10,... | collective-permute-start | bytes 1179656 | tf_op jit(solution)/shard_map/ppermute | solution.py:40
  5.1 2.9 %collective-permute-start.6 = (bf16[2,128,768]{2,1,0:T(8,128)(2,1)}, bf16[2,128,768]{2,1,0:T(8,128)(2,1)S(1)}, u32[]{:S(2)}, u32[]{:S(2)}) collective-permute-start(bf16[2,128,768]{2,1,0:T(8,128)(2,1)} %param.7), channel_id=1, source_target_pairs={{0,64},{1,65},{2,66},{3,67},{4,68},{5,69},{6,70},{7,71},{8,72},{9,... | collective-permute-start | bytes 1179656 | tf_op jit(solution)/shard_map/ppermute | solution.py:40
  9.7 5.1 %collective-permute-done.9.refs_11_ = bf16[2,128,768]{2,1,0:T(8,128)(2,1)S(1)} collective-permute-done((bf16[2,128,768]{2,1,0:T(8,128)(2,1)}, bf16[2,128,768]{2,1,0:T(8,128)(2,1)S(1)}, u32[]{:S(2)}, u32[]{:S(2)}) %collective-permute-start.9) | collective-permute-done | bytes 393248 | tf_op jit(solution)/shard_map/ppermute | solution.py:40
  15.5 2.8 %collective-permute-start.1 = (bf16[2,128,768]{2,1,0:T(8,128)(2,1)S(1)}, bf16[2,128,768]{2,1,0:T(8,128)(2,1)S(1)}, u32[]{:S(2)}, u32[]{:S(2)}) collective-permute-start(bf16[2,128,768]{2,1,0:T(8,128)(2,1)S(1)} %pad_maximum_fusion.3.refs_0_), channel_id=1, source_target_pairs={{0,32},{1,33},{2,34},{3,35},{4,36},{5,37},{6,38},{7,39},{8,40},{9,... | collective-permute-start | bytes 1179656 | tf_op jit(solution)/shard_map/ppermute | solution.py:40
  18.4 1.6 %collective-permute-done.3.refs_7_ = bf16[2,128,768]{2,1,0:T(8,128)(2,1)S(1)} collective-permute-done((bf16[2,128,768]{2,1,0:T(8,128)(2,1)S(1)}, bf16[2,128,768]{2,1,0:T(8,128)(2,1)S(1)}, u32[]{:S(2)}, u32[]{:S(2)}) %collective-permute-start.3) | collective-permute-done | bytes 393248 | tf_op jit(solution)/shard_map/ppermute | solution.py:40
  20.0 3.0 %collective-permute-done.1.refs_2_ = bf16[2,128,768]{2,1,0:T(8,128)(2,1)S(1)} collective-permute-done((bf16[2,128,768]{2,1,0:T(8,128)(2,1)S(1)}, bf16[2,128,768]{2,1,0:T(8,128)(2,1)S(1)}, u32[]{:S(2)}, u32[]{:S(2)}) %collective-permute-start.1) | collective-permute-done | bytes 393248 | tf_op jit(solution)/shard_map/ppermute | solution.py:40
  23.1 1.5 %collective-permute-start.2 = (bf16[2,128,768]{2,1,0:T(8,128)(2,1)S(1)}, bf16[2,128,768]{2,1,0:T(8,128)(2,1)S(1)}, u32[]{:S(2)}, u32[]{:S(2)}) collective-permute-start(bf16[2,128,768]{2,1,0:T(8,128)(2,1)S(1)} %collective-permute-done.1.refs_2_), channel_id=1, source_target_pairs={{0,16},{1,17},{2,18},{3,19},{4,20},{5,21},{6,22},{7,23},{8,24},{9,... | collective-permute-start | bytes 1179656 | tf_op jit(solution)/shard_map/ppermute | solution.py:40
  25.7 1.8 %collective-permute-start.16 = (bf16[2,3,128,768]{3,2,1,0:T(8,128)(2,1)S(1)}, bf16[2,3,128,768]{3,2,1,0:T(8,128)(2,1)}, u32[]{:S(2)}, u32[]{:S(2)}) collective-permute-start(bf16[2,3,128,768]{3,2,1,0:T(8,128)(2,1)S(1)} %pad_maximum_fusion.1), channel_id=1, source_target_pairs={{0,32},{1,33},{2,34},{3,35},{4,36},{5,37},{6,38},{7,39},{8,40},{9,... | collective-permute-start | bytes 3538952 | tf_op jit(solution)/shard_map/ppermute | solution.py:40
  28.3 3.5 %collective-permute-start.12 = (bf16[2,3,128,768]{3,2,1,0:T(8,128)(2,1)S(1)}, bf16[2,3,128,768]{3,2,1,0:T(8,128)(2,1)S(1)}, u32[]{:S(2)}, u32[]{:S(2)}) collective-permute-start(bf16[2,3,128,768]{3,2,1,0:T(8,128)(2,1)S(1)} %pad_maximum_fusion), channel_id=1, source_target_pairs={{0,1},{1,2},{2,3},{3,0},{4,5},{5,6},{6,7},{7,4},{8,9},{9,10},{10,1... | collective-permute-start | bytes 3538952 | tf_op jit(solution)/shard_map/ppermute | solution.py:40
  32.4 8.8 %collective-permute-done.16.refs_17_ = bf16[2,3,128,768]{3,2,1,0:T(8,128)(2,1)} collective-permute-done((bf16[2,3,128,768]{3,2,1,0:T(8,128)(2,1)S(1)}, bf16[2,3,128,768]{3,2,1,0:T(8,128)(2,1)}, u32[]{:S(2)}, u32[]{:S(2)}) %collective-permute-start.16) | collective-permute-done | bytes 1179680 | tf_op jit(solution)/shard_map/ppermute | solution.py:40
  42.3 2.9 %collective-permute-start.18 = (bf16[3,128,768]{2,1,0:T(8,128)(2,1)S(1)}, bf16[3,128,768]{2,1,0:T(8,128)(2,1)}, u32[]{:S(2)}, u32[]{:S(2)}) collective-permute-start(bf16[3,128,768]{2,1,0:T(8,128)(2,1)S(1)} %slice_bitcast_fusion), channel_id=1, source_target_pairs={{0,32},{1,33},{2,34},{3,35},{4,36},{5,37},{6,38},{7,39},{8,40},{9,... | collective-permute-start | bytes 1769480 | tf_op jit(solution)/shard_map/ppermute | solution.py:40
  45.2 3.3 %collective-permute-start.14 = (bf16[3,128,768]{2,1,0:T(8,128)(2,1)S(1)}, bf16[3,128,768]{2,1,0:T(8,128)(2,1)}, u32[]{:S(2)}, u32[]{:S(2)}) collective-permute-start(bf16[3,128,768]{2,1,0:T(8,128)(2,1)S(1)} %slice_bitcast_fusion.1), channel_id=1, source_target_pairs={{0,1},{1,2},{2,3},{3,0},{4,5},{5,6},{6,7},{7,4},{8,9},{9,10},{10,1... | collective-permute-start | bytes 1769480 | tf_op jit(solution)/shard_map/ppermute | solution.py:40
  49.6 2.4 %collective-permute-done.18.refs_19_ = bf16[3,128,768]{2,1,0:T(8,128)(2,1)} collective-permute-done((bf16[3,128,768]{2,1,0:T(8,128)(2,1)S(1)}, bf16[3,128,768]{2,1,0:T(8,128)(2,1)}, u32[]{:S(2)}, u32[]{:S(2)}) %collective-permute-start.18) | collective-permute-done | bytes 589856 | tf_op jit(solution)/shard_map/ppermute | solution.py:40
  52.0 3.7 %collective-permute-start.19 = (bf16[3,128,768]{2,1,0:T(8,128)(2,1)}, bf16[3,128,768]{2,1,0:T(8,128)(2,1)}, u32[]{:S(2)}, u32[]{:S(2)}) collective-permute-start(bf16[3,128,768]{2,1,0:T(8,128)(2,1)} %collective-permute-done.18.refs_19_), channel_id=1, source_target_pairs={{0,16},{1,17},{2,18},{3,19},{4,20},{5,21},{6,22},{7,23},{8,24},{9,... | collective-permute-start | bytes 1769480 | tf_op jit(solution)/shard_map/ppermute | solution.py:40
  58.6 6.1 %shard_map.75 = (bf16[3,192,384]{2,1,0:T(8,128)(2,1)S(1)}, bf16[3,192,384]{2,1,0:T(8,128)(2,1)S(1)}) custom-call(s32[6]{0:T(128)S(1)} %stack.72.here, s32[2,48]{1,0:T(2,128)S(1)} %bitcast.21, bf16[48,768,384]{2,1,0:T(8,128)(2,1)} %maps.7, bf16[2,128,768]{2,1,0:T(8,128)(2,1)} %copy-done.8, bf16[2,128,768]{2,1,0:T(8,128)(2,1)} %copy-done.6, ...), custom_call_target="tpu_custom_call" | custom-call | flops 22649241600 | bytes 82575360 | tf_op jit(solution)/shard_map/pallas_call | solution.py:271
  66.0 6.7 %shard_map.76 = (bf16[3,192,384]{2,1,0:T(8,128)(2,1)S(1)}, f32[3,192,384]{2,1,0:T(8,128)S(1)}) custom-call(s32[6]{0:T(128)S(1)} %stack.72.here, s32[2,48]{1,0:T(2,128)S(1)} %bitcast.22, bf16[48,768,384]{2,1,0:T(8,128)(2,1)} %maps.7, bf16[2,128,768]{2,1,0:T(8,128)(2,1)} %copy-done.8, bf16[2,128,768]{2,1,0:T(8,128)(2,1)} %copy-done.6, ...), custom_call_target="tpu_custom_call" | custom-call | flops 22649241600 | bytes 82575360 | tf_op jit(solution)/shard_map/pallas_call | solution.py:271
  73.3 2.1 %collective-permute-start.20 = (bf16[3,192,384]{2,1,0:T(8,128)(2,1)S(1)}, bf16[3,192,384]{2,1,0:T(8,128)(2,1)S(1)}, u32[]{:S(2)}, u32[]{:S(2)}) collective-permute-start(bf16[3,192,384]{2,1,0:T(8,128)(2,1)S(1)} %get-tuple-element.18), channel_id=1, source_target_pairs={{0,4},{1,5},{2,6},{3,7},{4,8},{5,9},{6,10},{7,11},{8,12},{9,13},{1... | collective-permute-start | bytes 1327112 | tf_op jit(solution)/shard_map/ppermute | solution.py:40
  75.5 6.1 %shard_map.74 = (f32[3,192,384]{2,1,0:T(8,128)S(1)}, bf16[3,192,384]{2,1,0:T(8,128)(2,1)S(1)}) custom-call(s32[6]{0:T(128)S(1)} %stack.72.here, s32[2,48]{1,0:T(2,128)S(1)} %bitcast.23, bf16[48,768,384]{2,1,0:T(8,128)(2,1)} %maps.7, bf16[2,128,768]{2,1,0:T(8,128)(2,1)} %copy-done.8, bf16[2,128,768]{2,1,0:T(8,128)(2,1)} %copy-done.6, ...), custom_call_target="tpu_custom_call" | custom-call | flops 22649241600 | bytes 82575360 | tf_op jit(solution)/shard_map/pallas_call | solution.py:271
  81.9 1.4 %collective-permute-start.25 = (bf16[3,192,384]{2,1,0:T(8,128)(2,1)S(1)}, bf16[3,192,384]{2,1,0:T(8,128)(2,1)S(1)}, u32[]{:S(2)}, u32[]{:S(2)}) collective-permute-start(bf16[3,192,384]{2,1,0:T(8,128)(2,1)S(1)} %add_convert_fusion), channel_id=1, source_target_pairs={{0,12},{1,13},{2,14},{3,15},{4,0},{5,1},{6,2},{7,3},{8,4},{9,5},{1... | collective-permute-start | bytes 1327112 | tf_op jit(solution)/shard_map/ppermute | solution.py:40
  83.3 1.8 %collective-permute-done.20 = bf16[3,192,384]{2,1,0:T(8,128)(2,1)S(1)} collective-permute-done((bf16[3,192,384]{2,1,0:T(8,128)(2,1)S(1)}, bf16[3,192,384]{2,1,0:T(8,128)(2,1)S(1)}, u32[]{:S(2)}, u32[]{:S(2)}) %collective-permute-start.20) | collective-permute-done | bytes 442400 | tf_op jit(solution)/shard_map/ppermute | solution.py:40
  85.2 3.2 %collective-permute-start.21 = (bf16[3,192,384]{2,1,0:T(8,128)(2,1)S(1)}, bf16[3,192,384]{2,1,0:T(8,128)(2,1)S(1)}, u32[]{:S(2)}, u32[]{:S(2)}) collective-permute-start(bf16[3,192,384]{2,1,0:T(8,128)(2,1)S(1)} %add_convert_fusion.1), channel_id=1, source_target_pairs={{0,4},{1,5},{2,6},{3,7},{4,8},{5,9},{6,10},{7,11},{8,12},{9,13},{1... | collective-permute-start | bytes 1327112 | tf_op jit(solution)/shard_map/ppermute | solution.py:40
  88.5 6.1 %shard_map.73.acc = f32[3,384,384]{2,1,0:T(8,128)S(1)} custom-call(s32[6]{0:T(128)S(1)} %stack.72.here, s32[2,48]{1,0:T(2,128)S(1)} %bitcast.24, bf16[48,768,384]{2,1,0:T(8,128)(2,1)} %maps.7, bf16[2,128,768]{2,1,0:T(8,128)(2,1)} %copy-done.8, bf16[2,128,768]{2,1,0:T(8,128)(2,1)} %copy-done.6, bf16[2,128,768]{2,1,0:T(8,128)(2,1)} %copy-done.9, ...), custom_call_target="tpu_custom_call" | custom-call | flops 22649241600 | bytes 82575360 | tf_op jit(solution)/shard_map/pallas_call | solution.py:271
  95.3 4.6 %collective-permute-done.21.up_top = bf16[3,192,384]{2,1,0:T(8,128)(2,1)S(1)} collective-permute-done((bf16[3,192,384]{2,1,0:T(8,128)(2,1)S(1)}, bf16[3,192,384]{2,1,0:T(8,128)(2,1)S(1)}, u32[]{:S(2)}, u32[]{:S(2)}) %collective-permute-start.21) | collective-permute-done | bytes 442400 | tf_op jit(solution)/shard_map/ppermute | solution.py:40
  99.8 1.9 %shard_map.77 = f32[3,384,384]{2,1,0:T(8,128)} custom-call(s32[3]{0:T(128)S(1)} %copy-done, f32[3,384,384]{2,1,0:T(8,128)S(1)} %shard_map.73.acc, bf16[3,192,384]{2,1,0:T(8,128)(2,1)S(1)} %collective-permute-done.21.up_top, bf16[3,192,384]{2,1,0:T(8,128)(2,1)S(1)} %collective-permute-done.22.up_bottom, ...), custom_call_target="tpu_custom_call" | custom-call | tf_op jit(solution)/shard_map/pallas_call | solution.py:305
  (94 shorter events, 14.2 us)
Async XLA Ops:
  0.0 9.1 %collective-permute-start = (bf16[2,128,768]{2,1,0:T(8,128)(2,1)}, bf16[2,128,768]{2,1,0:T(8,128)(2,1)S(1)}, u32[]{:S(2)}, u32[]{:S(2)}) collective-permute-start(bf16[2,128,768]{2,1,0:T(8,128)(2,1)} %param.7), channel_id=1, source_target_pairs={{0,16},{1,17},{2,18},{3,19},{4,20},{5,21},{6,22},{7,23},{8,24},{9,... | collective-permute-start | bytes 1179656 | tf_op jit(solution)/shard_map/ppermute | solution.py:40
  1.4 13.4 %collective-permute-start.9 = (bf16[2,128,768]{2,1,0:T(8,128)(2,1)}, bf16[2,128,768]{2,1,0:T(8,128)(2,1)S(1)}, u32[]{:S(2)}, u32[]{:S(2)}) collective-permute-start(bf16[2,128,768]{2,1,0:T(8,128)(2,1)} %param.7), channel_id=1, source_target_pairs={{0,2},{1,3},{2,0},{3,1},{4,6},{5,7},{6,4},{7,5},{8,10},{9,11},{10,... | collective-permute-start | bytes 1179656 | tf_op jit(solution)/shard_map/ppermute | solution.py:40
  5.1 13.2 %collective-permute-start.6 = (bf16[2,128,768]{2,1,0:T(8,128)(2,1)}, bf16[2,128,768]{2,1,0:T(8,128)(2,1)S(1)}, u32[]{:S(2)}, u32[]{:S(2)}) collective-permute-start(bf16[2,128,768]{2,1,0:T(8,128)(2,1)} %param.7), channel_id=1, source_target_pairs={{0,64},{1,65},{2,66},{3,67},{4,68},{5,69},{6,70},{7,71},{8,72},{9,... | collective-permute-start | bytes 1179656 | tf_op jit(solution)/shard_map/ppermute | solution.py:40
  9.2 10.8 %collective-permute-start.3 = (bf16[2,128,768]{2,1,0:T(8,128)(2,1)S(1)}, bf16[2,128,768]{2,1,0:T(8,128)(2,1)S(1)}, u32[]{:S(2)}, u32[]{:S(2)}) collective-permute-start(bf16[2,128,768]{2,1,0:T(8,128)(2,1)S(1)} %pad_maximum_fusion.4.refs_1_), channel_id=1, source_target_pairs={{0,1},{1,2},{2,3},{3,0},{4,5},{5,6},{6,7},{7,4},{8,9},{9,10},{10,1... | collective-permute-start | bytes 1179656 | tf_op jit(solution)/shard_map/ppermute | solution.py:40
  14.8 5.2 %collective-permute-start.10 = (bf16[2,128,768]{2,1,0:T(8,128)(2,1)S(1)}, bf16[2,128,768]{2,1,0:T(8,128)(2,1)S(1)}, u32[]{:S(2)}, u32[]{:S(2)}) collective-permute-start(bf16[2,128,768]{2,1,0:T(8,128)(2,1)S(1)} %collective-permute-done.9.refs_11_), channel_id=1, source_target_pairs={{0,16},{1,17},{2,18},{3,19},{4,20},{5,21},{6,22},{7,23},{8,24},{9,... | collective-permute-start | bytes 1179656 | tf_op jit(solution)/shard_map/ppermute | solution.py:40
  15.5 7.5 %collective-permute-start.1 = (bf16[2,128,768]{2,1,0:T(8,128)(2,1)S(1)}, bf16[2,128,768]{2,1,0:T(8,128)(2,1)S(1)}, u32[]{:S(2)}, u32[]{:S(2)}) collective-permute-start(bf16[2,128,768]{2,1,0:T(8,128)(2,1)S(1)} %pad_maximum_fusion.3.refs_0_), channel_id=1, source_target_pairs={{0,32},{1,33},{2,34},{3,35},{4,36},{5,37},{6,38},{7,39},{8,40},{9,... | collective-permute-start | bytes 1179656 | tf_op jit(solution)/shard_map/ppermute | solution.py:40
  18.3 6.2 %collective-permute-start.7 = (bf16[2,128,768]{2,1,0:T(8,128)(2,1)S(1)}, bf16[2,128,768]{2,1,0:T(8,128)(2,1)S(1)}, u32[]{:S(2)}, u32[]{:S(2)}) collective-permute-start(bf16[2,128,768]{2,1,0:T(8,128)(2,1)S(1)} %collective-permute-done.6.refs_9_), channel_id=1, source_target_pairs={{0,16},{1,17},{2,18},{3,19},{4,20},{5,21},{6,22},{7,23},{8,24},{9,... | collective-permute-start | bytes 1179656 | tf_op jit(solution)/shard_map/ppermute | solution.py:40
  20.0 4.7 %collective-permute-start.8 = (bf16[2,128,768]{2,1,0:T(8,128)(2,1)S(1)}, bf16[2,128,768]{2,1,0:T(8,128)(2,1)S(1)}, u32[]{:S(2)}, u32[]{:S(2)}) collective-permute-start(bf16[2,128,768]{2,1,0:T(8,128)(2,1)S(1)} %collective-permute-done.3.refs_7_), channel_id=1, source_target_pairs={{0,16},{1,17},{2,18},{3,19},{4,20},{5,21},{6,22},{7,23},{8,24},{9,... | collective-permute-start | bytes 1179656 | tf_op jit(solution)/shard_map/ppermute | solution.py:40
  25.7 15.5 %collective-permute-start.16 = (bf16[2,3,128,768]{3,2,1,0:T(8,128)(2,1)S(1)}, bf16[2,3,128,768]{3,2,1,0:T(8,128)(2,1)}, u32[]{:S(2)}, u32[]{:S(2)}) collective-permute-start(bf16[2,3,128,768]{3,2,1,0:T(8,128)(2,1)S(1)} %pad_maximum_fusion.1), channel_id=1, source_target_pairs={{0,32},{1,33},{2,34},{3,35},{4,36},{5,37},{6,38},{7,39},{8,40},{9,... | collective-permute-start | bytes 3538952 | tf_op jit(solution)/shard_map/ppermute | solution.py:40
  28.3 16.8 %collective-permute-start.12 = (bf16[2,3,128,768]{3,2,1,0:T(8,128)(2,1)S(1)}, bf16[2,3,128,768]{3,2,1,0:T(8,128)(2,1)S(1)}, u32[]{:S(2)}, u32[]{:S(2)}) collective-permute-start(bf16[2,3,128,768]{3,2,1,0:T(8,128)(2,1)S(1)} %pad_maximum_fusion), channel_id=1, source_target_pairs={{0,1},{1,2},{2,3},{3,0},{4,5},{5,6},{6,7},{7,4},{8,9},{9,10},{10,1... | collective-permute-start | bytes 3538952 | tf_op jit(solution)/shard_map/ppermute | solution.py:40
  31.8 16.7 %collective-permute-start.4 = (bf16[2,128,768]{2,1,0:T(8,128)(2,1)S(1)}, bf16[2,128,768]{2,1,0:T(8,128)(2,1)S(1)}, u32[]{:S(2)}, u32[]{:S(2)}) collective-permute-start(bf16[2,128,768]{2,1,0:T(8,128)(2,1)S(1)} %pad_maximum_fusion.4.refs_1_), channel_id=1, source_target_pairs={{0,32},{1,33},{2,34},{3,35},{4,36},{5,37},{6,38},{7,39},{8,40},{9,... | collective-permute-start | bytes 1179656 | tf_op jit(solution)/shard_map/ppermute | solution.py:40
  32.3 16.9 %collective-permute-start.5 = (bf16[2,128,768]{2,1,0:T(8,128)(2,1)S(1)}, bf16[2,128,768]{2,1,0:T(8,128)(2,1)S(1)}, u32[]{:S(2)}, u32[]{:S(2)}) collective-permute-start(bf16[2,128,768]{2,1,0:T(8,128)(2,1)S(1)} %pad_maximum_fusion.3.refs_0_), channel_id=1, source_target_pairs={{0,1},{1,2},{2,3},{3,0},{4,5},{5,6},{6,7},{7,4},{8,9},{9,10},{10,1... | collective-permute-start | bytes 1179656 | tf_op jit(solution)/shard_map/ppermute | solution.py:40
  42.3 9.7 %collective-permute-start.18 = (bf16[3,128,768]{2,1,0:T(8,128)(2,1)S(1)}, bf16[3,128,768]{2,1,0:T(8,128)(2,1)}, u32[]{:S(2)}, u32[]{:S(2)}) collective-permute-start(bf16[3,128,768]{2,1,0:T(8,128)(2,1)S(1)} %slice_bitcast_fusion), channel_id=1, source_target_pairs={{0,32},{1,33},{2,34},{3,35},{4,36},{5,37},{6,38},{7,39},{8,40},{9,... | collective-permute-start | bytes 1769480 | tf_op jit(solution)/shard_map/ppermute | solution.py:40
  45.2 10.5 %collective-permute-start.14 = (bf16[3,128,768]{2,1,0:T(8,128)(2,1)S(1)}, bf16[3,128,768]{2,1,0:T(8,128)(2,1)}, u32[]{:S(2)}, u32[]{:S(2)}) collective-permute-start(bf16[3,128,768]{2,1,0:T(8,128)(2,1)S(1)} %slice_bitcast_fusion.1), channel_id=1, source_target_pairs={{0,1},{1,2},{2,3},{3,0},{4,5},{5,6},{6,7},{7,4},{8,9},{9,10},{10,1... | collective-permute-start | bytes 1769480 | tf_op jit(solution)/shard_map/ppermute | solution.py:40
  48.5 10.0 %collective-permute-start.17 = (bf16[2,3,128,768]{3,2,1,0:T(8,128)(2,1)}, bf16[2,3,128,768]{3,2,1,0:T(8,128)(2,1)}, u32[]{:S(2)}, u32[]{:S(2)}) collective-permute-start(bf16[2,3,128,768]{3,2,1,0:T(8,128)(2,1)} %collective-permute-done.16.refs_17_), channel_id=1, source_target_pairs={{0,16},{1,17},{2,18},{3,19},{4,20},{5,21},{6,22},{7,23},{8,24},{9,... | collective-permute-start | bytes 3538952 | tf_op jit(solution)/shard_map/ppermute | solution.py:40
  48.6 10.0 %collective-permute-start.13 = (bf16[2,3,128,768]{3,2,1,0:T(8,128)(2,1)S(1)}, bf16[2,3,128,768]{3,2,1,0:T(8,128)(2,1)}, u32[]{:S(2)}, u32[]{:S(2)}) collective-permute-start(bf16[2,3,128,768]{3,2,1,0:T(8,128)(2,1)S(1)} %collective-permute-done.12.refs_13_), channel_id=1, source_target_pairs={{0,16},{1,17},{2,18},{3,19},{4,20},{5,21},{6,22},{7,23},{8,24},{9,... | collective-permute-start | bytes 3538952 | tf_op jit(solution)/shard_map/ppermute | solution.py:40
  49.3 7.3 %collective-permute-start.11 = (bf16[2,2,128,768]{3,2,1,0:T(8,128)(2,1)S(1)}, bf16[2,2,128,768]{3,2,1,0:T(8,128)(2,1)}, u32[]{:S(2)}, u32[]{:S(2)}) collective-permute-start(bf16[2,2,128,768]{3,2,1,0:T(8,128)(2,1)S(1)} %pad_maximum_fusion.2), channel_id=1, source_target_pairs={{0,16},{1,17},{2,18},{3,19},{4,20},{5,21},{6,22},{7,23},{8,24},{9,... | collective-permute-start | bytes 2359304 | tf_op jit(solution)/shard_map/ppermute | solution.py:40
  52.0 5.7 %collective-permute-start.19 = (bf16[3,128,768]{2,1,0:T(8,128)(2,1)}, bf16[3,128,768]{2,1,0:T(8,128)(2,1)}, u32[]{:S(2)}, u32[]{:S(2)}) collective-permute-start(bf16[3,128,768]{2,1,0:T(8,128)(2,1)} %collective-permute-done.18.refs_19_), channel_id=1, source_target_pairs={{0,16},{1,17},{2,18},{3,19},{4,20},{5,21},{6,22},{7,23},{8,24},{9,... | collective-permute-start | bytes 1769480 | tf_op jit(solution)/shard_map/ppermute | solution.py:40
  64.7 17.1 %collective-permute-start.24 = (bf16[3,192,384]{2,1,0:T(8,128)(2,1)S(1)}, bf16[3,192,384]{2,1,0:T(8,128)(2,1)S(1)}, u32[]{:S(2)}, u32[]{:S(2)}) collective-permute-start(bf16[3,192,384]{2,1,0:T(8,128)(2,1)S(1)} %get-tuple-element.22), channel_id=1, source_target_pairs={{0,12},{1,13},{2,14},{3,15},{4,0},{5,1},{6,2},{7,3},{8,4},{9,5},{1... | collective-permute-start | bytes 1327112 | tf_op jit(solution)/shard_map/ppermute | solution.py:40
  72.7 21.9 %collective-permute-start.23 = (bf16[3,192,384]{2,1,0:T(8,128)(2,1)S(1)}, bf16[3,192,384]{2,1,0:T(8,128)(2,1)S(1)}, u32[]{:S(2)}, u32[]{:S(2)}) collective-permute-start(bf16[3,192,384]{2,1,0:T(8,128)(2,1)S(1)} %get-tuple-element.20), channel_id=1, source_target_pairs={{0,12},{1,13},{2,14},{3,15},{4,0},{5,1},{6,2},{7,3},{8,4},{9,5},{1... | collective-permute-start | bytes 1327112 | tf_op jit(solution)/shard_map/ppermute | solution.py:40
  73.3 11.8 %collective-permute-start.20 = (bf16[3,192,384]{2,1,0:T(8,128)(2,1)S(1)}, bf16[3,192,384]{2,1,0:T(8,128)(2,1)S(1)}, u32[]{:S(2)}, u32[]{:S(2)}) collective-permute-start(bf16[3,192,384]{2,1,0:T(8,128)(2,1)S(1)} %get-tuple-element.18), channel_id=1, source_target_pairs={{0,4},{1,5},{2,6},{3,7},{4,8},{5,9},{6,10},{7,11},{8,12},{9,13},{1... | collective-permute-start | bytes 1327112 | tf_op jit(solution)/shard_map/ppermute | solution.py:40
  81.6 13.0 %collective-permute-start.22 = (bf16[3,192,384]{2,1,0:T(8,128)(2,1)S(1)}, bf16[3,192,384]{2,1,0:T(8,128)(2,1)S(1)}, u32[]{:S(2)}, u32[]{:S(2)}) collective-permute-start(bf16[3,192,384]{2,1,0:T(8,128)(2,1)S(1)} %get-tuple-element.19), channel_id=1, source_target_pairs={{0,4},{1,5},{2,6},{3,7},{4,8},{5,9},{6,10},{7,11},{8,12},{9,13},{1... | collective-permute-start | bytes 1327112 | tf_op jit(solution)/shard_map/ppermute | solution.py:40
  81.9 13.4 %collective-permute-start.25 = (bf16[3,192,384]{2,1,0:T(8,128)(2,1)S(1)}, bf16[3,192,384]{2,1,0:T(8,128)(2,1)S(1)}, u32[]{:S(2)}, u32[]{:S(2)}) collective-permute-start(bf16[3,192,384]{2,1,0:T(8,128)(2,1)S(1)} %add_convert_fusion), channel_id=1, source_target_pairs={{0,12},{1,13},{2,14},{3,15},{4,0},{5,1},{6,2},{7,3},{8,4},{9,5},{1... | collective-permute-start | bytes 1327112 | tf_op jit(solution)/shard_map/ppermute | solution.py:40
  85.2 14.6 %collective-permute-start.21 = (bf16[3,192,384]{2,1,0:T(8,128)(2,1)S(1)}, bf16[3,192,384]{2,1,0:T(8,128)(2,1)S(1)}, u32[]{:S(2)}, u32[]{:S(2)}) collective-permute-start(bf16[3,192,384]{2,1,0:T(8,128)(2,1)S(1)} %add_convert_fusion.1), channel_id=1, source_target_pairs={{0,4},{1,5},{2,6},{3,7},{4,8},{5,9},{6,10},{7,11},{8,12},{9,13},{1... | collective-permute-start | bytes 1327112 | tf_op jit(solution)/shard_map/ppermute | solution.py:40
  (21 other events, 149.4 us)

commit v6 on v5

--- a/solution.py
+++ b/solution.py
@@ -243,8 +243,11 @@
             part = pl.ds(begin, rows)
             total = acc[p, part] + near[p].astype(jnp.float32) + late[p].astype(jnp.float32)
             staged[p, part] = jnp.where((a < size) & (b < size), total, 0.0)
-        copies.append(pltpu.make_async_copy(staged.at[p], out.at[p], sems.at[p]))
-        copies[-1].start()
+            for i in range(2):
+                piece = pl.ds(begin + i * (rows // 2), rows // 2)
+                sem = sems.at[p, 2 * (begin // rows) + i]
+                copies.append(pltpu.make_async_copy(staged.at[p, piece], out.at[p, piece], sem))
+                copies[-1].start()
     for copy in copies:
         copy.wait()
 
@@ -307,7 +310,7 @@
         in_specs=[smem, vmem, vmem, vmem, vmem, vmem],
         out_specs=anywhere,
         out_shape=whole,
-        scratch_shapes=[pltpu.VMEM((owned, width, width), f32), pltpu.SemaphoreType.DMA((owned,))],
+        scratch_shapes=[pltpu.VMEM((owned, width, width), f32), pltpu.SemaphoreType.DMA((owned, 4))],
         compiler_params=params,
     )(pair_class, acc, up_top, up_bottom, down_top, down_bottom)
 

time: 102 us -> 102 us (level)
  transfers between devices with their start and end apart: 26 -> 26, of which waited for: 11 -> 10; matrix products, arithmetic and copies ran while one was open for 3% -> 3% of each run, Pallas kernels for 19% -> 18%
where the time goes in v6:
time: 102 us
  starting transfers between devices  40.2 us (39%)
  waiting for transfers between devices  30.1 us (30%)
  Pallas kernels  26.3 us (26%)
  local copies, waits for them, and re-layouts  3.72 us (4%)
    ppermute x26, starting transfers between devices, send(): return lax.ppermute(value, AXES, way)  40.2 us
    ppermute x26, waiting for transfers between devices, send(): return lax.ppermute(value, AXES, way)  30.1 us
    pallas_call x4, Pallas kernels, call(): pl.pallas_call(kernel, in_specs=[smem, smem, anywhere] + [anywhere] * N_P...  24.4 us
  transfers between devices with their start and end apart: 26, of which 10 were waited for; matrix products, arithmetic and copies ran while one was open for 3% of the time, Pallas kernels for 18%

profile of v6, /device:TPU:1, one launch (start us, length us, event | category | flops | bytes accessed | tf_op | source)
XLA Modules:
  0.0 101.8 jit_solution(3929101317579220437)
XLA Ops:
  0.0 1.4 %collective-permute-start = (bf16[2,128,768]{2,1,0:T(8,128)(2,1)}, bf16[2,128,768]{2,1,0:T(8,128)(2,1)S(1)}, u32[]{:S(2)}, u32[]{:S(2)}) collective-permute-start(bf16[2,128,768]{2,1,0:T(8,128)(2,1)} %param.7), channel_id=1, source_target_pairs={{0,16},{1,17},{2,18},{3,19},{4,20},{5,21},{6,22},{7,23},{8,24},{9,... | collective-permute-start | bytes 1179656 | tf_op jit(solution)/shard_map/ppermute | solution.py:40
  1.4 3.7 %collective-permute-start.9 = (bf16[2,128,768]{2,1,0:T(8,128)(2,1)}, bf16[2,128,768]{2,1,0:T(8,128)(2,1)S(1)}, u32[]{:S(2)}, u32[]{:S(2)}) collective-permute-start(bf16[2,128,768]{2,1,0:T(8,128)(2,1)} %param.7), channel_id=1, source_target_pairs={{0,2},{1,3},{2,0},{3,1},{4,6},{5,7},{6,4},{7,5},{8,10},{9,11},{10,... | collective-permute-start | bytes 1179656 | tf_op jit(solution)/shard_map/ppermute | solution.py:40
  5.1 2.9 %collective-permute-start.6 = (bf16[2,128,768]{2,1,0:T(8,128)(2,1)}, bf16[2,128,768]{2,1,0:T(8,128)(2,1)S(1)}, u32[]{:S(2)}, u32[]{:S(2)}) collective-permute-start(bf16[2,128,768]{2,1,0:T(8,128)(2,1)} %param.7), channel_id=1, source_target_pairs={{0,64},{1,65},{2,66},{3,67},{4,68},{5,69},{6,70},{7,71},{8,72},{9,... | collective-permute-start | bytes 1179656 | tf_op jit(solution)/shard_map/ppermute | solution.py:40
  9.7 5.1 %collective-permute-done.9.refs_11_ = bf16[2,128,768]{2,1,0:T(8,128)(2,1)S(1)} collective-permute-done((bf16[2,128,768]{2,1,0:T(8,128)(2,1)}, bf16[2,128,768]{2,1,0:T(8,128)(2,1)S(1)}, u32[]{:S(2)}, u32[]{:S(2)}) %collective-permute-start.9) | collective-permute-done | bytes 393248 | tf_op jit(solution)/shard_map/ppermute | solution.py:40
  15.5 2.8 %collective-permute-start.1 = (bf16[2,128,768]{2,1,0:T(8,128)(2,1)S(1)}, bf16[2,128,768]{2,1,0:T(8,128)(2,1)S(1)}, u32[]{:S(2)}, u32[]{:S(2)}) collective-permute-start(bf16[2,128,768]{2,1,0:T(8,128)(2,1)S(1)} %pad_maximum_fusion.3.refs_0_), channel_id=1, source_target_pairs={{0,32},{1,33},{2,34},{3,35},{4,36},{5,37},{6,38},{7,39},{8,40},{9,... | collective-permute-start | bytes 1179656 | tf_op jit(solution)/shard_map/ppermute | solution.py:40
  18.4 1.6 %collective-permute-done.3.refs_7_ = bf16[2,128,768]{2,1,0:T(8,128)(2,1)S(1)} collective-permute-done((bf16[2,128,768]{2,1,0:T(8,128)(2,1)S(1)}, bf16[2,128,768]{2,1,0:T(8,128)(2,1)S(1)}, u32[]{:S(2)}, u32[]{:S(2)}) %collective-permute-start.3) | collective-permute-done | bytes 393248 | tf_op jit(solution)/shard_map/ppermute | solution.py:40
  20.0 3.0 %collective-permute-done.1.refs_2_ = bf16[2,128,768]{2,1,0:T(8,128)(2,1)S(1)} collective-permute-done((bf16[2,128,768]{2,1,0:T(8,128)(2,1)S(1)}, bf16[2,128,768]{2,1,0:T(8,128)(2,1)S(1)}, u32[]{:S(2)}, u32[]{:S(2)}) %collective-permute-start.1) | collective-permute-done | bytes 393248 | tf_op jit(solution)/shard_map/ppermute | solution.py:40
  23.1 1.5 %collective-permute-start.2 = (bf16[2,128,768]{2,1,0:T(8,128)(2,1)S(1)}, bf16[2,128,768]{2,1,0:T(8,128)(2,1)S(1)}, u32[]{:S(2)}, u32[]{:S(2)}) collective-permute-start(bf16[2,128,768]{2,1,0:T(8,128)(2,1)S(1)} %collective-permute-done.1.refs_2_), channel_id=1, source_target_pairs={{0,16},{1,17},{2,18},{3,19},{4,20},{5,21},{6,22},{7,23},{8,24},{9,... | collective-permute-start | bytes 1179656 | tf_op jit(solution)/shard_map/ppermute | solution.py:40
  25.7 1.8 %collective-permute-start.16 = (bf16[2,3,128,768]{3,2,1,0:T(8,128)(2,1)S(1)}, bf16[2,3,128,768]{3,2,1,0:T(8,128)(2,1)}, u32[]{:S(2)}, u32[]{:S(2)}) collective-permute-start(bf16[2,3,128,768]{3,2,1,0:T(8,128)(2,1)S(1)} %pad_maximum_fusion.1), channel_id=1, source_target_pairs={{0,32},{1,33},{2,34},{3,35},{4,36},{5,37},{6,38},{7,39},{8,40},{9,... | collective-permute-start | bytes 3538952 | tf_op jit(solution)/shard_map/ppermute | solution.py:40
  28.3 3.5 %collective-permute-start.12 = (bf16[2,3,128,768]{3,2,1,0:T(8,128)(2,1)S(1)}, bf16[2,3,128,768]{3,2,1,0:T(8,128)(2,1)S(1)}, u32[]{:S(2)}, u32[]{:S(2)}) collective-permute-start(bf16[2,3,128,768]{3,2,1,0:T(8,128)(2,1)S(1)} %pad_maximum_fusion), channel_id=1, source_target_pairs={{0,1},{1,2},{2,3},{3,0},{4,5},{5,6},{6,7},{7,4},{8,9},{9,10},{10,1... | collective-permute-start | bytes 3538952 | tf_op jit(solution)/shard_map/ppermute | solution.py:40
  32.4 8.8 %collective-permute-done.16.refs_17_ = bf16[2,3,128,768]{3,2,1,0:T(8,128)(2,1)} collective-permute-done((bf16[2,3,128,768]{3,2,1,0:T(8,128)(2,1)S(1)}, bf16[2,3,128,768]{3,2,1,0:T(8,128)(2,1)}, u32[]{:S(2)}, u32[]{:S(2)}) %collective-permute-start.16) | collective-permute-done | bytes 1179680 | tf_op jit(solution)/shard_map/ppermute | solution.py:40
  42.3 2.9 %collective-permute-start.18 = (bf16[3,128,768]{2,1,0:T(8,128)(2,1)S(1)}, bf16[3,128,768]{2,1,0:T(8,128)(2,1)}, u32[]{:S(2)}, u32[]{:S(2)}) collective-permute-start(bf16[3,128,768]{2,1,0:T(8,128)(2,1)S(1)} %slice_bitcast_fusion), channel_id=1, source_target_pairs={{0,32},{1,33},{2,34},{3,35},{4,36},{5,37},{6,38},{7,39},{8,40},{9,... | collective-permute-start | bytes 1769480 | tf_op jit(solution)/shard_map/ppermute | solution.py:40
  45.2 3.3 %collective-permute-start.14 = (bf16[3,128,768]{2,1,0:T(8,128)(2,1)S(1)}, bf16[3,128,768]{2,1,0:T(8,128)(2,1)}, u32[]{:S(2)}, u32[]{:S(2)}) collective-permute-start(bf16[3,128,768]{2,1,0:T(8,128)(2,1)S(1)} %slice_bitcast_fusion.1), channel_id=1, source_target_pairs={{0,1},{1,2},{2,3},{3,0},{4,5},{5,6},{6,7},{7,4},{8,9},{9,10},{10,1... | collective-permute-start | bytes 1769480 | tf_op jit(solution)/shard_map/ppermute | solution.py:40
  49.6 2.4 %collective-permute-done.18.refs_19_ = bf16[3,128,768]{2,1,0:T(8,128)(2,1)} collective-permute-done((bf16[3,128,768]{2,1,0:T(8,128)(2,1)S(1)}, bf16[3,128,768]{2,1,0:T(8,128)(2,1)}, u32[]{:S(2)}, u32[]{:S(2)}) %collective-permute-start.18) | collective-permute-done | bytes 589856 | tf_op jit(solution)/shard_map/ppermute | solution.py:40
  52.0 3.7 %collective-permute-start.19 = (bf16[3,128,768]{2,1,0:T(8,128)(2,1)}, bf16[3,128,768]{2,1,0:T(8,128)(2,1)}, u32[]{:S(2)}, u32[]{:S(2)}) collective-permute-start(bf16[3,128,768]{2,1,0:T(8,128)(2,1)} %collective-permute-done.18.refs_19_), channel_id=1, source_target_pairs={{0,16},{1,17},{2,18},{3,19},{4,20},{5,21},{6,22},{7,23},{8,24},{9,... | collective-permute-start | bytes 1769480 | tf_op jit(solution)/shard_map/ppermute | solution.py:40
  58.6 6.1 %shard_map.75 = (bf16[3,192,384]{2,1,0:T(8,128)(2,1)S(1)}, bf16[3,192,384]{2,1,0:T(8,128)(2,1)S(1)}) custom-call(s32[6]{0:T(128)S(1)} %stack.72.here, s32[2,48]{1,0:T(2,128)S(1)} %bitcast.21, bf16[48,768,384]{2,1,0:T(8,128)(2,1)} %maps.7, bf16[2,128,768]{2,1,0:T(8,128)(2,1)} %copy-done.8, bf16[2,128,768]{2,1,0:T(8,128)(2,1)} %copy-done.6, ...), custom_call_target="tpu_custom_call" | custom-call | flops 22649241600 | bytes 82575360 | tf_op jit(solution)/shard_map/pallas_call | solution.py:274
  66.0 6.1 %shard_map.76 = (bf16[3,192,384]{2,1,0:T(8,128)(2,1)S(1)}, f32[3,192,384]{2,1,0:T(8,128)S(1)}) custom-call(s32[6]{0:T(128)S(1)} %stack.72.here, s32[2,48]{1,0:T(2,128)S(1)} %bitcast.22, bf16[48,768,384]{2,1,0:T(8,128)(2,1)} %maps.7, bf16[2,128,768]{2,1,0:T(8,128)(2,1)} %copy-done.8, bf16[2,128,768]{2,1,0:T(8,128)(2,1)} %copy-done.6, ...), custom_call_target="tpu_custom_call" | custom-call | flops 22649241600 | bytes 82575360 | tf_op jit(solution)/shard_map/pallas_call | solution.py:274
  73.3 1.5 %collective-permute-start.20 = (bf16[3,192,384]{2,1,0:T(8,128)(2,1)S(1)}, bf16[3,192,384]{2,1,0:T(8,128)(2,1)S(1)}, u32[]{:S(2)}, u32[]{:S(2)}) collective-permute-start(bf16[3,192,384]{2,1,0:T(8,128)(2,1)S(1)} %get-tuple-element.18), channel_id=1, source_target_pairs={{0,4},{1,5},{2,6},{3,7},{4,8},{5,9},{6,10},{7,11},{8,12},{9,13},{1... | collective-permute-start | bytes 1327112 | tf_op jit(solution)/shard_map/ppermute | solution.py:40
  74.8 6.1 %shard_map.74 = (f32[3,192,384]{2,1,0:T(8,128)S(1)}, bf16[3,192,384]{2,1,0:T(8,128)(2,1)S(1)}) custom-call(s32[6]{0:T(128)S(1)} %stack.72.here, s32[2,48]{1,0:T(2,128)S(1)} %bitcast.23, bf16[48,768,384]{2,1,0:T(8,128)(2,1)} %maps.7, bf16[2,128,768]{2,1,0:T(8,128)(2,1)} %copy-done.8, bf16[2,128,768]{2,1,0:T(8,128)(2,1)} %copy-done.6, ...), custom_call_target="tpu_custom_call" | custom-call | flops 22649241600 | bytes 82575360 | tf_op jit(solution)/shard_map/pallas_call | solution.py:274
  82.8 1.7 %collective-permute-done.20 = bf16[3,192,384]{2,1,0:T(8,128)(2,1)S(1)} collective-permute-done((bf16[3,192,384]{2,1,0:T(8,128)(2,1)S(1)}, bf16[3,192,384]{2,1,0:T(8,128)(2,1)S(1)}, u32[]{:S(2)}, u32[]{:S(2)}) %collective-permute-start.20) | collective-permute-done | bytes 442400 | tf_op jit(solution)/shard_map/ppermute | solution.py:40
  84.7 3.5 %collective-permute-start.21 = (bf16[3,192,384]{2,1,0:T(8,128)(2,1)S(1)}, bf16[3,192,384]{2,1,0:T(8,128)(2,1)S(1)}, u32[]{:S(2)}, u32[]{:S(2)}) collective-permute-start(bf16[3,192,384]{2,1,0:T(8,128)(2,1)S(1)} %add_convert_fusion.1), channel_id=1, source_target_pairs={{0,4},{1,5},{2,6},{3,7},{4,8},{5,9},{6,10},{7,11},{8,12},{9,13},{1... | collective-permute-start | bytes 1327112 | tf_op jit(solution)/shard_map/ppermute | solution.py:40
  88.2 6.1 %shard_map.73.acc = f32[3,384,384]{2,1,0:T(8,128)S(1)} custom-call(s32[6]{0:T(128)S(1)} %stack.72.here, s32[2,48]{1,0:T(2,128)S(1)} %bitcast.24, bf16[48,768,384]{2,1,0:T(8,128)(2,1)} %maps.7, bf16[2,128,768]{2,1,0:T(8,128)(2,1)} %copy-done.8, bf16[2,128,768]{2,1,0:T(8,128)(2,1)} %copy-done.6, bf16[2,128,768]{2,1,0:T(8,128)(2,1)} %copy-done.9, ...), custom_call_target="tpu_custom_call" | custom-call | flops 22649241600 | bytes 82575360 | tf_op jit(solution)/shard_map/pallas_call | solution.py:274
  94.3 5.4 %collective-permute-done.21.up_top = bf16[3,192,384]{2,1,0:T(8,128)(2,1)S(1)} collective-permute-done((bf16[3,192,384]{2,1,0:T(8,128)(2,1)S(1)}, bf16[3,192,384]{2,1,0:T(8,128)(2,1)S(1)}, u32[]{:S(2)}, u32[]{:S(2)}) %collective-permute-start.21) | collective-permute-done | bytes 442400 | tf_op jit(solution)/shard_map/ppermute | solution.py:40
  99.7 1.9 %shard_map.77 = f32[3,384,384]{2,1,0:T(8,128)} custom-call(s32[3]{0:T(128)S(1)} %copy-done, f32[3,384,384]{2,1,0:T(8,128)S(1)} %shard_map.73.acc, bf16[3,192,384]{2,1,0:T(8,128)(2,1)S(1)} %collective-permute-done.21.up_top, bf16[3,192,384]{2,1,0:T(8,128)(2,1)S(1)} %collective-permute-done.22.up_bottom, ...), custom_call_target="tpu_custom_call" | custom-call | tf_op jit(solution)/shard_map/pallas_call | solution.py:308
  (94 shorter events, 14.4 us)
Async XLA Ops:
  0.0 9.1 %collective-permute-start = (bf16[2,128,768]{2,1,0:T(8,128)(2,1)}, bf16[2,128,768]{2,1,0:T(8,128)(2,1)S(1)}, u32[]{:S(2)}, u32[]{:S(2)}) collective-permute-start(bf16[2,128,768]{2,1,0:T(8,128)(2,1)} %param.7), channel_id=1, source_target_pairs={{0,16},{1,17},{2,18},{3,19},{4,20},{5,21},{6,22},{7,23},{8,24},{9,... | collective-permute-start | bytes 1179656 | tf_op jit(solution)/shard_map/ppermute | solution.py:40
  1.4 13.4 %collective-permute-start.9 = (bf16[2,128,768]{2,1,0:T(8,128)(2,1)}, bf16[2,128,768]{2,1,0:T(8,128)(2,1)S(1)}, u32[]{:S(2)}, u32[]{:S(2)}) collective-permute-start(bf16[2,128,768]{2,1,0:T(8,128)(2,1)} %param.7), channel_id=1, source_target_pairs={{0,2},{1,3},{2,0},{3,1},{4,6},{5,7},{6,4},{7,5},{8,10},{9,11},{10,... | collective-permute-start | bytes 1179656 | tf_op jit(solution)/shard_map/ppermute | solution.py:40
  5.1 13.2 %collective-permute-start.6 = (bf16[2,128,768]{2,1,0:T(8,128)(2,1)}, bf16[2,128,768]{2,1,0:T(8,128)(2,1)S(1)}, u32[]{:S(2)}, u32[]{:S(2)}) collective-permute-start(bf16[2,128,768]{2,1,0:T(8,128)(2,1)} %param.7), channel_id=1, source_target_pairs={{0,64},{1,65},{2,66},{3,67},{4,68},{5,69},{6,70},{7,71},{8,72},{9,... | collective-permute-start | bytes 1179656 | tf_op jit(solution)/shard_map/ppermute | solution.py:40
  9.2 10.8 %collective-permute-start.3 = (bf16[2,128,768]{2,1,0:T(8,128)(2,1)S(1)}, bf16[2,128,768]{2,1,0:T(8,128)(2,1)S(1)}, u32[]{:S(2)}, u32[]{:S(2)}) collective-permute-start(bf16[2,128,768]{2,1,0:T(8,128)(2,1)S(1)} %pad_maximum_fusion.4.refs_1_), channel_id=1, source_target_pairs={{0,1},{1,2},{2,3},{3,0},{4,5},{5,6},{6,7},{7,4},{8,9},{9,10},{10,1... | collective-permute-start | bytes 1179656 | tf_op jit(solution)/shard_map/ppermute | solution.py:40
  14.8 5.2 %collective-permute-start.10 = (bf16[2,128,768]{2,1,0:T(8,128)(2,1)S(1)}, bf16[2,128,768]{2,1,0:T(8,128)(2,1)S(1)}, u32[]{:S(2)}, u32[]{:S(2)}) collective-permute-start(bf16[2,128,768]{2,1,0:T(8,128)(2,1)S(1)} %collective-permute-done.9.refs_11_), channel_id=1, source_target_pairs={{0,16},{1,17},{2,18},{3,19},{4,20},{5,21},{6,22},{7,23},{8,24},{9,... | collective-permute-start | bytes 1179656 | tf_op jit(solution)/shard_map/ppermute | solution.py:40
  15.5 7.5 %collective-permute-start.1 = (bf16[2,128,768]{2,1,0:T(8,128)(2,1)S(1)}, bf16[2,128,768]{2,1,0:T(8,128)(2,1)S(1)}, u32[]{:S(2)}, u32[]{:S(2)}) collective-permute-start(bf16[2,128,768]{2,1,0:T(8,128)(2,1)S(1)} %pad_maximum_fusion.3.refs_0_), channel_id=1, source_target_pairs={{0,32},{1,33},{2,34},{3,35},{4,36},{5,37},{6,38},{7,39},{8,40},{9,... | collective-permute-start | bytes 1179656 | tf_op jit(solution)/shard_map/ppermute | solution.py:40
  18.3 6.2 %collective-permute-start.7 = (bf16[2,128,768]{2,1,0:T(8,128)(2,1)S(1)}, bf16[2,128,768]{2,1,0:T(8,128)(2,1)S(1)}, u32[]{:S(2)}, u32[]{:S(2)}) collective-permute-start(bf16[2,128,768]{2,1,0:T(8,128)(2,1)S(1)} %collective-permute-done.6.refs_9_), channel_id=1, source_target_pairs={{0,16},{1,17},{2,18},{3,19},{4,20},{5,21},{6,22},{7,23},{8,24},{9,... | collective-permute-start | bytes 1179656 | tf_op jit(solution)/shard_map/ppermute | solution.py:40
  20.0 4.7 %collective-permute-start.8 = (bf16[2,128,768]{2,1,0:T(8,128)(2,1)S(1)}, bf16[2,128,768]{2,1,0:T(8,128)(2,1)S(1)}, u32[]{:S(2)}, u32[]{:S(2)}) collective-permute-start(bf16[2,128,768]{2,1,0:T(8,128)(2,1)S(1)} %collective-permute-done.3.refs_7_), channel_id=1, source_target_pairs={{0,16},{1,17},{2,18},{3,19},{4,20},{5,21},{6,22},{7,23},{8,24},{9,... | collective-permute-start | bytes 1179656 | tf_op jit(solution)/shard_map/ppermute | solution.py:40
  25.7 15.5 %collective-permute-start.16 = (bf16[2,3,128,768]{3,2,1,0:T(8,128)(2,1)S(1)}, bf16[2,3,128,768]{3,2,1,0:T(8,128)(2,1)}, u32[]{:S(2)}, u32[]{:S(2)}) collective-permute-start(bf16[2,3,128,768]{3,2,1,0:T(8,128)(2,1)S(1)} %pad_maximum_fusion.1), channel_id=1, source_target_pairs={{0,32},{1,33},{2,34},{3,35},{4,36},{5,37},{6,38},{7,39},{8,40},{9,... | collective-permute-start | bytes 3538952 | tf_op jit(solution)/shard_map/ppermute | solution.py:40
  28.3 16.8 %collective-permute-start.12 = (bf16[2,3,128,768]{3,2,1,0:T(8,128)(2,1)S(1)}, bf16[2,3,128,768]{3,2,1,0:T(8,128)(2,1)S(1)}, u32[]{:S(2)}, u32[]{:S(2)}) collective-permute-start(bf16[2,3,128,768]{3,2,1,0:T(8,128)(2,1)S(1)} %pad_maximum_fusion), channel_id=1, source_target_pairs={{0,1},{1,2},{2,3},{3,0},{4,5},{5,6},{6,7},{7,4},{8,9},{9,10},{10,1... | collective-permute-start | bytes 3538952 | tf_op jit(solution)/shard_map/ppermute | solution.py:40
  31.8 16.7 %collective-permute-start.4 = (bf16[2,128,768]{2,1,0:T(8,128)(2,1)S(1)}, bf16[2,128,768]{2,1,0:T(8,128)(2,1)S(1)}, u32[]{:S(2)}, u32[]{:S(2)}) collective-permute-start(bf16[2,128,768]{2,1,0:T(8,128)(2,1)S(1)} %pad_maximum_fusion.4.refs_1_), channel_id=1, source_target_pairs={{0,32},{1,33},{2,34},{3,35},{4,36},{5,37},{6,38},{7,39},{8,40},{9,... | collective-permute-start | bytes 1179656 | tf_op jit(solution)/shard_map/ppermute | solution.py:40
  32.3 16.9 %collective-permute-start.5 = (bf16[2,128,768]{2,1,0:T(8,128)(2,1)S(1)}, bf16[2,128,768]{2,1,0:T(8,128)(2,1)S(1)}, u32[]{:S(2)}, u32[]{:S(2)}) collective-permute-start(bf16[2,128,768]{2,1,0:T(8,128)(2,1)S(1)} %pad_maximum_fusion.3.refs_0_), channel_id=1, source_target_pairs={{0,1},{1,2},{2,3},{3,0},{4,5},{5,6},{6,7},{7,4},{8,9},{9,10},{10,1... | collective-permute-start | bytes 1179656 | tf_op jit(solution)/shard_map/ppermute | solution.py:40
  42.3 9.7 %collective-permute-start.18 = (bf16[3,128,768]{2,1,0:T(8,128)(2,1)S(1)}, bf16[3,128,768]{2,1,0:T(8,128)(2,1)}, u32[]{:S(2)}, u32[]{:S(2)}) collective-permute-start(bf16[3,128,768]{2,1,0:T(8,128)(2,1)S(1)} %slice_bitcast_fusion), channel_id=1, source_target_pairs={{0,32},{1,33},{2,34},{3,35},{4,36},{5,37},{6,38},{7,39},{8,40},{9,... | collective-permute-start | bytes 1769480 | tf_op jit(solution)/shard_map/ppermute | solution.py:40
  45.2 10.5 %collective-permute-start.14 = (bf16[3,128,768]{2,1,0:T(8,128)(2,1)S(1)}, bf16[3,128,768]{2,1,0:T(8,128)(2,1)}, u32[]{:S(2)}, u32[]{:S(2)}) collective-permute-start(bf16[3,128,768]{2,1,0:T(8,128)(2,1)S(1)} %slice_bitcast_fusion.1), channel_id=1, source_target_pairs={{0,1},{1,2},{2,3},{3,0},{4,5},{5,6},{6,7},{7,4},{8,9},{9,10},{10,1... | collective-permute-start | bytes 1769480 | tf_op jit(solution)/shard_map/ppermute | solution.py:40
  48.5 10.0 %collective-permute-start.17 = (bf16[2,3,128,768]{3,2,1,0:T(8,128)(2,1)}, bf16[2,3,128,768]{3,2,1,0:T(8,128)(2,1)}, u32[]{:S(2)}, u32[]{:S(2)}) collective-permute-start(bf16[2,3,128,768]{3,2,1,0:T(8,128)(2,1)} %collective-permute-done.16.refs_17_), channel_id=1, source_target_pairs={{0,16},{1,17},{2,18},{3,19},{4,20},{5,21},{6,22},{7,23},{8,24},{9,... | collective-permute-start | bytes 3538952 | tf_op jit(solution)/shard_map/ppermute | solution.py:40
  48.6 10.0 %collective-permute-start.13 = (bf16[2,3,128,768]{3,2,1,0:T(8,128)(2,1)S(1)}, bf16[2,3,128,768]{3,2,1,0:T(8,128)(2,1)}, u32[]{:S(2)}, u32[]{:S(2)}) collective-permute-start(bf16[2,3,128,768]{3,2,1,0:T(8,128)(2,1)S(1)} %collective-permute-done.12.refs_13_), channel_id=1, source_target_pairs={{0,16},{1,17},{2,18},{3,19},{4,20},{5,21},{6,22},{7,23},{8,24},{9,... | collective-permute-start | bytes 3538952 | tf_op jit(solution)/shard_map/ppermute | solution.py:40
  49.3 7.3 %collective-permute-start.11 = (bf16[2,2,128,768]{3,2,1,0:T(8,128)(2,1)S(1)}, bf16[2,2,128,768]{3,2,1,0:T(8,128)(2,1)}, u32[]{:S(2)}, u32[]{:S(2)}) collective-permute-start(bf16[2,2,128,768]{3,2,1,0:T(8,128)(2,1)S(1)} %pad_maximum_fusion.2), channel_id=1, source_target_pairs={{0,16},{1,17},{2,18},{3,19},{4,20},{5,21},{6,22},{7,23},{8,24},{9,... | collective-permute-start | bytes 2359304 | tf_op jit(solution)/shard_map/ppermute | solution.py:40
  52.0 5.7 %collective-permute-start.19 = (bf16[3,128,768]{2,1,0:T(8,128)(2,1)}, bf16[3,128,768]{2,1,0:T(8,128)(2,1)}, u32[]{:S(2)}, u32[]{:S(2)}) collective-permute-start(bf16[3,128,768]{2,1,0:T(8,128)(2,1)} %collective-permute-done.18.refs_19_), channel_id=1, source_target_pairs={{0,16},{1,17},{2,18},{3,19},{4,20},{5,21},{6,22},{7,23},{8,24},{9,... | collective-permute-start | bytes 1769480 | tf_op jit(solution)/shard_map/ppermute | solution.py:40
  64.7 16.7 %collective-permute-start.24 = (bf16[3,192,384]{2,1,0:T(8,128)(2,1)S(1)}, bf16[3,192,384]{2,1,0:T(8,128)(2,1)S(1)}, u32[]{:S(2)}, u32[]{:S(2)}) collective-permute-start(bf16[3,192,384]{2,1,0:T(8,128)(2,1)S(1)} %get-tuple-element.22), channel_id=1, source_target_pairs={{0,12},{1,13},{2,14},{3,15},{4,0},{5,1},{6,2},{7,3},{8,4},{9,5},{1... | collective-permute-start | bytes 1327112 | tf_op jit(solution)/shard_map/ppermute | solution.py:40
  72.1 22.3 %collective-permute-start.23 = (bf16[3,192,384]{2,1,0:T(8,128)(2,1)S(1)}, bf16[3,192,384]{2,1,0:T(8,128)(2,1)S(1)}, u32[]{:S(2)}, u32[]{:S(2)}) collective-permute-start(bf16[3,192,384]{2,1,0:T(8,128)(2,1)S(1)} %get-tuple-element.20), channel_id=1, source_target_pairs={{0,12},{1,13},{2,14},{3,15},{4,0},{5,1},{6,2},{7,3},{8,4},{9,5},{1... | collective-permute-start | bytes 1327112 | tf_op jit(solution)/shard_map/ppermute | solution.py:40
  73.3 11.2 %collective-permute-start.20 = (bf16[3,192,384]{2,1,0:T(8,128)(2,1)S(1)}, bf16[3,192,384]{2,1,0:T(8,128)(2,1)S(1)}, u32[]{:S(2)}, u32[]{:S(2)}) collective-permute-start(bf16[3,192,384]{2,1,0:T(8,128)(2,1)S(1)} %get-tuple-element.18), channel_id=1, source_target_pairs={{0,4},{1,5},{2,6},{3,7},{4,8},{5,9},{6,10},{7,11},{8,12},{9,13},{1... | collective-permute-start | bytes 1327112 | tf_op jit(solution)/shard_map/ppermute | solution.py:40
  80.9 13.4 %collective-permute-start.22 = (bf16[3,192,384]{2,1,0:T(8,128)(2,1)S(1)}, bf16[3,192,384]{2,1,0:T(8,128)(2,1)S(1)}, u32[]{:S(2)}, u32[]{:S(2)}) collective-permute-start(bf16[3,192,384]{2,1,0:T(8,128)(2,1)S(1)} %get-tuple-element.19), channel_id=1, source_target_pairs={{0,4},{1,5},{2,6},{3,7},{4,8},{5,9},{6,10},{7,11},{8,12},{9,13},{1... | collective-permute-start | bytes 1327112 | tf_op jit(solution)/shard_map/ppermute | solution.py:40
  81.5 12.8 %collective-permute-start.25 = (bf16[3,192,384]{2,1,0:T(8,128)(2,1)S(1)}, bf16[3,192,384]{2,1,0:T(8,128)(2,1)S(1)}, u32[]{:S(2)}, u32[]{:S(2)}) collective-permute-start(bf16[3,192,384]{2,1,0:T(8,128)(2,1)S(1)} %add_convert_fusion), channel_id=1, source_target_pairs={{0,12},{1,13},{2,14},{3,15},{4,0},{5,1},{6,2},{7,3},{8,4},{9,5},{1... | collective-permute-start | bytes 1327112 | tf_op jit(solution)/shard_map/ppermute | solution.py:40
  84.7 15.0 %collective-permute-start.21 = (bf16[3,192,384]{2,1,0:T(8,128)(2,1)S(1)}, bf16[3,192,384]{2,1,0:T(8,128)(2,1)S(1)}, u32[]{:S(2)}, u32[]{:S(2)}) collective-permute-start(bf16[3,192,384]{2,1,0:T(8,128)(2,1)S(1)} %add_convert_fusion.1), channel_id=1, source_target_pairs={{0,4},{1,5},{2,6},{3,7},{4,8},{5,9},{6,10},{7,11},{8,12},{9,13},{1... | collective-permute-start | bytes 1327112 | tf_op jit(solution)/shard_map/ppermute | solution.py:40
  (21 other events, 150.0 us)
